TPU v7x, 128 devices: a whole 4x4x4 slice. The times are simulated.
128 devices in a mesh: bx: 16 (over y, x), by: 8 (over z, core).
Axes of the slice: x: 4, y: 4, z: 4, core: 2. Of those that a mesh axis runs over, the one named last changes fastest.
Arguments:
- currents: bfloat16 [128, 128, 128, 128], P(('bx', 'by')), may hold values from -6 to 6
- counts: int32 [128, 128], P(('bx', 'by')), may hold values from 0 to 128, as said below
- box_of: int32 [128, 128, 128], P(('bx', 'by')), may hold values from 0 to 15
- source_map: bfloat16 [128, 128], replicated, may hold values from -0.02734375 to 0.02734375
- phases: float32 [5, 64, 1048576], P(None, None, ('bx', 'by')), may hold values from -3.140625 to 3.140625
- trans: bfloat16 [4, 2, 2, 128, 128], replicated, may hold values from -0.375 to 0.375
Outputs:
- far_field: bfloat16 [128, 1048576], P(None, ('bx', 'by'))
Inputs may be any that keep to these rules, and one draw needn't show every extreme that they name: counts[s, d] <= 128; in every draw some owner receives exactly 128 rows from every partition.
All inputs are finite; a program needn't handle non-finite values.
Results may differ from a plain program's by a relative error of at most 0.012.
Values may be sent and summed in bfloat16 or wider, within the bound.
No kernel may reach another device: no remote copies, remote signals or barrier semaphores. Data moves between devices by JAX's collectives and lax.ppermute only.
A program may use at most 64 MiB of HBM per device.

v0:
```python
import jax
import jax.numpy as jnp
from jax import lax
from jax.sharding import PartitionSpec as P

BOXES = 16
DIRS = 512


def partner_2(value, axis, distance):
    mask = 2**distance
    pairs = [(source, source ^ mask) for source in range(lax.axis_size(axis))]
    return lax.ppermute(value, axis, pairs)


def rotate(z, angle):
    half = z.shape[0] // 2
    re = z[:half]
    im = z[half:]
    cosine = jnp.cos(angle)
    sine = jnp.sin(angle)
    return jnp.concatenate([re * cosine - im * sine, re * sine + im * cosine], axis=0)


def advance(state, partner, mats, angle):
    mixed = jnp.einsum("io,ir->or", mats[0], state, preferred_element_type=jnp.float32)
    mixed = mixed + jnp.einsum("io,ir->or", mats[1], partner, preferred_element_type=jnp.float32)
    return rotate(mixed, angle).astype(jnp.bfloat16)


def pick(trans, level, position, bit):
    beta = jnp.bitwise_and(jnp.right_shift(position, bit), 1)
    return lax.dynamic_index_in_dim(trans[level], beta, 0, keepdims=False)


def per_device(currents, counts, box_of, source_map, phases, trans):
    rows = currents[0]
    slot_count = rows.shape[1]
    slots = jnp.arange(slot_count, dtype=jnp.int32)
    live = slots[None, :] < counts[0][:, None]
    tag = jnp.where(live, box_of[0], -1)
    labels = jnp.arange(BOXES, dtype=jnp.int32)
    got_rows, got_tag = (
        lax.all_to_all(rows, ("bx", "by"), split_axis=0, concat_axis=0, tiled=True),
        lax.all_to_all(tag, ("bx", "by"), split_axis=0, concat_axis=0, tiled=True),
    )
    onehot = (got_tag[:, :, None] == labels).astype(jnp.bfloat16)
    box_sum = jnp.einsum("ncb,ncq->bq", onehot, got_rows, preferred_element_type=jnp.float32)
    box_sum = box_sum.astype(jnp.bfloat16)
    expansion = jnp.dot(box_sum, source_map, preferred_element_type=jnp.float32)
    width = expansion.shape[1]
    spread = jnp.broadcast_to(expansion.T[:, :, None], (width, BOXES, DIRS)).reshape(
        width, BOXES * DIRS
    )
    state = rotate(spread, phases[0]).astype(jnp.bfloat16)
    box_pos = lax.axis_index("bx")
    dir_pos = lax.axis_index("by")
    for bit in range(2):
        partner = partner_2(state, "bx", bit)
        state = advance(state, partner, pick(trans, 2 * bit, box_pos, bit), phases[2 * bit + 1])
        partner = partner_2(state, "by", bit)
        state = advance(state, partner, pick(trans, 2 * bit + 1, dir_pos, bit), phases[2 * bit + 2])
    return state


def solution(mesh):
    placed = (
        P(("bx", "by"), None, None, None),
        P(("bx", "by"), None),
        P(("bx", "by"), None, None),
        P(),
        P(None, None, ("bx", "by")),
        P(),
    )
    return jax.shard_map(
        per_device, mesh=mesh, in_specs=placed, out_specs=P(None, ("bx", "by")), check_vma=False
    )
```

profile of v0, /device:TPU:0, one launch (start us, length us, event | category | flops | bytes accessed | tf_op | source)
XLA Modules:
  0.0 297.2 jit_solution(229856614734765843)
XLA Ops:
  0.0 0.0 copy-start
  0.0 1.0 compare_select_fusion
  1.1 20.5 %all_to_all.11 = s32[128,1,128]{2,1,0:T(1,128)S(1)} all-to-all(s32[128,1,128]{2,1,0:T(1,128)S(1)} %compare_select_fusion), channel_id=1, replica_groups=mesh['bx'=16,'by'=8] {'bx','by'}, dimensions={0} | all-to-all | bytes 131072 | tf_op jit(solution)/shard_map/all_to_all | solution.py:45
  21.5 58.6 %all_to_all.12 = bf16[128,128,128]{2,1,0:T(8,128)(2,1)} all-to-all(bf16[128,128,128]{2,1,0:T(8,128)(2,1)} %bitcast.140), channel_id=1, replica_groups=mesh['bx'=16,'by'=8] {'bx','by'}, dimensions={0} | all-to-all | bytes 8388608 | tf_op jit(solution)/shard_map/all_to_all | solution.py:44
  80.1 0.0 copy-done
  80.1 3.0 convolution_bitcast_fusion
  83.0 0.1 fusion.36
  83.1 0.1 copy.11
  83.2 0.2 broadcast_in_dim.16
  83.4 2.5 copy.13
  85.9 0.1 copy.12
  86.0 0.2 broadcast_in_dim.17
  86.2 0.0 copy-start.2
  86.2 1.2 copy.14
  87.5 0.3 copy-done.2
  87.8 8.8 %fusion.17 = (bf16[64,8192]{1,0:T(8,128)(2,1)S(1)}, bf16[64,8192]{1,0:T(8,128)(2,1)S(1)}) fusion(f32[64,8192]{1,0:T(8,128)S(1)} %bitcast.139, f32[64,8192]{1,0:T(8,128)S(1)} %bitcast.138, f32[5,64,8192]{2,1,0:T(8,128)} %param.10), kind=kLoop, calls=%fused_computation.44 | loop fusion | flops 4194304 | bytes 8388608 | tf_op jit(solution)/shard_map/convert.8
  96.6 0.0 copy-start.3
  96.6 1.5 pad_maximum_fusion
  98.1 0.7 collective-permute-start
  98.8 0.0 copy-done.3
  98.9 0.7 fusion.23
  99.6 45.8 %collective-permute-done = bf16[128,8192]{1,0:T(8,128)(2,1)} collective-permute-done((bf16[128,8192]{1,0:T(8,128)(2,1)}, bf16[128,8192]{1,0:T(8,128)(2,1)}, u32[]{:S(2)}, u32[]{:S(2)}) %collective-permute-start) | collective-permute-done | bytes 2097184 | tf_op jit(solution)/shard_map/ppermute | solution.py:13
  145.4 2.4 convolution_add_fusion.3
  147.8 8.8 %fusion.13 = (bf16[64,8192]{1,0:T(8,128)(2,1)S(1)}, bf16[64,8192]{1,0:T(8,128)(2,1)S(1)}) fusion(f32[128,8192]{1,0:T(8,128)S(1)} %convolution_add_fusion.3, f32[5,64,8192]{2,1,0:T(8,128)} %param.10), kind=kLoop, calls=%fused_computation.36 | loop fusion | flops 4194304 | bytes 8388608 | tf_op jit(solution)/shard_map/convert.6
  156.6 1.5 pad_maximum_fusion.1
  158.1 0.0 collective-permute-start.1
  158.1 0.7 fusion.24
  158.8 3.8 %collective-permute-done.1 = bf16[128,8192]{1,0:T(8,128)(2,1)} collective-permute-done((bf16[128,8192]{1,0:T(8,128)(2,1)}, bf16[128,8192]{1,0:T(8,128)(2,1)}, u32[]{:S(2)}, u32[]{:S(2)}) %collective-permute-start.1) | collective-permute-done | bytes 2097184 | tf_op jit(solution)/shard_map/ppermute | solution.py:13
  162.6 2.4 convolution_add_fusion.2
  164.9 8.8 %fusion.9 = (bf16[64,8192]{1,0:T(8,128)(2,1)S(1)}, bf16[64,8192]{1,0:T(8,128)(2,1)S(1)}) fusion(f32[128,8192]{1,0:T(8,128)S(1)} %convolution_add_fusion.2, f32[5,64,8192]{2,1,0:T(8,128)} %param.10), kind=kLoop, calls=%fused_computation.28 | loop fusion | flops 4194304 | bytes 8388608 | tf_op jit(solution)/shard_map/convert.4
  173.7 1.5 pad_maximum_fusion.2
  175.2 1.6 collective-permute-start.2
  176.8 0.7 fusion.25
  177.5 47.2 %collective-permute-done.2 = bf16[128,8192]{1,0:T(8,128)(2,1)} collective-permute-done((bf16[128,8192]{1,0:T(8,128)(2,1)}, bf16[128,8192]{1,0:T(8,128)(2,1)}, u32[]{:S(2)}, u32[]{:S(2)}) %collective-permute-start.2) | collective-permute-done | bytes 2097184 | tf_op jit(solution)/shard_map/ppermute | solution.py:13
  224.7 2.4 convolution_add_fusion.1
  227.1 8.8 %fusion.5 = (bf16[64,8192]{1,0:T(8,128)(2,1)S(1)}, bf16[64,8192]{1,0:T(8,128)(2,1)S(1)}) fusion(f32[128,8192]{1,0:T(8,128)S(1)} %convolution_add_fusion.1, f32[5,64,8192]{2,1,0:T(8,128)} %param.10), kind=kLoop, calls=%fused_computation.20 | loop fusion | flops 4194304 | bytes 8388608 | tf_op jit(solution)/shard_map/convert.2
  235.9 1.5 pad_maximum_fusion.3
  237.3 0.4 collective-permute-start.3
  237.8 0.7 fusion.26
  238.5 46.0 %collective-permute-done.3 = bf16[128,8192]{1,0:T(8,128)(2,1)} collective-permute-done((bf16[128,8192]{1,0:T(8,128)(2,1)}, bf16[128,8192]{1,0:T(8,128)(2,1)}, u32[]{:S(2)}, u32[]{:S(2)}) %collective-permute-start.3) | collective-permute-done | bytes 2097184 | tf_op jit(solution)/shard_map/ppermute | solution.py:13
  284.5 2.4 convolution_add_fusion
  286.9 8.8 %fusion.1 = (bf16[64,8192]{1,0:T(8,128)(2,1)S(1)}, bf16[64,8192]{1,0:T(8,128)(2,1)S(1)}) fusion(f32[128,8192]{1,0:T(8,128)S(1)} %convolution_add_fusion, f32[5,64,8192]{2,1,0:T(8,128)} %param.10), kind=kLoop, calls=%fused_computation.12 | loop fusion | flops 4194304 | bytes 8388608 | tf_op jit(solution)/shard_map/convert
  295.7 0.0 copy-start.1
  295.7 1.5 pad_maximum_fusion.4
  297.2 0.0 copy-done.1
  (1 shorter events, 0.0 us)
Async XLA Ops:
  0.0 80.1 %copy-start = (bf16[128,128]{1,0:T(8,128)(2,1)S(1)}, bf16[128,128]{1,0:T(8,128)(2,1)}, u32[]{:S(2)}) copy-start(bf16[128,128]{1,0:T(8,128)(2,1)} %param.9) | copy-start | bytes 98308
  86.2 1.6 copy-start.2
  96.6 2.2 copy-start.3
  98.1 47.3 %collective-permute-start = (bf16[128,8192]{1,0:T(8,128)(2,1)}, bf16[128,8192]{1,0:T(8,128)(2,1)}, u32[]{:S(2)}, u32[]{:S(2)}) collective-permute-start(bf16[128,8192]{1,0:T(8,128)(2,1)} %pad_maximum_fusion), channel_id=1, source_target_pairs={{0,8},{8,0},{16,24},{24,16},{32,40},{40,32},{48,56},{56,48},{64,72... | collective-permute-start | bytes 6291464 | tf_op jit(solution)/shard_map/ppermute | solution.py:13
  158.1 4.5 %collective-permute-start.1 = (bf16[128,8192]{1,0:T(8,128)(2,1)}, bf16[128,8192]{1,0:T(8,128)(2,1)}, u32[]{:S(2)}, u32[]{:S(2)}) collective-permute-start(bf16[128,8192]{1,0:T(8,128)(2,1)} %pad_maximum_fusion.1), channel_id=1, source_target_pairs={{0,1},{1,0},{2,3},{3,2},{4,5},{5,4},{6,7},{7,6},{8,9},{9,8},{10,11... | collective-permute-start | bytes 6291464 | tf_op jit(solution)/shard_map/ppermute | solution.py:13
  175.2 49.5 %collective-permute-start.2 = (bf16[128,8192]{1,0:T(8,128)(2,1)}, bf16[128,8192]{1,0:T(8,128)(2,1)}, u32[]{:S(2)}, u32[]{:S(2)}) collective-permute-start(bf16[128,8192]{1,0:T(8,128)(2,1)} %pad_maximum_fusion.2), channel_id=1, source_target_pairs={{0,16},{8,24},{16,0},{24,8},{32,48},{40,56},{48,32},{56,40},{64,80... | collective-permute-start | bytes 6291464 | tf_op jit(solution)/shard_map/ppermute | solution.py:13
  237.3 47.2 %collective-permute-start.3 = (bf16[128,8192]{1,0:T(8,128)(2,1)}, bf16[128,8192]{1,0:T(8,128)(2,1)}, u32[]{:S(2)}, u32[]{:S(2)}) collective-permute-start(bf16[128,8192]{1,0:T(8,128)(2,1)} %pad_maximum_fusion.3), channel_id=1, source_target_pairs={{0,2},{1,3},{2,0},{3,1},{4,6},{5,7},{6,4},{7,5},{8,10},{9,11},{10,... | collective-permute-start | bytes 6291464 | tf_op jit(solution)/shard_map/ppermute | solution.py:13
  295.7 1.5 copy-start.1
where the time goes:
time: 298 us; the launch traced here: 297 us
  waiting for transfers between devices  143 us (48%)
  blocking collectives  79 us (27%)
  other arithmetic  52.3 us (18%)
  matrix products  15.4 us (5%)
  local copies, waits for them, and re-layouts  4.8 us (2%)
    ppermute x4, waiting for transfers between devices, partner_2(): return lax.ppermute(value, axis, pairs)  143 us
    all_to_all x1, blocking collectives, per_device(): lax.all_to_all(rows, ('bx', 'by'), split_axis=0, concat_axis=0, tiled=True)  58.6 us
    another operation x5, other arithmetic  44 us
    all_to_all x1, blocking collectives, per_device(): lax.all_to_all(tag, ('bx', 'by'), split_axis=0, concat_axis=0, tiled=True)  20.5 us
    dot_general x4, matrix products, advance(): jnp.einsum('io,ir->or', mats[1], partner, preferred_element_type=jnp.floa...  9.47 us
    concatenate x5, other arithmetic, rotate(): jnp.concatenate([re * cosine - im * sine, re * sine + im * cosine], axis=0)  7.32 us
  transfers between devices with their start and end apart: 4, of which 4 were waited for; matrix products, arithmetic and copies ran while one was open for 1% of the time, Pallas kernels for 0%

commit v1 on v0

v1 whole, which is shorter than its diff:
```python
import functools

import jax
import jax.numpy as jnp
from jax import lax
from jax.experimental import pallas as pl
from jax.experimental.pallas import tpu as pltpu
from jax.sharding import PartitionSpec as P

BOXES = 16
DIRS = 512
HALF = 64
WIDTH = 128
ROWS = BOXES * DIRS
SPLIT = 4
OWNERS_PER_STEP = 16

TURN = 32767.0 / 3.141592653589793
SIN_HALF = (0.7071043848991394, -0.02945953793823719, 0.0003670926089398563, -2.0290131033107173e-06)
COS_HALF = (
    1.4142135381698608,
    -0.17677636444568634,
    0.003682575887069106,
    -3.061274401261471e-05,
    1.2791403491974052e-07,
)


def horner(terms, square):
    total = jnp.full_like(square, terms[-1])
    for term in terms[-2::-1]:
        total = total * square + term
    return total


def cos_sin(angle):
    square = angle * angle
    sine = horner(SIN_HALF, square) * angle
    cosine = horner(COS_HALF, square)
    return 1.0 - sine * sine, sine * cosine


def turn(re, im, angle):
    cosine, sine = cos_sin(angle)
    top = re * cosine - im * sine
    low = re * sine + im * cosine
    return jnp.concatenate([top, low], axis=0).astype(jnp.bfloat16)


def box_sums_kernel(counts_ref, tag_ref, rows_ref, out_ref):
    first = pl.program_id(0) * OWNERS_PER_STEP
    slot = lax.broadcasted_iota(jnp.int32, (BOXES, WIDTH), 1)
    label = lax.broadcasted_iota(jnp.int32, (BOXES, WIDTH), 0)
    for j in range(OWNERS_PER_STEP):
        live = slot < counts_ref[0, first + j]
        hit = jnp.logical_and(tag_ref[j : j + 1, :] == label, live)
        picks = jnp.where(hit, 1.0, 0.0).astype(jnp.bfloat16)
        out_ref[j] = jnp.dot(picks, rows_ref[j], preferred_element_type=jnp.float32).astype(jnp.bfloat16)


def box_sums(counts, tag, rows):
    owners = rows.shape[0]
    step = OWNERS_PER_STEP
    return pl.pallas_call(
        box_sums_kernel,
        grid=(owners // step,),
        in_specs=[
            pl.BlockSpec(memory_space=pltpu.SMEM),
            pl.BlockSpec((step, WIDTH), lambda i: (i, 0)),
            pl.BlockSpec((step, WIDTH, WIDTH), lambda i: (i, 0, 0)),
        ],
        out_specs=pl.BlockSpec((step, BOXES, WIDTH), lambda i: (i, 0, 0)),
        out_shape=jax.ShapeDtypeStruct((owners, BOXES, WIDTH), jnp.bfloat16),
        name="box_sums",
    )(counts, tag, rows)


def expand_kernel(parts_ref, map_ref, out_ref):
    total = jnp.sum(parts_ref[...].astype(jnp.float32), axis=0)
    out_ref[...] = jnp.dot(total.astype(jnp.bfloat16), map_ref[...], preferred_element_type=jnp.float32)


def expand(parts, source_map):
    return pl.pallas_call(
        expand_kernel,
        out_shape=jax.ShapeDtypeStruct((BOXES, WIDTH), jnp.float32),
        name="expand",
    )(parts, source_map)


def column(x_ref, box):
    row = jnp.broadcast_to(x_ref[pl.ds(box, 1), :], (8, WIDTH))
    return row.T[:, :1]


def first_kernel(start, x_ref, other_x_ref, mats_ref, angle0_ref, other_ref, angle1_ref, out_ref):
    box = start + pl.program_id(0)
    mine = column(x_ref, box)
    state = turn(mine[:HALF], mine[HALF:], angle0_ref[...])
    theirs = column(other_x_ref, box)
    angle = other_ref[...].astype(jnp.int32).astype(jnp.float32) * (1.0 / TURN)
    partner = turn(theirs[:HALF], theirs[HALF:], angle)
    both = jnp.concatenate([state, partner], axis=0)
    mixed = jnp.dot(mats_ref[...], both, preferred_element_type=jnp.float32)
    out_ref[...] = turn(mixed[:HALF], mixed[HALF:], angle1_ref[...])


def first_level(part, x, other_x, mats, phases, other_turns):
    blocks = BOXES // SPLIT
    start = part * blocks
    whole = lambda i: (0, 0)
    return pl.pallas_call(
        functools.partial(first_kernel, start),
        grid=(blocks,),
        in_specs=[
            pl.BlockSpec((BOXES, WIDTH), whole),
            pl.BlockSpec((BOXES, WIDTH), whole),
            pl.BlockSpec((WIDTH, 2 * WIDTH), whole),
            pl.BlockSpec((None, HALF, DIRS), lambda i: (0, 0, start + i)),
            pl.BlockSpec((HALF, DIRS), lambda i: (0, start + i)),
            pl.BlockSpec((None, HALF, DIRS), lambda i: (1, 0, start + i)),
        ],
        out_specs=pl.BlockSpec((WIDTH, DIRS), lambda i: (0, i)),
        out_shape=jax.ShapeDtypeStruct((WIDTH, ROWS // SPLIT), jnp.bfloat16),
        name="first_level",
    )(x, other_x, mats, phases, other_turns, phases)


def level_kernel(state_ref, partner_ref, mats_ref, angle_ref, out_ref):
    both = jnp.concatenate([state_ref[...], partner_ref[...]], axis=0)
    mixed = jnp.dot(mats_ref[...], both, preferred_element_type=jnp.float32)
    out_ref[...] = turn(mixed[:HALF], mixed[HALF:], angle_ref[...])


def last_kernel(state_ref, partner_ref, mats_ref, angle_ref, held_ref, out_ref):
    level_kernel(state_ref, partner_ref, mats_ref, angle_ref, out_ref)


def next_level(part, level, state, partner, mats, phases, held=None):
    blocks = BOXES // SPLIT
    start = part * blocks
    in_specs = [
        pl.BlockSpec((WIDTH, DIRS), lambda i: (0, i)),
        pl.BlockSpec((WIDTH, DIRS), lambda i: (0, i)),
        pl.BlockSpec((WIDTH, 2 * WIDTH), lambda i: (0, 0)),
        pl.BlockSpec((None, HALF, DIRS), lambda i: (level + 1, 0, start + i)),
    ]
    operands = [state, partner, mats, phases]
    last = level == 3
    aliases = {}
    if held is not None:
        in_specs.append(pl.BlockSpec(memory_space=pl.ANY))
        operands.append(held)
        aliases = {4: 0}
    return pl.pallas_call(
        level_kernel if held is None else last_kernel,
        grid=(blocks,),
        in_specs=in_specs,
        out_specs=pl.BlockSpec((WIDTH, DIRS), (lambda i: (0, start + i)) if last else (lambda i: (0, i))),
        out_shape=jax.ShapeDtypeStruct((WIDTH, ROWS if last else ROWS // SPLIT), jnp.bfloat16),
        input_output_aliases=aliases,
        name="level_%d" % level,
    )(*operands)


def swap(value, axis, bit):
    mask = 1 << bit
    return lax.ppermute(value, axis, [(s, s ^ mask) for s in range(lax.axis_size(axis))])


def pick(trans, level, position, bit):
    beta = jnp.bitwise_and(jnp.right_shift(position, bit), 1)
    mats = lax.dynamic_index_in_dim(trans[level], beta, 0, keepdims=False)
    return mats.reshape(2 * WIDTH, WIDTH).T


def per_device(currents, counts, box_of, source_map, phases, trans):
    turns = jnp.round(phases[0] * TURN).astype(jnp.int16)
    other_turns = swap(turns, "bx", 0)
    sums = box_sums(counts, box_of[0], currents[0])
    parts = lax.all_to_all(sums, ("bx", "by"), split_axis=0, concat_axis=0, tiled=True)
    x = expand(parts, source_map)
    other_x = swap(x, "bx", 0)
    bx = lax.axis_index("bx")
    by = lax.axis_index("by")
    mats = [pick(trans, 0, bx, 0), pick(trans, 1, by, 0), pick(trans, 2, bx, 1), pick(trans, 3, by, 1)]
    state = [first_level(p, x, other_x, mats[0], phases, other_turns) for p in range(SPLIT)]
    for level, (axis, bit) in ((1, ("by", 0)), (2, ("bx", 1))):
        state = [next_level(p, level, s, swap(s, axis, bit), mats[level], phases) for p, s in enumerate(state)]
    held = None
    for p, s in enumerate(state):
        held = next_level(p, 3, s, swap(s, "by", 1), mats[3], phases, held)
    return held


def solution(mesh):
    placed = (
        P(("bx", "by"), None, None, None),
        P(("bx", "by"), None),
        P(("bx", "by"), None, None),
        P(),
        P(None, None, ("bx", "by")),
        P(),
    )
    return jax.shard_map(
        per_device, mesh=mesh, in_specs=placed, out_specs=P(None, ("bx", "by")), check_vma=False
    )
```

time: 298 us -> 152 us (0.51)
  waiting for transfers between devices: 143 us -> 38.1 us
  blocking collectives: 79 us -> 0 us
  Pallas kernels: 0 us -> 73.4 us
  other arithmetic: 52.3 us -> 1.9 us
  starting transfers between devices: 2.75 us -> 21.7 us
  matrix products: 15.4 us -> 0 us
  local copies, waits for them, and re-layouts: 4.8 us -> 15.8 us
    ppermute x4 -> x14, waiting for transfers between devices: 143 us -> 19 us  [swap(): lax.ppermute(value, axis, [(s, s ^ mask) for s in range(lax.axis_size(axi...]
    all_to_all x2 -> x0, blocking collectives: 79 us -> none  [the longest x1 58.6 us: per_device(): lax.all_to_all(rows, ('bx', 'by'), split_axis=0, concat_axis=0, tiled=True)]
    pallas_call x0 -> x18, Pallas kernels: none -> 73.4 us  [the longest x12 46.6 us: next_level(): pl.pallas_call(level_kernel if held is None else last_kernel, grid=(block...]
    another operation x5 -> x0, other arithmetic: 44 us -> none
    all_to_all x0 -> x1, waiting for transfers between devices: none -> 19 us  [per_device(): lax.all_to_all(sums, ('bx', 'by'), split_axis=0, concat_axis=0, tiled=True)]
    dot_general x9 -> x0, matrix products: 15.4 us -> none  [the longest x4 9.47 us: advance(): jnp.einsum('io,ir->or', mats[1], partner, preferred_element_type=jnp.floa...]
    all_to_all x0 -> x1, starting transfers between devices: none -> 10.8 us  [per_device(): lax.all_to_all(sums, ('bx', 'by'), split_axis=0, concat_axis=0, tiled=True)]
    ppermute x4 -> x14, starting transfers between devices: 2.75 us -> 10.9 us  [swap(): lax.ppermute(value, axis, [(s, s ^ mask) for s in range(lax.axis_size(axi...]
  transfers between devices with their start and end apart: 4 -> 15, of which waited for: 4 -> 7; matrix products, arithmetic and copies ran while one was open for 1% -> 3% of each run, Pallas kernels for 0% -> 43%
where the time goes in v1:
time: 152 us; the launch traced here: 151 us
  Pallas kernels  73.4 us (48%)
  waiting for transfers between devices  38.1 us (25%)
  starting transfers between devices  21.7 us (14%)
  local copies, waits for them, and re-layouts  15.8 us (10%)
  other arithmetic  1.9 us (1%)
    pallas_call x12, Pallas kernels, next_level(): pl.pallas_call(level_kernel if held is None else last_kernel, grid=(block...  46.6 us
    all_to_all x1, waiting for transfers between devices, per_device(): lax.all_to_all(sums, ('bx', 'by'), split_axis=0, concat_axis=0, tiled=True)  19 us
    ppermute x14, waiting for transfers between devices, swap(): lax.ppermute(value, axis, [(s, s ^ mask) for s in range(lax.axis_size(axi...  19 us
    pallas_call x4, Pallas kernels, first_level(): pl.pallas_call(functools.partial(first_kernel, start), grid=(blocks,), in...  18.2 us
    unnamed x32, local copies, waits for them, and re-layouts  11.3 us
    ppermute x14, starting transfers between devices, swap(): lax.ppermute(value, axis, [(s, s ^ mask) for s in range(lax.axis_size(axi...  10.9 us
    all_to_all x1, starting transfers between devices, per_device(): lax.all_to_all(sums, ('bx', 'by'), split_axis=0, concat_axis=0, tiled=True)  10.8 us
    pallas_call x1, Pallas kernels, box_sums(): pl.pallas_call(box_sums_kernel, grid=(owners // step,), in_specs=[pl.Bloc...  6.75 us
  transfers between devices with their start and end apart: 15, of which 7 were waited for; matrix products, arithmetic and copies ran while one was open for 3% of the time, Pallas kernels for 43%

profile of v1, /device:TPU:0, one launch (start us, length us, event | category | flops | bytes accessed | tf_op | source)
XLA Modules:
  0.0 150.9 jit_solution(11704435551840977879)
XLA Ops:
  0.0 1.9 %fusion = s16[64,8192]{1,0:T(8,128)(2,1)S(1)} fusion(f32[5,64,8192]{2,1,0:T(8,128)} %angle_ref.23), kind=kLoop, calls=%fused_computation.1 | loop fusion | flops 1572864 | bytes 3145728 | tf_op jit(solution)/shard_map/convert_element_type | solution.py:178
  1.9 1.7 %collective-permute-start.1 = (s16[64,8192]{1,0:T(8,128)(2,1)S(1)}, s16[64,8192]{1,0:T(8,128)(2,1)S(1)}, u32[]{:S(2)}, u32[]{:S(2)}) collective-permute-start(s16[64,8192]{1,0:T(8,128)(2,1)S(1)} %fusion), channel_id=1, source_target_pairs={{0,8},{8,0},{16,24},{24,16},{32,40},{40,32},{48,56},{56,48},{64,72... | collective-permute-start | bytes 3145736 | tf_op jit(solution)/shard_map/ppermute | solution.py:168
  3.6 6.8 %box_sums.1 = bf16[128,16,128]{2,1,0:T(8,128)(2,1)} custom-call(s32[1,128]{1,0:T(1,128)} %counts_ref.1, s32[128,128]{1,0:T(8,128)} %bitcast.33, bf16[128,128,128]{2,1,0:T(8,128)(2,1)} %bitcast.12), custom_call_target="tpu_custom_call" | custom-call | tf_op jit(solution)/shard_map/box_sums/pallas_call | solution.py:64
  10.3 10.8 %all-to-all-start = ((bf16[128,16,128]{2,1,0:T(8,128)(2,1)}), bf16[128,16,128]{2,1,0:T(8,128)(2,1)S(1)}, u32[]{:S(2)}, u32[]{:S(2)}) async-start(bf16[128,16,128]{2,1,0:T(8,128)(2,1)} %box_sums.1), calls=%async_computation | async-start | bytes 1048576 | tf_op jit(solution)/shard_map/all_to_all | solution.py:181
  21.8 19.0 %all-to-all-done.parts_ref = bf16[128,16,128]{2,1,0:T(8,128)(2,1)S(1)} async-done(((bf16[128,16,128]{2,1,0:T(8,128)(2,1)}), bf16[128,16,128]{2,1,0:T(8,128)(2,1)S(1)}, u32[]{:S(2)}, u32[]{:S(2)}) %all-to-all-start) | async-done | bytes 524320 | tf_op jit(solution)/shard_map/all_to_all | solution.py:181
  40.8 0.8 copy-done.1
  41.6 1.9 %expand.1.x_ref = f32[16,128]{1,0:T(8,128)} custom-call(bf16[128,16,128]{2,1,0:T(8,128)(2,1)} %copy-done.1, bf16[128,128]{1,0:T(8,128)(2,1)} %map_ref.1), custom_call_target="tpu_custom_call" | custom-call | tf_op jit(solution)/shard_map/expand/pallas_call | solution.py:84
  43.8 0.8 constant_dynamic-slice_fusion.2
  44.6 0.7 copy.14
  45.4 2.0 %collective-permute-done.other_x_ref = f32[16,128]{1,0:T(8,128)S(1)} collective-permute-done((f32[16,128]{1,0:T(8,128)}, f32[16,128]{1,0:T(8,128)S(1)}, u32[]{:S(2)}, u32[]{:S(2)}) %collective-permute-start) | collective-permute-done | bytes 8224 | tf_op jit(solution)/shard_map/ppermute | solution.py:168
  48.4 4.6 %first_level.7.state_ref = bf16[128,2048]{1,0:T(8,128)(2,1)} custom-call(f32[16,128]{1,0:T(8,128)} %expand.1.x_ref, f32[16,128]{1,0:T(8,128)} %copy-done.15, bf16[128,256]{1,0:T(8,128)(2,1)} %bitcast.21, f32[5,64,8192]{2,1,0:T(8,128)} %angle_ref.23, s16[64,8192]{1,0:T(8,128)(2,1)} %copy-done, f32[5,64,8192]{2,1,0:T(8,128)} %angle_ref.23), custom_call_target="tpu_custom_call" | custom-call | tf_op jit(solution)/shard_map/first_level/pallas_call | solution.py:112
  52.9 4.6 %first_level.6.state_ref = bf16[128,2048]{1,0:T(8,128)(2,1)} custom-call(f32[16,128]{1,0:T(8,128)} %expand.1.x_ref, f32[16,128]{1,0:T(8,128)} %copy-done.15, bf16[128,256]{1,0:T(8,128)(2,1)} %bitcast.22, f32[5,64,8192]{2,1,0:T(8,128)} %angle_ref.23, s16[64,8192]{1,0:T(8,128)(2,1)} %copy-done, f32[5,64,8192]{2,1,0:T(8,128)} %angle_ref.23), custom_call_target="tpu_custom_call" | custom-call | tf_op jit(solution)/shard_map/first_level/pallas_call | solution.py:112
  58.0 4.5 %first_level.5.state_ref = bf16[128,2048]{1,0:T(8,128)(2,1)} custom-call(f32[16,128]{1,0:T(8,128)} %expand.1.x_ref, f32[16,128]{1,0:T(8,128)} %copy-done.15, bf16[128,256]{1,0:T(8,128)(2,1)} %bitcast.23, f32[5,64,8192]{2,1,0:T(8,128)} %angle_ref.23, s16[64,8192]{1,0:T(8,128)(2,1)} %copy-done, f32[5,64,8192]{2,1,0:T(8,128)} %angle_ref.23), custom_call_target="tpu_custom_call" | custom-call | tf_op jit(solution)/shard_map/first_level/pallas_call | solution.py:112
  62.5 4.5 %first_level.4.state_ref = bf16[128,2048]{1,0:T(8,128)(2,1)} custom-call(f32[16,128]{1,0:T(8,128)} %expand.1.x_ref, f32[16,128]{1,0:T(8,128)} %copy-done.15, bf16[128,256]{1,0:T(8,128)(2,1)} %bitcast.24, f32[5,64,8192]{2,1,0:T(8,128)} %angle_ref.23, s16[64,8192]{1,0:T(8,128)(2,1)} %copy-done, f32[5,64,8192]{2,1,0:T(8,128)} %angle_ref.23), custom_call_target="tpu_custom_call" | custom-call | tf_op jit(solution)/shard_map/first_level/pallas_call | solution.py:112
  67.5 0.7 copy.15
  68.3 0.8 copy-done.12
  69.1 3.9 %level_1.7.state_ref = bf16[128,2048]{1,0:T(8,128)(2,1)} custom-call(bf16[128,2048]{1,0:T(8,128)(2,1)} %first_level.7.state_ref, bf16[128,2048]{1,0:T(8,128)(2,1)} %copy-done.12, bf16[128,256]{1,0:T(8,128)(2,1)} %bitcast.13, f32[5,64,8192]{2,1,0:T(8,128)} %angle_ref.23), custom_call_target="tpu_custom_call" | custom-call | tf_op jit(solution)/shard_map/level_1/pallas_call | solution.py:155
  73.5 0.8 copy-done.9
  74.3 3.9 %level_1.6.state_ref = bf16[128,2048]{1,0:T(8,128)(2,1)} custom-call(bf16[128,2048]{1,0:T(8,128)(2,1)} %first_level.6.state_ref, bf16[128,2048]{1,0:T(8,128)(2,1)} %copy-done.9, bf16[128,256]{1,0:T(8,128)(2,1)} %bitcast.14, f32[5,64,8192]{2,1,0:T(8,128)} %angle_ref.23), custom_call_target="tpu_custom_call" | custom-call | tf_op jit(solution)/shard_map/level_1/pallas_call | solution.py:155
  78.2 2.9 %collective-permute-start.9 = (bf16[128,2048]{1,0:T(8,128)(2,1)}, bf16[128,2048]{1,0:T(8,128)(2,1)S(1)}, u32[]{:S(2)}, u32[]{:S(2)}) collective-permute-start(bf16[128,2048]{1,0:T(8,128)(2,1)} %level_1.6.state_ref), channel_id=1, source_target_pairs={{0,16},{8,24},{16,0},{24,8},{32,48},{40,56},{48,32},{56,40},{64,80... | collective-permute-start | bytes 1572872 | tf_op jit(solution)/shard_map/ppermute | solution.py:168
  81.2 0.8 copy-done.7
  81.9 3.9 %level_1.5.state_ref = bf16[128,2048]{1,0:T(8,128)(2,1)} custom-call(bf16[128,2048]{1,0:T(8,128)(2,1)} %first_level.5.state_ref, bf16[128,2048]{1,0:T(8,128)(2,1)} %copy-done.7, bf16[128,256]{1,0:T(8,128)(2,1)} %bitcast.15, f32[5,64,8192]{2,1,0:T(8,128)} %angle_ref.23), custom_call_target="tpu_custom_call" | custom-call | tf_op jit(solution)/shard_map/level_1/pallas_call | solution.py:155
  86.5 0.8 copy-done.6
  87.3 3.9 %level_1.4.state_ref = bf16[128,2048]{1,0:T(8,128)(2,1)} custom-call(bf16[128,2048]{1,0:T(8,128)(2,1)} %first_level.4.state_ref, bf16[128,2048]{1,0:T(8,128)(2,1)} %copy-done.6, bf16[128,256]{1,0:T(8,128)(2,1)} %bitcast.16, f32[5,64,8192]{2,1,0:T(8,128)} %angle_ref.23), custom_call_target="tpu_custom_call" | custom-call | tf_op jit(solution)/shard_map/level_1/pallas_call | solution.py:155
  91.2 2.9 %collective-permute-start.3 = (bf16[128,2048]{1,0:T(8,128)(2,1)}, bf16[128,2048]{1,0:T(8,128)(2,1)S(1)}, u32[]{:S(2)}, u32[]{:S(2)}) collective-permute-start(bf16[128,2048]{1,0:T(8,128)(2,1)} %level_1.4.state_ref), channel_id=1, source_target_pairs={{0,16},{8,24},{16,0},{24,8},{32,48},{40,56},{48,32},{56,40},{64,80... | collective-permute-start | bytes 1572872 | tf_op jit(solution)/shard_map/ppermute | solution.py:168
  94.1 0.7 copy.16
  94.8 0.8 copy-done.2
  95.6 3.9 %level_2.7.state_ref = bf16[128,2048]{1,0:T(8,128)(2,1)} custom-call(bf16[128,2048]{1,0:T(8,128)(2,1)} %level_1.7.state_ref, bf16[128,2048]{1,0:T(8,128)(2,1)} %copy-done.2, bf16[128,256]{1,0:T(8,128)(2,1)} %bitcast.17, f32[5,64,8192]{2,1,0:T(8,128)} %angle_ref.23), custom_call_target="tpu_custom_call" | custom-call | tf_op jit(solution)/shard_map/level_2/pallas_call | solution.py:155
  99.6 1.1 collective-permute-done.9.partner_ref
  100.7 0.8 copy-done.3
  101.5 3.9 %level_2.6.state_ref = bf16[128,2048]{1,0:T(8,128)(2,1)} custom-call(bf16[128,2048]{1,0:T(8,128)(2,1)} %level_1.6.state_ref, bf16[128,2048]{1,0:T(8,128)(2,1)} %copy-done.3, bf16[128,256]{1,0:T(8,128)(2,1)} %bitcast.18, f32[5,64,8192]{2,1,0:T(8,128)} %angle_ref.23), custom_call_target="tpu_custom_call" | custom-call | tf_op jit(solution)/shard_map/level_2/pallas_call | solution.py:155
  105.3 0.9 collective-permute-start.10
  106.2 5.7 %collective-permute-done.6.partner_ref = bf16[128,2048]{1,0:T(8,128)(2,1)S(1)} collective-permute-done((bf16[128,2048]{1,0:T(8,128)(2,1)}, bf16[128,2048]{1,0:T(8,128)(2,1)S(1)}, u32[]{:S(2)}, u32[]{:S(2)}) %collective-permute-start.6) | collective-permute-done | bytes 524320 | tf_op jit(solution)/shard_map/ppermute | solution.py:168
  111.9 0.8 copy-done.4
  112.7 3.9 %level_2.5.state_ref = bf16[128,2048]{1,0:T(8,128)(2,1)} custom-call(bf16[128,2048]{1,0:T(8,128)(2,1)} %level_1.5.state_ref, bf16[128,2048]{1,0:T(8,128)(2,1)} %copy-done.4, bf16[128,256]{1,0:T(8,128)(2,1)} %bitcast.19, f32[5,64,8192]{2,1,0:T(8,128)} %angle_ref.23), custom_call_target="tpu_custom_call" | custom-call | tf_op jit(solution)/shard_map/level_2/pallas_call | solution.py:155
  116.6 5.6 %collective-permute-done.3.partner_ref = bf16[128,2048]{1,0:T(8,128)(2,1)S(1)} collective-permute-done((bf16[128,2048]{1,0:T(8,128)(2,1)}, bf16[128,2048]{1,0:T(8,128)(2,1)S(1)}, u32[]{:S(2)}, u32[]{:S(2)}) %collective-permute-start.3) | collective-permute-done | bytes 524320 | tf_op jit(solution)/shard_map/ppermute | solution.py:168
  122.2 0.8 copy-done.5
  123.0 3.9 %level_2.4.state_ref = bf16[128,2048]{1,0:T(8,128)(2,1)} custom-call(bf16[128,2048]{1,0:T(8,128)(2,1)} %level_1.4.state_ref, bf16[128,2048]{1,0:T(8,128)(2,1)} %copy-done.5, bf16[128,256]{1,0:T(8,128)(2,1)} %bitcast.20, f32[5,64,8192]{2,1,0:T(8,128)} %angle_ref.23), custom_call_target="tpu_custom_call" | custom-call | tf_op jit(solution)/shard_map/level_2/pallas_call | solution.py:155
  126.9 0.7 copy.17
  127.6 0.8 copy-done.14
  128.4 3.9 %level_3.4.held_ref = bf16[128,8192]{1,0:T(8,128)(2,1)} custom-call(bf16[128,2048]{1,0:T(8,128)(2,1)} %level_2.7.state_ref, bf16[128,2048]{1,0:T(8,128)(2,1)} %copy-done.14, bf16[128,256]{1,0:T(8,128)(2,1)} %bitcast.25, f32[5,64,8192]{2,1,0:T(8,128)} %angle_ref.23), custom_call_target="tpu_custom_call" | custom-call | tf_op jit(solution)/shard_map/level_3/pallas_call | solution.py:155
  132.3 0.8 copy-done.8
  133.1 3.9 %level_3.5.held_ref = bf16[128,8192]{1,0:T(8,128)(2,1)} custom-call(bf16[128,2048]{1,0:T(8,128)(2,1)} %level_2.6.state_ref, bf16[128,2048]{1,0:T(8,128)(2,1)} %copy-done.8, bf16[128,256]{1,0:T(8,128)(2,1)} %bitcast.26, f32[5,64,8192]{2,1,0:T(8,128)} %angle_ref.23, bf16[128,8192]{1,0:T(8,128)(2,1)} %level_3.4.held_ref), custom_call_target="tpu_custom_call", output_to_operand_aliasing={{}: (4, {})} | custom-call | tf_op jit(solution)/shard_map/level_3/pallas_call | solution.py:155
  137.1 0.8 copy-done.10
  137.9 3.9 %level_3.6.held_ref = bf16[128,8192]{1,0:T(8,128)(2,1)} custom-call(bf16[128,2048]{1,0:T(8,128)(2,1)} %level_2.5.state_ref, bf16[128,2048]{1,0:T(8,128)(2,1)} %copy-done.10, bf16[128,256]{1,0:T(8,128)(2,1)} %bitcast.27, f32[5,64,8192]{2,1,0:T(8,128)} %angle_ref.23, bf16[128,8192]{1,0:T(8,128)(2,1)} %level_3.5.held_ref), custom_call_target="tpu_custom_call", output_to_operand_aliasing={{}: (4, {})} | custom-call | tf_op jit(solution)/shard_map/level_3/pallas_call | solution.py:155
  141.8 4.4 %collective-permute-done.4.partner_ref = bf16[128,2048]{1,0:T(8,128)(2,1)S(1)} collective-permute-done((bf16[128,2048]{1,0:T(8,128)(2,1)}, bf16[128,2048]{1,0:T(8,128)(2,1)S(1)}, u32[]{:S(2)}, u32[]{:S(2)}) %collective-permute-start.4) | collective-permute-done | bytes 524320 | tf_op jit(solution)/shard_map/ppermute | solution.py:168
  146.2 0.8 copy-done.11
  147.0 3.9 %level_3.7 = bf16[128,8192]{1,0:T(8,128)(2,1)} custom-call(bf16[128,2048]{1,0:T(8,128)(2,1)} %level_2.4.state_ref, bf16[128,2048]{1,0:T(8,128)(2,1)} %copy-done.11, bf16[128,256]{1,0:T(8,128)(2,1)} %bitcast.28, f32[5,64,8192]{2,1,0:T(8,128)} %angle_ref.23, bf16[128,8192]{1,0:T(8,128)(2,1)} %level_3.6.held_ref), custom_call_target="tpu_custom_call", output_to_operand_aliasing={{}: (4, {})} | custom-call | tf_op jit(solution)/shard_map/level_3/pallas_call | solution.py:155
  (40 shorter events, 4.4 us)
Async XLA Ops:
  1.9 45.5 %collective-permute-start.1 = (s16[64,8192]{1,0:T(8,128)(2,1)S(1)}, s16[64,8192]{1,0:T(8,128)(2,1)S(1)}, u32[]{:S(2)}, u32[]{:S(2)}) collective-permute-start(s16[64,8192]{1,0:T(8,128)(2,1)S(1)} %fusion), channel_id=1, source_target_pairs={{0,8},{8,0},{16,24},{24,16},{32,40},{40,32},{48,56},{56,48},{64,72... | collective-permute-start | bytes 3145736 | tf_op jit(solution)/shard_map/ppermute | solution.py:168
  3.6 17.5 %copy-start.13 = (bf16[4,2,2,128,128]{4,3,2,1,0:T(8,128)(2,1)S(1)}, bf16[4,2,2,128,128]{4,3,2,1,0:T(8,128)(2,1)}, u32[]{:S(2)}) copy-start(bf16[4,2,2,128,128]{4,3,2,1,0:T(8,128)(2,1)} %param.11) | copy-start | bytes 1572868
  10.3 30.5 %all-to-all-start = ((bf16[128,16,128]{2,1,0:T(8,128)(2,1)}), bf16[128,16,128]{2,1,0:T(8,128)(2,1)S(1)}, u32[]{:S(2)}, u32[]{:S(2)}) async-start(bf16[128,16,128]{2,1,0:T(8,128)(2,1)} %box_sums.1), calls=%async_computation | async-start | bytes 1048576 | tf_op jit(solution)/shard_map/all_to_all | solution.py:181
  40.8 0.8 copy-start.1
  43.5 3.9 %collective-permute-start = (f32[16,128]{1,0:T(8,128)}, f32[16,128]{1,0:T(8,128)S(1)}, u32[]{:S(2)}, u32[]{:S(2)}) collective-permute-start(f32[16,128]{1,0:T(8,128)} %expand.1.x_ref), channel_id=1, source_target_pairs={{0,8},{8,0},{16,24},{24,16},{32,40},{40,32},{48,56},{56,48},{64,72... | collective-permute-start | bytes 24584 | tf_op jit(solution)/shard_map/ppermute | solution.py:168
  47.4 0.6 copy-start.15
  47.4 1.0 copy-start
  52.9 15.3 %collective-permute-start.11 = (bf16[128,2048]{1,0:T(8,128)(2,1)}, bf16[128,2048]{1,0:T(8,128)(2,1)S(1)}, u32[]{:S(2)}, u32[]{:S(2)}) collective-permute-start(bf16[128,2048]{1,0:T(8,128)(2,1)} %first_level.7.state_ref), channel_id=1, source_target_pairs={{0,1},{1,0},{2,3},{3,2},{4,5},{5,4},{6,7},{7,6},{8,9},{9,8},{10,11... | collective-permute-start | bytes 1572872 | tf_op jit(solution)/shard_map/ppermute | solution.py:168
  57.5 16.1 %collective-permute-start.8 = (bf16[128,2048]{1,0:T(8,128)(2,1)}, bf16[128,2048]{1,0:T(8,128)(2,1)S(1)}, u32[]{:S(2)}, u32[]{:S(2)}) collective-permute-start(bf16[128,2048]{1,0:T(8,128)(2,1)} %first_level.6.state_ref), channel_id=1, source_target_pairs={{0,1},{1,0},{2,3},{3,2},{4,5},{5,4},{6,7},{7,6},{8,9},{9,8},{10,11... | collective-permute-start | bytes 1572872 | tf_op jit(solution)/shard_map/ppermute | solution.py:168
  62.5 18.7 %collective-permute-start.5 = (bf16[128,2048]{1,0:T(8,128)(2,1)}, bf16[128,2048]{1,0:T(8,128)(2,1)S(1)}, u32[]{:S(2)}, u32[]{:S(2)}) collective-permute-start(bf16[128,2048]{1,0:T(8,128)(2,1)} %first_level.5.state_ref), channel_id=1, source_target_pairs={{0,1},{1,0},{2,3},{3,2},{4,5},{5,4},{6,7},{7,6},{8,9},{9,8},{10,11... | collective-permute-start | bytes 1572872 | tf_op jit(solution)/shard_map/ppermute | solution.py:168
  67.1 19.4 %collective-permute-start.2 = (bf16[128,2048]{1,0:T(8,128)(2,1)}, bf16[128,2048]{1,0:T(8,128)(2,1)S(1)}, u32[]{:S(2)}, u32[]{:S(2)}) collective-permute-start(bf16[128,2048]{1,0:T(8,128)(2,1)} %first_level.4.state_ref), channel_id=1, source_target_pairs={{0,1},{1,0},{2,3},{3,2},{4,5},{5,4},{6,7},{7,6},{8,9},{9,8},{10,11... | collective-permute-start | bytes 1572872 | tf_op jit(solution)/shard_map/ppermute | solution.py:168
  68.3 0.8 copy-start.12
  72.9 21.9 %collective-permute-start.12 = (bf16[128,2048]{1,0:T(8,128)(2,1)}, bf16[128,2048]{1,0:T(8,128)(2,1)S(1)}, u32[]{:S(2)}, u32[]{:S(2)}) collective-permute-start(bf16[128,2048]{1,0:T(8,128)(2,1)} %level_1.7.state_ref), channel_id=1, source_target_pairs={{0,16},{8,24},{16,0},{24,8},{32,48},{40,56},{48,32},{56,40},{64,80... | collective-permute-start | bytes 1572872 | tf_op jit(solution)/shard_map/ppermute | solution.py:168
  73.5 0.8 copy-start.9
  78.2 22.4 %collective-permute-start.9 = (bf16[128,2048]{1,0:T(8,128)(2,1)}, bf16[128,2048]{1,0:T(8,128)(2,1)S(1)}, u32[]{:S(2)}, u32[]{:S(2)}) collective-permute-start(bf16[128,2048]{1,0:T(8,128)(2,1)} %level_1.6.state_ref), channel_id=1, source_target_pairs={{0,16},{8,24},{16,0},{24,8},{32,48},{40,56},{48,32},{56,40},{64,80... | collective-permute-start | bytes 1572872 | tf_op jit(solution)/shard_map/ppermute | solution.py:168
  81.2 0.8 copy-start.7
  85.9 26.0 %collective-permute-start.6 = (bf16[128,2048]{1,0:T(8,128)(2,1)}, bf16[128,2048]{1,0:T(8,128)(2,1)S(1)}, u32[]{:S(2)}, u32[]{:S(2)}) collective-permute-start(bf16[128,2048]{1,0:T(8,128)(2,1)} %level_1.5.state_ref), channel_id=1, source_target_pairs={{0,16},{8,24},{16,0},{24,8},{32,48},{40,56},{48,32},{56,40},{64,80... | collective-permute-start | bytes 1572872 | tf_op jit(solution)/shard_map/ppermute | solution.py:168
  86.5 0.8 copy-start.6
  91.2 31.0 %collective-permute-start.3 = (bf16[128,2048]{1,0:T(8,128)(2,1)}, bf16[128,2048]{1,0:T(8,128)(2,1)S(1)}, u32[]{:S(2)}, u32[]{:S(2)}) collective-permute-start(bf16[128,2048]{1,0:T(8,128)(2,1)} %level_1.4.state_ref), channel_id=1, source_target_pairs={{0,16},{8,24},{16,0},{24,8},{32,48},{40,56},{48,32},{56,40},{64,80... | collective-permute-start | bytes 1572872 | tf_op jit(solution)/shard_map/ppermute | solution.py:168
  94.8 0.8 copy-start.2
  99.5 28.1 %collective-permute-start.13 = (bf16[128,2048]{1,0:T(8,128)(2,1)}, bf16[128,2048]{1,0:T(8,128)(2,1)S(1)}, u32[]{:S(2)}, u32[]{:S(2)}) collective-permute-start(bf16[128,2048]{1,0:T(8,128)(2,1)} %level_2.7.state_ref), channel_id=1, source_target_pairs={{0,2},{1,3},{2,0},{3,1},{4,6},{5,7},{6,4},{7,5},{8,10},{9,11},{10,... | collective-permute-start | bytes 1572872 | tf_op jit(solution)/shard_map/ppermute | solution.py:168
  100.7 0.8 copy-start.3
  105.3 27.0 %collective-permute-start.10 = (bf16[128,2048]{1,0:T(8,128)(2,1)}, bf16[128,2048]{1,0:T(8,128)(2,1)S(1)}, u32[]{:S(2)}, u32[]{:S(2)}) collective-permute-start(bf16[128,2048]{1,0:T(8,128)(2,1)} %level_2.6.state_ref), channel_id=1, source_target_pairs={{0,2},{1,3},{2,0},{3,1},{4,6},{5,7},{6,4},{7,5},{8,10},{9,11},{10,... | collective-permute-start | bytes 1572872 | tf_op jit(solution)/shard_map/ppermute | solution.py:168
  111.9 0.8 copy-start.4
  116.6 20.5 %collective-permute-start.7 = (bf16[128,2048]{1,0:T(8,128)(2,1)}, bf16[128,2048]{1,0:T(8,128)(2,1)S(1)}, u32[]{:S(2)}, u32[]{:S(2)}) collective-permute-start(bf16[128,2048]{1,0:T(8,128)(2,1)} %level_2.5.state_ref), channel_id=1, source_target_pairs={{0,2},{1,3},{2,0},{3,1},{4,6},{5,7},{6,4},{7,5},{8,10},{9,11},{10,... | collective-permute-start | bytes 1572872 | tf_op jit(solution)/shard_map/ppermute | solution.py:168
  122.2 0.8 copy-start.5
  126.9 19.3 %collective-permute-start.4 = (bf16[128,2048]{1,0:T(8,128)(2,1)}, bf16[128,2048]{1,0:T(8,128)(2,1)S(1)}, u32[]{:S(2)}, u32[]{:S(2)}) collective-permute-start(bf16[128,2048]{1,0:T(8,128)(2,1)} %level_2.4.state_ref), channel_id=1, source_target_pairs={{0,2},{1,3},{2,0},{3,1},{4,6},{5,7},{6,4},{7,5},{8,10},{9,11},{10,... | collective-permute-start | bytes 1572872 | tf_op jit(solution)/shard_map/ppermute | solution.py:168
  127.6 0.8 copy-start.14
  132.3 0.8 copy-start.8
  137.1 0.8 copy-start.10
  146.2 0.8 copy-start.11

commit v2 on v0

v2 whole, which is shorter than its diff:
```python
import functools

import jax
import jax.numpy as jnp
from jax import lax
from jax.experimental import pallas as pl
from jax.experimental.pallas import tpu as pltpu
from jax.sharding import PartitionSpec as P

BOXES = 16
DIRS = 512
HALF = 64
WIDTH = 128
ROWS = BOXES * DIRS
LEVELS = 4
PARTS = (2, 2, 2, 2, 2, 2, 2, 2)
SENDS = (16,)
SPAN = 1024
FETCHES = 4
ALONG = 4
AHEAD = 4
MIB = 1 << 20

TURN = 32767.0 / 3.141592653589793
SIN_HALF = (0.7071043848991394, -0.02945953793823719, 0.0003670926089398563, -2.0290131033107173e-06)
COS_HALF = (
    1.4142135381698608,
    -0.17677636444568634,
    0.003682575887069106,
    -3.061274401261471e-05,
    1.2791403491974052e-07,
)

ANY = pl.BlockSpec(memory_space=pl.ANY)
VMEM = pl.BlockSpec(memory_space=pltpu.VMEM)
SMEM = pl.BlockSpec(memory_space=pltpu.SMEM)


def near(value):
    return pltpu.with_memory_space_constraint(value, pltpu.VMEM)


def far(value):
    return pltpu.with_memory_space_constraint(value, pltpu.HBM)


def limit(mib):
    return pltpu.CompilerParams(vmem_limit_bytes=mib * MIB)


def kernel_call(*args, **kwargs):
    cost = pl.CostEstimate(flops=1000, bytes_accessed=1000, transcendentals=0)
    return pl.pallas_call(*args, cost_estimate=cost, **kwargs)


def place_of(part):
    axis, shift, count = {"core": ("by", 0, 2), "z": ("by", 1, 4), "x": ("bx", 0, 4), "y": ("bx", 2, 4)}[part]
    return lax.rem(lax.div(lax.axis_index(axis).astype(jnp.int32), jnp.int32(1 << shift)), jnp.int32(count))


def horner(terms, square):
    total = jnp.full_like(square, terms[-1])
    for term in terms[-2::-1]:
        total = total * square + term
    return total


def cos_sin(angle):
    square = angle * angle
    sine = horner(SIN_HALF, square) * angle
    cosine = horner(COS_HALF, square)
    return 1.0 - sine * sine, sine * cosine


def turn(re, im, cosine, sine):
    top = re * cosine - im * sine
    low = re * sine + im * cosine
    return jnp.concatenate([top, low], axis=0).astype(jnp.bfloat16)


def encode_kernel(phases_ref, *rest):
    out_refs, (held, sems) = rest[: len(SENDS)], rest[len(SENDS) :]
    copies = []
    for i, n in enumerate(SENDS):
        cols = pl.ds(sum(SENDS[:i]) * DIRS, n * DIRS)
        copies.append(pltpu.make_async_copy(phases_ref.at[0, :, cols], held.at[:, cols], sems.at[i]))
        copies[-1].start()
    for i, n in enumerate(SENDS):
        copies[i].wait()
        cols = pl.ds(sum(SENDS[:i]) * DIRS, n * DIRS)
        out_refs[i][...] = jnp.round(held[:, cols] * TURN).astype(jnp.int32).astype(jnp.int16)


def encode(phases):
    return kernel_call(
        encode_kernel,
        in_specs=[ANY],
        out_specs=[VMEM] * len(SENDS),
        out_shape=[pltpu.VMEM((HALF, n * DIRS), jnp.int16) for n in SENDS],
        scratch_shapes=[pltpu.VMEM((HALF, ROWS), jnp.float32), pltpu.SemaphoreType.DMA((len(SENDS),))],
        compiler_params=limit(8),
        name="encode",
    )(far(phases))


def fetch_kernel(after_ref, phases_ref, out_ref, sems):
    copies = [pltpu.make_async_copy(phases_ref.at[k], out_ref.at[k], sems.at[k]) for k in range(LEVELS + 1)]
    for copy in copies:
        copy.start()
    for copy in copies:
        copy.wait()


def fetch(after, phases):
    return kernel_call(
        fetch_kernel,
        in_specs=[ANY, ANY],
        out_specs=VMEM,
        out_shape=pltpu.VMEM(phases.shape, jnp.float32),
        scratch_shapes=[pltpu.SemaphoreType.DMA((LEVELS + 1,))],
        compiler_params=limit(2),
        name="fetch",
    )(near(after), far(phases))


def box_sums_kernel(counts_ref, after_ref, tag_hbm_ref, rows_ref, keep_ref, send_ref, tag_ref, held, sems):
    step = WIDTH // FETCHES
    tags = pltpu.make_async_copy(tag_hbm_ref, tag_ref, sems.at[FETCHES])
    tags.start()
    copies = []
    for i in range(FETCHES):
        some = pl.ds(i * step, step)
        copies.append(pltpu.make_async_copy(rows_ref.at[some], held.at[some], sems.at[i]))
        copies[-1].start()
    tags.wait()
    slot = lax.broadcasted_iota(jnp.int32, (BOXES, WIDTH), 1)
    label = lax.broadcasted_iota(jnp.int32, (BOXES, WIDTH), 0)
    first = place_of("core") == 0

    def picks(j):
        hit = jnp.logical_and(tag_ref[j : j + 1, :] == label, slot < counts_ref[0, j])
        return jnp.where(hit, 1.0, 0.0).astype(jnp.bfloat16)

    for i in range(FETCHES):
        copies[i].wait()
        for j in range(i * step, (i + 1) * step, 2):
            left = jnp.concatenate([picks(j), picks(j + 1)], axis=0)
            right = jnp.concatenate([held[j], held[j + 1]], axis=1)
            sums = jnp.dot(left, right, preferred_element_type=jnp.float32)
            even, odd = sums[:BOXES, :WIDTH], sums[BOXES:, WIDTH:]
            keep_ref[j // 2] = jnp.where(first, even, odd).astype(jnp.bfloat16)
            send_ref[j // 2] = jnp.where(first, odd, even).astype(jnp.bfloat16)


def box_sums(counts, after, tag, rows):
    owners = rows.shape[0]
    return kernel_call(
        box_sums_kernel,
        in_specs=[SMEM, ANY, ANY, ANY],
        out_specs=[VMEM] * 2,
        out_shape=[pltpu.VMEM((owners // 2, BOXES, WIDTH), jnp.bfloat16)] * 2,
        scratch_shapes=[
            pltpu.VMEM(tag.shape, jnp.int32),
            pltpu.VMEM(rows.shape, jnp.bfloat16),
            pltpu.SemaphoreType.DMA((FETCHES + 1,)),
        ],
        compiler_params=limit(8),
        name="box_sums",
    )(counts, near(after), far(tag), far(rows))


def spread_kernel(part, inner, after_ref, *refs):
    parts, outs = refs[:-ALONG], refs[-ALONG:]
    place = place_of(part)
    for k, out_ref in enumerate(outs):
        there = jnp.bitwise_xor(place, k)
        if inner:
            for i in range(out_ref.shape[0]):
                total = sum(p[i * ALONG + there].astype(jnp.float32) for p in parts)
                out_ref[i] = total.astype(out_ref.dtype)
        else:
            some = pl.ds(there * out_ref.shape[0], out_ref.shape[0])
            out_ref[...] = sum(p[some].astype(jnp.float32) for p in parts).astype(out_ref.dtype)


def spread(part, inner, after, parts, sent):
    owners = parts[0].shape[0] // ALONG
    kinds = [jnp.float32] + [sent] * (ALONG - 1)
    return kernel_call(
        functools.partial(spread_kernel, part, inner),
        in_specs=[ANY] + [VMEM] * len(parts),
        out_specs=[VMEM] * ALONG,
        out_shape=[pltpu.VMEM((owners, BOXES, WIDTH), kind) for kind in kinds],
        compiler_params=limit(4),
        name="by_" + part,
    )(near(after), *map(near, parts))


def add_kernel(after_ref, *refs):
    refs[-1][...] = sum(r[...] for r in refs[:-1])


def add(after, parts):
    return kernel_call(
        add_kernel,
        in_specs=[ANY] + [VMEM] * len(parts),
        out_specs=VMEM,
        out_shape=pltpu.VMEM(parts[0].shape, jnp.float32),
        compiler_params=limit(4),
        name="add",
    )(near(after), *map(near, parts))


def expand_kernel(map_ref, *refs):
    parts, (mine_ref, other_ref) = refs[:-2], refs[-2:]
    place = place_of("x")
    for there, out_ref in ((place, mine_ref), (jnp.bitwise_xor(place, 1), other_ref)):
        total = sum(p[there] for p in parts).astype(jnp.bfloat16)
        out_ref[...] = jnp.dot(total, map_ref[...], preferred_element_type=jnp.float32)


def expand(source_map, parts):
    return kernel_call(
        expand_kernel,
        in_specs=[VMEM] * (1 + len(parts)),
        out_specs=[VMEM] * 2,
        out_shape=[pltpu.VMEM((BOXES, WIDTH), jnp.float32)] * 2,
        compiler_params=limit(4),
        name="expand",
    )(near(source_map), *map(near, parts))


def mats_kernel(after_ref, trans_ref, *out_refs):
    for level, out_ref in enumerate(out_refs):
        place = place_of(("x", "core", "x", "z")[level])
        pair = trans_ref[level, lax.rem(lax.div(place, jnp.int32(1 + (level == 2))), jnp.int32(2))]
        out_ref[:, :WIDTH] = pair[0].T
        out_ref[:, WIDTH:] = pair[1].T


def pick_mats(after, trans):
    return kernel_call(
        mats_kernel,
        in_specs=[ANY, VMEM],
        out_specs=[VMEM] * LEVELS,
        out_shape=[pltpu.VMEM((WIDTH, 2 * WIDTH), jnp.bfloat16)] * LEVELS,
        compiler_params=limit(4),
        name="mats",
    )(near(after), near(trans))


def column(x_ref, box):
    row = jnp.broadcast_to(x_ref[box : box + 1, :], (8, WIDTH))
    return row.T[:, :1]


def first_kernel(start, boxes, skip, x_ref, other_x_ref, mats_ref, phases_ref, other_ref, *rest):
    out_ref = rest[-1]
    per = min(boxes, SPAN // DIRS)
    for b in range(0, boxes, per):
        both = []
        for box in range(start + b, start + b + per):
            cols = pl.ds(box * DIRS, DIRS)
            mine = column(x_ref, box)
            state = turn(mine[:HALF], mine[HALF:], *cos_sin(phases_ref[0, :, cols]))
            theirs = column(other_x_ref, box)
            there = pl.ds((box - skip) * DIRS, DIRS)
            angle = other_ref[:, there].astype(jnp.int32).astype(jnp.float32) * (1.0 / TURN)
            partner = turn(theirs[:HALF], theirs[HALF:], *cos_sin(angle))
            both.append(jnp.concatenate([state, partner], axis=0))
        mixed = jnp.dot(mats_ref[...], jnp.concatenate(both, axis=1), preferred_element_type=jnp.float32)
        cols = pl.ds((start + b) * DIRS, per * DIRS)
        out_ref[:, b * DIRS : (b + per) * DIRS] = turn(mixed[:HALF], mixed[HALF:], *cos_sin(phases_ref[1, :, cols]))


def first_level(start, boxes, x, other_x, mats, phases, others, after):
    piece = 0
    while start >= sum(SENDS[: piece + 1]):
        piece += 1
    return kernel_call(
        functools.partial(first_kernel, start, boxes, sum(SENDS[:piece])),
        in_specs=[VMEM] * 5 + [ANY] * len(after),
        out_specs=VMEM,
        out_shape=pltpu.VMEM((WIDTH, boxes * DIRS), jnp.bfloat16),
        compiler_params=limit(8),
        name="first_level",
    )(near(x), near(other_x), near(mats), near(phases), near(others[piece]), *map(near, after))


def mix(start, level, cols, state_ref, partner_ref, mats_ref, phases_ref):
    both = jnp.concatenate([state_ref[:, cols], partner_ref[:, cols]], axis=0)
    mixed = jnp.dot(mats_ref[...], both, preferred_element_type=jnp.float32)
    there = pl.ds(start * DIRS + cols.start, cols.size)
    return turn(mixed[:HALF], mixed[HALF:], *cos_sin(phases_ref[level + 1, :, there]))


def spans(boxes):
    size = min(boxes * DIRS, SPAN)
    return [pl.ds(b, size) for b in range(0, boxes * DIRS, size)]


def level_kernel(start, boxes, level, state_ref, partner_ref, mats_ref, phases_ref, *rest):
    out_ref = rest[-1]
    for cols in spans(boxes):
        out_ref[:, cols] = mix(start, level, cols, state_ref, partner_ref, mats_ref, phases_ref)


def next_level(start, boxes, level, state, partner, mats, phases, after):
    return kernel_call(
        functools.partial(level_kernel, start, boxes, level),
        in_specs=[VMEM] * 4 + [ANY] * len(after),
        out_specs=VMEM,
        out_shape=pltpu.VMEM((WIDTH, boxes * DIRS), jnp.bfloat16),
        compiler_params=limit(8),
        name="level_%d" % level,
    )(near(state), near(partner), near(mats), near(phases), *map(near, after))


def last_kernel(start, boxes, state_ref, partner_ref, mats_ref, phases_ref, *rest):
    out_ref, token_ref, held, sems = rest[-4:]
    token_ref[...] = jnp.zeros_like(token_ref)
    copies = []
    for i, cols in enumerate(spans(boxes)):
        held[:, cols] = mix(start, LEVELS - 1, cols, state_ref, partner_ref, mats_ref, phases_ref)
        there = pl.ds(start * DIRS + cols.start, cols.size)
        copies.append(pltpu.make_async_copy(held.at[:, cols], out_ref.at[:, there], sems.at[i]))
        copies[-1].start()
    for copy in copies:
        copy.wait()


def last_level(start, boxes, state, partner, mats, phases, before, after):
    kept = [] if before is None else [far(before)]

    return kernel_call(
        functools.partial(last_kernel, start, boxes),
        in_specs=[VMEM] * 4 + [ANY] * (len(kept) + len(after)),
        out_specs=[ANY, VMEM],
        out_shape=[jax.ShapeDtypeStruct((WIDTH, ROWS), jnp.bfloat16), pltpu.VMEM((8, WIDTH), jnp.float32)],
        input_output_aliases={4: 0} if kept else {},
        scratch_shapes=[
            pltpu.VMEM((WIDTH, boxes * DIRS), jnp.bfloat16),
            pltpu.SemaphoreType.DMA((len(spans(boxes)),)),
        ],
        compiler_params=limit(8),
        name="last_level",
    )(near(state), near(partner), near(mats), near(phases), *kept, *map(near, after))


def move(value, axis, mask):
    return lax.ppermute(value, axis, [(s, s ^ mask) for s in range(lax.axis_size(axis))])


def per_device(currents, counts, box_of, source_map, phases, trans):
    turns = encode(phases)
    others = [move(t, "bx", 1) for t in turns]
    keep, send = box_sums(counts, turns[0], box_of[0], currents[0])
    got = move(send, "by", 1)
    own, *sent = spread("z", True, keep, [keep, got], jnp.bfloat16)
    angles = fetch(own, phases)
    got = [move(v, "by", 2 * k + 2) for k, v in enumerate(sent)]
    own, *sent = spread("y", False, angles, [own] + got, jnp.float32)
    mats = pick_mats(own, trans)
    row = add(mats[0], [own] + [move(v, "bx", 4 * k + 4) for k, v in enumerate(sent)])
    mine, theirs = expand(source_map, [row] + [move(row, "bx", k) for k in (1, 2, 3)])

    starts = [sum(PARTS[:i]) for i in range(len(PARTS))]
    count = len(PARTS)
    states = [{}, {}, {}, {}]
    latest = []

    def step(level, i):
        if not 0 <= i < count:
            return
        where = (starts[i], PARTS[i])
        after = latest[-1:]
        if level == 0:
            done = first_level(*where, mine, theirs, mats[0], angles, others, after)
        else:
            value = states[level - 1][i]
            other = move(value, *(("by", 1), ("bx", 2), ("by", 2))[level - 1])
            if level < 3:
                done = next_level(*where, level, value, other, mats[level], angles, after)
            else:
                states[3][i], done = last_level(*where, value, other, mats[level], angles, states[3].get(i - 1), after)
        if level < 3:
            states[level][i] = done
        latest.append(done)

    for i in range(-AHEAD, count + 2):
        step(0, i + AHEAD)
        step(1, i + AHEAD - 1)
        step(2, i)
        step(3, i - 2)
    return states[3][count - 1]


def solution(mesh):
    placed = (
        P(("bx", "by"), None, None, None),
        P(("bx", "by"), None),
        P(("bx", "by"), None, None),
        P(),
        P(None, None, ("bx", "by")),
        P(),
    )
    return jax.shard_map(
        per_device, mesh=mesh, in_specs=placed, out_specs=P(None, ("bx", "by")), check_vma=False
    )
```

time: 298 us -> 109 us (0.37)
  waiting for transfers between devices: 143 us -> 43.1 us
  blocking collectives: 79 us -> 0 us
  other arithmetic: 52.3 us -> 0 us
  starting transfers between devices: 2.75 us -> 34.2 us
  Pallas kernels: 0 us -> 30.6 us
  matrix products: 15.4 us -> 0 us
  local copies, waits for them, and re-layouts: 4.8 us -> 0.02 us
    ppermute x4 -> x35, waiting for transfers between devices: 143 us -> 43.1 us  [move(): lax.ppermute(value, axis, [(s, s ^ mask) for s in range(lax.axis_size(axi...]
    all_to_all x2 -> x0, blocking collectives: 79 us -> none  [the longest x1 58.6 us: per_device(): lax.all_to_all(rows, ('bx', 'by'), split_axis=0, concat_axis=0, tiled=True)]
    another operation x5 -> x0, other arithmetic: 44 us -> none
    ppermute x4 -> x35, starting transfers between devices: 2.75 us -> 34.2 us  [move(): lax.ppermute(value, axis, [(s, s ^ mask) for s in range(lax.axis_size(axi...]
    pallas_call x0 -> x40, Pallas kernels: none -> 30.6 us  [the longest x8 8.97 us: last_level(): kernel_call(functools.partial(last_kernel, start, boxes), in_specs=[VMEM]...]
    dot_general x9 -> x0, matrix products: 15.4 us -> none  [the longest x4 9.47 us: advance(): jnp.einsum('io,ir->or', mats[1], partner, preferred_element_type=jnp.floa...]
    concatenate x5 -> x0, other arithmetic: 7.32 us -> none  [rotate(): jnp.concatenate([re * cosine - im * sine, re * sine + im * cosine], axis=0)]
    unnamed x10 -> x6, local copies, waits for them, and re-layouts: 4.11 us -> 0.02 us
  transfers between devices with their start and end apart: 4 -> 35, of which waited for: 4 -> 18; matrix products, arithmetic and copies ran while one was open for 1% -> 0% of each run, Pallas kernels for 0% -> 24%
where the time goes in v2:
time: 109 us
  waiting for transfers between devices  43.1 us (40%)
  starting transfers between devices  34.2 us (31%)
  Pallas kernels  30.6 us (28%)
    ppermute x35, waiting for transfers between devices, move(): lax.ppermute(value, axis, [(s, s ^ mask) for s in range(lax.axis_size(axi...  43.1 us
    ppermute x35, starting transfers between devices, move(): lax.ppermute(value, axis, [(s, s ^ mask) for s in range(lax.axis_size(axi...  34.2 us
    pallas_call x8, Pallas kernels, last_level(): kernel_call(functools.partial(last_kernel, start, boxes), in_specs=[VMEM]...  8.97 us
    pallas_call x8, Pallas kernels, first_level(): kernel_call(functools.partial(first_kernel, start, boxes, sum(SENDS[:piec...  7.01 us
    pallas_call x16, Pallas kernels, next_level(): kernel_call(functools.partial(level_kernel, start, boxes, level), in_spec...  5.31 us
    pallas_call x1, Pallas kernels, fetch(): kernel_call(fetch_kernel, in_specs=[ANY, ANY], out_specs=VMEM, out_shape=...  4.11 us
    pallas_call x1, Pallas kernels, box_sums(): kernel_call(box_sums_kernel, in_specs=[SMEM, ANY, ANY, ANY], out_specs=[V...  3.07 us
  transfers between devices with their start and end apart: 35, of which 18 were waited for; matrix products, arithmetic and copies ran while one was open for 0% of the time, Pallas kernels for 24%

profile of v2, /device:TPU:0, one launch (start us, length us, event | category | flops | bytes accessed | tf_op | source)
XLA Modules:
  0.0 108.6 jit_solution(16197447226638023340)
XLA Ops:
  0.0 1.8 %encode.1.after_ref = s16[64,8192]{1,0:T(8,128)(2,1)S(1)} custom-call(f32[5,64,8192]{2,1,0:T(8,128)} %phases_ref.3), custom_call_target="tpu_custom_call" | custom-call | flops 1000 | bytes 1000 | tf_op jit(solution)/shard_map/encode/pallas_call | solution.py:95
  1.8 1.7 %collective-permute-start.10 = (s16[64,8192]{1,0:T(8,128)(2,1)S(1)}, s16[64,8192]{1,0:T(8,128)(2,1)S(1)}, u32[]{:S(2)}, u32[]{:S(2)}) collective-permute-start(s16[64,8192]{1,0:T(8,128)(2,1)S(1)} %encode.1.after_ref), channel_id=1, source_target_pairs={{0,8},{8,0},{16,24},{24,16},{32,40},{40,32},{48,56},{56,48},{64,72... | collective-permute-start | bytes 3145736 | tf_op jit(solution)/shard_map/ppermute | solution.py:351
  3.5 3.1 %box_sums.1 = (bf16[64,16,128]{2,1,0:T(8,128)(2,1)S(1)}, bf16[64,16,128]{2,1,0:T(8,128)(2,1)S(1)}) custom-call(s32[1,128]{1,0:T(1,128)S(1)} %copy-done.2, s16[64,8192]{1,0:T(8,128)(2,1)S(1)} %encode.1.after_ref, s32[128,128]{1,0:T(8,128)} %bitcast.3, bf16[128,128,128]{2,1,0:T(8,128)(2,1)} %bitcast.2), custom_call_target="tpu_custom_call" | custom-call | flops 1000 | bytes 1000 | tf_op jit(solution)/shard_map/box_sums/pallas_call | solution.py:157
  6.6 1.5 %collective-permute-done.refs_1_ = bf16[64,16,128]{2,1,0:T(8,128)(2,1)S(1)} collective-permute-done((bf16[64,16,128]{2,1,0:T(8,128)(2,1)S(1)}, bf16[64,16,128]{2,1,0:T(8,128)(2,1)S(1)}, u32[]{:S(2)}, u32[]{:S(2)}) %collective-permute-start) | collective-permute-done | bytes 262176 | tf_op jit(solution)/shard_map/ppermute | solution.py:351
  8.2 2.0 %collective-permute-start.1 = (bf16[16,16,128]{2,1,0:T(8,128)(2,1)S(1)}, bf16[16,16,128]{2,1,0:T(8,128)(2,1)S(1)}, u32[]{:S(2)}, u32[]{:S(2)}) collective-permute-start(bf16[16,16,128]{2,1,0:T(8,128)(2,1)S(1)} %get-tuple-element.39), channel_id=1, source_target_pairs={{0,2},{1,3},{2,0},{3,1},{4,6},{5,7},{6,4},{7,5},{8,10},{9,11},{10,... | collective-permute-start | bytes 196616 | tf_op jit(solution)/shard_map/ppermute | solution.py:351
  10.2 3.6 %collective-permute-start.2 = (bf16[16,16,128]{2,1,0:T(8,128)(2,1)S(1)}, bf16[16,16,128]{2,1,0:T(8,128)(2,1)S(1)}, u32[]{:S(2)}, u32[]{:S(2)}) collective-permute-start(bf16[16,16,128]{2,1,0:T(8,128)(2,1)S(1)} %get-tuple-element.40), channel_id=1, source_target_pairs={{0,4},{1,5},{2,6},{3,7},{4,0},{5,1},{6,2},{7,3},{8,12},{9,13},{10,... | collective-permute-start | bytes 196616 | tf_op jit(solution)/shard_map/ppermute | solution.py:351
  13.8 4.1 %fetch.1.after_ref.phases_ref = f32[5,64,8192]{2,1,0:T(8,128)S(1)} custom-call(f32[16,16,128]{2,1,0:T(8,128)S(1)} %get-tuple-element.38.after_ref.refs_0_, f32[5,64,8192]{2,1,0:T(8,128)} %phases_ref.3), custom_call_target="tpu_custom_call" | custom-call | flops 1000 | bytes 1000 | tf_op jit(solution)/shard_map/fetch/pallas_call | solution.py:115
  18.0 1.3 %collective-permute-done.3.refs_3_ = bf16[16,16,128]{2,1,0:T(8,128)(2,1)S(1)} collective-permute-done((bf16[16,16,128]{2,1,0:T(8,128)(2,1)S(1)}, bf16[16,16,128]{2,1,0:T(8,128)(2,1)S(1)}, u32[]{:S(2)}, u32[]{:S(2)}) %collective-permute-start.3) | collective-permute-done | bytes 65568 | tf_op jit(solution)/shard_map/ppermute | solution.py:351
  19.3 1.7 %collective-permute-start.4 = (f32[4,16,128]{2,1,0:T(8,128)S(1)}, f32[4,16,128]{2,1,0:T(8,128)S(1)}, u32[]{:S(2)}, u32[]{:S(2)}) collective-permute-start(f32[4,16,128]{2,1,0:T(8,128)S(1)} %get-tuple-element.44), channel_id=1, source_target_pairs={{0,32},{8,40},{16,48},{24,56},{32,0},{40,8},{48,16},{56,24},{64,96... | collective-permute-start | bytes 98312 | tf_op jit(solution)/shard_map/ppermute | solution.py:351
  21.0 2.9 %collective-permute-start.5 = (f32[4,16,128]{2,1,0:T(8,128)S(1)}, f32[4,16,128]{2,1,0:T(8,128)S(1)}, u32[]{:S(2)}, u32[]{:S(2)}) collective-permute-start(f32[4,16,128]{2,1,0:T(8,128)S(1)} %get-tuple-element.45), channel_id=1, source_target_pairs={{0,64},{8,72},{16,80},{24,88},{32,96},{40,104},{48,112},{56,120},{... | collective-permute-start | bytes 98312 | tf_op jit(solution)/shard_map/ppermute | solution.py:351
  24.2 2.2 %collective-permute-done.5.refs_2_ = f32[4,16,128]{2,1,0:T(8,128)S(1)} collective-permute-done((f32[4,16,128]{2,1,0:T(8,128)S(1)}, f32[4,16,128]{2,1,0:T(8,128)S(1)}, u32[]{:S(2)}, u32[]{:S(2)}) %collective-permute-start.5) | collective-permute-done | bytes 32800 | tf_op jit(solution)/shard_map/ppermute | solution.py:351
  26.4 2.6 %collective-permute-done.6.refs_3_ = f32[4,16,128]{2,1,0:T(8,128)S(1)} collective-permute-done((f32[4,16,128]{2,1,0:T(8,128)S(1)}, f32[4,16,128]{2,1,0:T(8,128)S(1)}, u32[]{:S(2)}, u32[]{:S(2)}) %collective-permute-start.6) | collective-permute-done | bytes 32800 | tf_op jit(solution)/shard_map/ppermute | solution.py:351
  29.6 3.0 %collective-permute-start.8 = (f32[4,16,128]{2,1,0:T(8,128)S(1)}, f32[4,16,128]{2,1,0:T(8,128)S(1)}, u32[]{:S(2)}, u32[]{:S(2)}) collective-permute-start(f32[4,16,128]{2,1,0:T(8,128)S(1)} %add.1.refs_0_), channel_id=1, source_target_pairs={{0,16},{8,24},{16,0},{24,8},{32,48},{40,56},{48,32},{56,40},{64,80... | collective-permute-start | bytes 98312 | tf_op jit(solution)/shard_map/ppermute | solution.py:351
  32.6 1.1 %collective-permute-start.9 = (f32[4,16,128]{2,1,0:T(8,128)S(1)}, f32[4,16,128]{2,1,0:T(8,128)S(1)}, u32[]{:S(2)}, u32[]{:S(2)}) collective-permute-start(f32[4,16,128]{2,1,0:T(8,128)S(1)} %add.1.refs_0_), channel_id=1, source_target_pairs={{0,24},{8,16},{16,8},{24,0},{32,56},{40,48},{48,40},{56,32},{64,88... | collective-permute-start | bytes 98312 | tf_op jit(solution)/shard_map/ppermute | solution.py:351
  33.8 1.3 %collective-permute-done.8.refs_2_ = f32[4,16,128]{2,1,0:T(8,128)S(1)} collective-permute-done((f32[4,16,128]{2,1,0:T(8,128)S(1)}, f32[4,16,128]{2,1,0:T(8,128)S(1)}, u32[]{:S(2)}, u32[]{:S(2)}) %collective-permute-start.8) | collective-permute-done | bytes 32800 | tf_op jit(solution)/shard_map/ppermute | solution.py:351
  35.0 2.7 %collective-permute-done.9.refs_3_ = f32[4,16,128]{2,1,0:T(8,128)S(1)} collective-permute-done((f32[4,16,128]{2,1,0:T(8,128)S(1)}, f32[4,16,128]{2,1,0:T(8,128)S(1)}, u32[]{:S(2)}, u32[]{:S(2)}) %collective-permute-start.9) | collective-permute-done | bytes 32800 | tf_op jit(solution)/shard_map/ppermute | solution.py:351
  37.9 0.9 first_level.8.rest_0_.state_ref
  38.9 0.9 first_level.9.rest_0_.state_ref
  40.8 0.9 first_level.10.rest_0_.state_ref
  42.2 0.9 first_level.11.rest_0_.state_ref
  44.2 0.9 first_level.12.rest_0_.state_ref
  45.2 3.5 %collective-permute-start.19 = (bf16[128,1024]{1,0:T(8,128)(2,1)S(1)}, bf16[128,1024]{1,0:T(8,128)(2,1)S(1)}, u32[]{:S(2)}, u32[]{:S(2)}) collective-permute-start(bf16[128,1024]{1,0:T(8,128)(2,1)S(1)} %level_1.9.rest_0_.state_ref), channel_id=1, source_target_pairs={{0,16},{8,24},{16,0},{24,8},{32,48},{40,56},{48,32},{56,40},{64,80... | collective-permute-start | bytes 786440 | tf_op jit(solution)/shard_map/ppermute | solution.py:351
  49.0 5.2 %collective-permute-done.12.partner_ref = bf16[128,1024]{1,0:T(8,128)(2,1)S(1)} collective-permute-done((bf16[128,1024]{1,0:T(8,128)(2,1)S(1)}, bf16[128,1024]{1,0:T(8,128)(2,1)S(1)}, u32[]{:S(2)}, u32[]{:S(2)}) %collective-permute-start.12) | collective-permute-done | bytes 262176 | tf_op jit(solution)/shard_map/ppermute | solution.py:351
  54.5 0.9 first_level.13.rest_0_.state_ref
  56.1 2.9 %collective-permute-done.19.partner_ref = bf16[128,1024]{1,0:T(8,128)(2,1)S(1)} collective-permute-done((bf16[128,1024]{1,0:T(8,128)(2,1)S(1)}, bf16[128,1024]{1,0:T(8,128)(2,1)S(1)}, u32[]{:S(2)}, u32[]{:S(2)}) %collective-permute-start.19) | collective-permute-done | bytes 262176 | tf_op jit(solution)/shard_map/ppermute | solution.py:351
  59.3 0.9 first_level.14.rest_0_.state_ref
  61.0 1.9 %collective-permute-start.22 = (bf16[128,1024]{1,0:T(8,128)(2,1)S(1)}, bf16[128,1024]{1,0:T(8,128)(2,1)S(1)}, u32[]{:S(2)}, u32[]{:S(2)}) collective-permute-start(bf16[128,1024]{1,0:T(8,128)(2,1)S(1)} %level_2.9.rest_0_.state_ref), channel_id=1, source_target_pairs={{0,2},{1,3},{2,0},{3,1},{4,6},{5,7},{6,4},{7,5},{8,10},{9,11},{10,... | collective-permute-start | bytes 786440 | tf_op jit(solution)/shard_map/ppermute | solution.py:351
  63.2 3.0 %collective-permute-done.17.partner_ref = bf16[128,1024]{1,0:T(8,128)(2,1)S(1)} collective-permute-done((bf16[128,1024]{1,0:T(8,128)(2,1)S(1)}, bf16[128,1024]{1,0:T(8,128)(2,1)S(1)}, u32[]{:S(2)}, u32[]{:S(2)}) %collective-permute-start.17) | collective-permute-done | bytes 262176 | tf_op jit(solution)/shard_map/ppermute | solution.py:351
  66.6 1.1 last_level.8
  67.6 0.9 first_level.15.rest_0_.state_ref
  68.6 1.8 %collective-permute-start.26 = (bf16[128,1024]{1,0:T(8,128)(2,1)S(1)}, bf16[128,1024]{1,0:T(8,128)(2,1)S(1)}, u32[]{:S(2)}, u32[]{:S(2)}) collective-permute-start(bf16[128,1024]{1,0:T(8,128)(2,1)S(1)} %level_1.12.rest_0_.state_ref), channel_id=1, source_target_pairs={{0,16},{8,24},{16,0},{24,8},{32,48},{40,56},{48,32},{56,40},{64,80... | collective-permute-start | bytes 786440 | tf_op jit(solution)/shard_map/ppermute | solution.py:351
  71.4 1.3 %collective-permute-start.30 = (bf16[128,1024]{1,0:T(8,128)(2,1)S(1)}, bf16[128,1024]{1,0:T(8,128)(2,1)S(1)}, u32[]{:S(2)}, u32[]{:S(2)}) collective-permute-start(bf16[128,1024]{1,0:T(8,128)(2,1)S(1)} %level_1.13.rest_0_.state_ref), channel_id=1, source_target_pairs={{0,16},{8,24},{16,0},{24,8},{32,48},{40,56},{48,32},{56,40},{64,80... | collective-permute-start | bytes 786440 | tf_op jit(solution)/shard_map/ppermute | solution.py:351
  73.0 2.1 %collective-permute-start.28 = (bf16[128,1024]{1,0:T(8,128)(2,1)S(1)}, bf16[128,1024]{1,0:T(8,128)(2,1)S(1)}, u32[]{:S(2)}, u32[]{:S(2)}) collective-permute-start(bf16[128,1024]{1,0:T(8,128)(2,1)S(1)} %level_2.11.rest_1_.state_ref), channel_id=1, source_target_pairs={{0,2},{1,3},{2,0},{3,1},{4,6},{5,7},{6,4},{7,5},{8,10},{9,11},{10,... | collective-permute-start | bytes 786440 | tf_op jit(solution)/shard_map/ppermute | solution.py:351
  75.1 1.0 last_level.9
  76.2 1.8 %collective-permute-start.31 = (bf16[128,1024]{1,0:T(8,128)(2,1)S(1)}, bf16[128,1024]{1,0:T(8,128)(2,1)S(1)}, u32[]{:S(2)}, u32[]{:S(2)}) collective-permute-start(bf16[128,1024]{1,0:T(8,128)(2,1)S(1)} %level_1.14.rest_0_.state_ref), channel_id=1, source_target_pairs={{0,16},{8,24},{16,0},{24,8},{32,48},{40,56},{48,32},{56,40},{64,80... | collective-permute-start | bytes 786440 | tf_op jit(solution)/shard_map/ppermute | solution.py:351
  78.3 1.0 collective-permute-done.26.partner_ref
  79.7 1.8 %collective-permute-start.25 = (bf16[128,1024]{1,0:T(8,128)(2,1)S(1)}, bf16[128,1024]{1,0:T(8,128)(2,1)S(1)}, u32[]{:S(2)}, u32[]{:S(2)}) collective-permute-start(bf16[128,1024]{1,0:T(8,128)(2,1)S(1)} %level_1.15.rest_0_.state_ref), channel_id=1, source_target_pairs={{0,16},{8,24},{16,0},{24,8},{32,48},{40,56},{48,32},{56,40},{64,80... | collective-permute-start | bytes 786440 | tf_op jit(solution)/shard_map/ppermute | solution.py:351
  81.5 1.0 last_level.10
  82.6 2.3 %collective-permute-done.30.partner_ref = bf16[128,1024]{1,0:T(8,128)(2,1)S(1)} collective-permute-done((bf16[128,1024]{1,0:T(8,128)(2,1)S(1)}, bf16[128,1024]{1,0:T(8,128)(2,1)S(1)}, u32[]{:S(2)}, u32[]{:S(2)}) %collective-permute-start.30) | collective-permute-done | bytes 262176 | tf_op jit(solution)/shard_map/ppermute | solution.py:351
  85.4 1.1 last_level.11
  86.4 4.1 %collective-permute-done.31.partner_ref = bf16[128,1024]{1,0:T(8,128)(2,1)S(1)} collective-permute-done((bf16[128,1024]{1,0:T(8,128)(2,1)S(1)}, bf16[128,1024]{1,0:T(8,128)(2,1)S(1)}, u32[]{:S(2)}, u32[]{:S(2)}) %collective-permute-start.31) | collective-permute-done | bytes 262176 | tf_op jit(solution)/shard_map/ppermute | solution.py:351
  91.0 1.1 last_level.12
  92.0 3.6 %collective-permute-done.25.partner_ref = bf16[128,1024]{1,0:T(8,128)(2,1)S(1)} collective-permute-done((bf16[128,1024]{1,0:T(8,128)(2,1)S(1)}, bf16[128,1024]{1,0:T(8,128)(2,1)S(1)}, u32[]{:S(2)}, u32[]{:S(2)}) %collective-permute-start.25) | collective-permute-done | bytes 262176 | tf_op jit(solution)/shard_map/ppermute | solution.py:351
  96.4 1.0 last_level.13
  97.5 4.6 %collective-permute-done.33.partner_ref = bf16[128,1024]{1,0:T(8,128)(2,1)S(1)} collective-permute-done((bf16[128,1024]{1,0:T(8,128)(2,1)S(1)}, bf16[128,1024]{1,0:T(8,128)(2,1)S(1)}, u32[]{:S(2)}, u32[]{:S(2)}) %collective-permute-start.33) | collective-permute-done | bytes 262176 | tf_op jit(solution)/shard_map/ppermute | solution.py:351
  102.0 1.0 last_level.14
  103.1 3.8 %collective-permute-done.32.partner_ref = bf16[128,1024]{1,0:T(8,128)(2,1)S(1)} collective-permute-done((bf16[128,1024]{1,0:T(8,128)(2,1)S(1)}, bf16[128,1024]{1,0:T(8,128)(2,1)S(1)}, u32[]{:S(2)}, u32[]{:S(2)}) %collective-permute-start.32) | collective-permute-done | bytes 262176 | tf_op jit(solution)/shard_map/ppermute | solution.py:351
  106.8 1.6 %last_level.15 = (bf16[128,8192]{1,0:T(8,128)(2,1)}, f32[8,128]{1,0:T(8,128)}) custom-call(bf16[128,1024]{1,0:T(8,128)(2,1)S(1)} %level_2.15.rest_1_.state_ref, bf16[128,1024]{1,0:T(8,128)(2,1)S(1)} %collective-permute-done.32.partner_ref, bf16[128,256]{1,0:T(8,128)(2,1)S(1)} %get-tuple-element.51.mats_ref, ...), custom_call_target="tpu_custom_call", output_to_operand_aliasing={{0}: (4, {})} | custom-call | flops 1000 | bytes 1000 | tf_op jit(solution)/shard_map/last_level/pallas_call | solution.py:335
  (68 shorter events, 10.8 us)
Async XLA Ops:
  0.0 3.5 %copy-start.2 = (s32[1,128]{1,0:T(1,128)S(1)}, s32[1,128]{1,0:T(1,128)}, u32[]{:S(2)}) copy-start(s32[1,128]{1,0:T(1,128)} %counts_ref.1) | copy-start | bytes 1540
  1.8 36.1 %collective-permute-start.10 = (s16[64,8192]{1,0:T(8,128)(2,1)S(1)}, s16[64,8192]{1,0:T(8,128)(2,1)S(1)}, u32[]{:S(2)}, u32[]{:S(2)}) collective-permute-start(s16[64,8192]{1,0:T(8,128)(2,1)S(1)} %encode.1.after_ref), channel_id=1, source_target_pairs={{0,8},{8,0},{16,24},{24,16},{32,40},{40,32},{48,56},{56,48},{64,72... | collective-permute-start | bytes 3145736 | tf_op jit(solution)/shard_map/ppermute | solution.py:351
  6.5 1.6 %collective-permute-start = (bf16[64,16,128]{2,1,0:T(8,128)(2,1)S(1)}, bf16[64,16,128]{2,1,0:T(8,128)(2,1)S(1)}, u32[]{:S(2)}, u32[]{:S(2)}) collective-permute-start(bf16[64,16,128]{2,1,0:T(8,128)(2,1)S(1)} %get-tuple-element.37), channel_id=1, source_target_pairs={{0,1},{1,0},{2,3},{3,2},{4,5},{5,4},{6,7},{7,6},{8,9},{9,8},{10,11... | collective-permute-start | bytes 786440 | tf_op jit(solution)/shard_map/ppermute | solution.py:351
  8.2 9.7 %collective-permute-start.1 = (bf16[16,16,128]{2,1,0:T(8,128)(2,1)S(1)}, bf16[16,16,128]{2,1,0:T(8,128)(2,1)S(1)}, u32[]{:S(2)}, u32[]{:S(2)}) collective-permute-start(bf16[16,16,128]{2,1,0:T(8,128)(2,1)S(1)} %get-tuple-element.39), channel_id=1, source_target_pairs={{0,2},{1,3},{2,0},{3,1},{4,6},{5,7},{6,4},{7,5},{8,10},{9,11},{10,... | collective-permute-start | bytes 196616 | tf_op jit(solution)/shard_map/ppermute | solution.py:351
  10.2 7.7 %collective-permute-start.2 = (bf16[16,16,128]{2,1,0:T(8,128)(2,1)S(1)}, bf16[16,16,128]{2,1,0:T(8,128)(2,1)S(1)}, u32[]{:S(2)}, u32[]{:S(2)}) collective-permute-start(bf16[16,16,128]{2,1,0:T(8,128)(2,1)S(1)} %get-tuple-element.40), channel_id=1, source_target_pairs={{0,4},{1,5},{2,6},{3,7},{4,0},{5,1},{6,2},{7,3},{8,12},{9,13},{10,... | collective-permute-start | bytes 196616 | tf_op jit(solution)/shard_map/ppermute | solution.py:351
  13.8 5.5 %collective-permute-start.3 = (bf16[16,16,128]{2,1,0:T(8,128)(2,1)S(1)}, bf16[16,16,128]{2,1,0:T(8,128)(2,1)S(1)}, u32[]{:S(2)}, u32[]{:S(2)}) collective-permute-start(bf16[16,16,128]{2,1,0:T(8,128)(2,1)S(1)} %get-tuple-element.41), channel_id=1, source_target_pairs={{0,6},{1,7},{2,4},{3,5},{4,2},{5,3},{6,0},{7,1},{8,14},{9,15},{10,... | collective-permute-start | bytes 196616 | tf_op jit(solution)/shard_map/ppermute | solution.py:351
  17.9 6.2 %copy-start = (bf16[4,2,2,128,128]{4,3,2,1,0:T(8,128)(2,1)S(1)}, bf16[4,2,2,128,128]{4,3,2,1,0:T(8,128)(2,1)}, u32[]{:S(2)}) copy-start(bf16[4,2,2,128,128]{4,3,2,1,0:T(8,128)(2,1)} %trans_ref.1) | copy-start | bytes 1572868
  17.9 19.8 %copy-start.1 = (bf16[128,128]{1,0:T(8,128)(2,1)S(1)}, bf16[128,128]{1,0:T(8,128)(2,1)}, u32[]{:S(2)}) copy-start(bf16[128,128]{1,0:T(8,128)(2,1)} %map_ref.1) | copy-start | bytes 98308
  19.3 4.9 %collective-permute-start.4 = (f32[4,16,128]{2,1,0:T(8,128)S(1)}, f32[4,16,128]{2,1,0:T(8,128)S(1)}, u32[]{:S(2)}, u32[]{:S(2)}) collective-permute-start(f32[4,16,128]{2,1,0:T(8,128)S(1)} %get-tuple-element.44), channel_id=1, source_target_pairs={{0,32},{8,40},{16,48},{24,56},{32,0},{40,8},{48,16},{56,24},{64,96... | collective-permute-start | bytes 98312 | tf_op jit(solution)/shard_map/ppermute | solution.py:351
  21.0 5.4 %collective-permute-start.5 = (f32[4,16,128]{2,1,0:T(8,128)S(1)}, f32[4,16,128]{2,1,0:T(8,128)S(1)}, u32[]{:S(2)}, u32[]{:S(2)}) collective-permute-start(f32[4,16,128]{2,1,0:T(8,128)S(1)} %get-tuple-element.45), channel_id=1, source_target_pairs={{0,64},{8,72},{16,80},{24,88},{32,96},{40,104},{48,112},{56,120},{... | collective-permute-start | bytes 98312 | tf_op jit(solution)/shard_map/ppermute | solution.py:351
  23.9 5.1 %collective-permute-start.6 = (f32[4,16,128]{2,1,0:T(8,128)S(1)}, f32[4,16,128]{2,1,0:T(8,128)S(1)}, u32[]{:S(2)}, u32[]{:S(2)}) collective-permute-start(f32[4,16,128]{2,1,0:T(8,128)S(1)} %get-tuple-element.46), channel_id=1, source_target_pairs={{0,96},{8,104},{16,112},{24,120},{32,64},{40,72},{48,80},{56,88},{... | collective-permute-start | bytes 98312 | tf_op jit(solution)/shard_map/ppermute | solution.py:351
  29.0 4.8 %collective-permute-start.7 = (f32[4,16,128]{2,1,0:T(8,128)S(1)}, f32[4,16,128]{2,1,0:T(8,128)S(1)}, u32[]{:S(2)}, u32[]{:S(2)}) collective-permute-start(f32[4,16,128]{2,1,0:T(8,128)S(1)} %add.1.refs_0_), channel_id=1, source_target_pairs={{0,8},{8,0},{16,24},{24,16},{32,40},{40,32},{48,56},{56,48},{64,72... | collective-permute-start | bytes 98312 | tf_op jit(solution)/shard_map/ppermute | solution.py:351
  29.6 5.4 %collective-permute-start.8 = (f32[4,16,128]{2,1,0:T(8,128)S(1)}, f32[4,16,128]{2,1,0:T(8,128)S(1)}, u32[]{:S(2)}, u32[]{:S(2)}) collective-permute-start(f32[4,16,128]{2,1,0:T(8,128)S(1)} %add.1.refs_0_), channel_id=1, source_target_pairs={{0,16},{8,24},{16,0},{24,8},{32,48},{40,56},{48,32},{56,40},{64,80... | collective-permute-start | bytes 98312 | tf_op jit(solution)/shard_map/ppermute | solution.py:351
  32.6 5.1 %collective-permute-start.9 = (f32[4,16,128]{2,1,0:T(8,128)S(1)}, f32[4,16,128]{2,1,0:T(8,128)S(1)}, u32[]{:S(2)}, u32[]{:S(2)}) collective-permute-start(f32[4,16,128]{2,1,0:T(8,128)S(1)} %add.1.refs_0_), channel_id=1, source_target_pairs={{0,24},{8,16},{16,8},{24,0},{32,56},{40,48},{48,40},{56,32},{64,88... | collective-permute-start | bytes 98312 | tf_op jit(solution)/shard_map/ppermute | solution.py:351
  38.8 1.6 %collective-permute-start.11 = (bf16[128,1024]{1,0:T(8,128)(2,1)S(1)}, bf16[128,1024]{1,0:T(8,128)(2,1)S(1)}, u32[]{:S(2)}, u32[]{:S(2)}) collective-permute-start(bf16[128,1024]{1,0:T(8,128)(2,1)S(1)} %first_level.8.rest_0_.state_ref), channel_id=1, source_target_pairs={{0,1},{1,0},{2,3},{3,2},{4,5},{5,4},{6,7},{7,6},{8,9},{9,8},{10,11... | collective-permute-start | bytes 786440 | tf_op jit(solution)/shard_map/ppermute | solution.py:351
  39.8 2.1 %collective-permute-start.13 = (bf16[128,1024]{1,0:T(8,128)(2,1)S(1)}, bf16[128,1024]{1,0:T(8,128)(2,1)S(1)}, u32[]{:S(2)}, u32[]{:S(2)}) collective-permute-start(bf16[128,1024]{1,0:T(8,128)(2,1)S(1)} %first_level.9.rest_0_.state_ref), channel_id=1, source_target_pairs={{0,1},{1,0},{2,3},{3,2},{4,5},{5,4},{6,7},{7,6},{8,9},{9,8},{10,11... | collective-permute-start | bytes 786440 | tf_op jit(solution)/shard_map/ppermute | solution.py:351
  41.6 2.2 %collective-permute-start.15 = (bf16[128,1024]{1,0:T(8,128)(2,1)S(1)}, bf16[128,1024]{1,0:T(8,128)(2,1)S(1)}, u32[]{:S(2)}, u32[]{:S(2)}) collective-permute-start(bf16[128,1024]{1,0:T(8,128)(2,1)S(1)} %first_level.10.rest_0_.state_ref), channel_id=1, source_target_pairs={{0,1},{1,0},{2,3},{3,2},{4,5},{5,4},{6,7},{7,6},{8,9},{9,8},{10,11... | collective-permute-start | bytes 786440 | tf_op jit(solution)/shard_map/ppermute | solution.py:351
  43.1 5.6 %collective-permute-start.14 = (bf16[128,1024]{1,0:T(8,128)(2,1)S(1)}, bf16[128,1024]{1,0:T(8,128)(2,1)S(1)}, u32[]{:S(2)}, u32[]{:S(2)}) collective-permute-start(bf16[128,1024]{1,0:T(8,128)(2,1)S(1)} %first_level.11.rest_0_.state_ref), channel_id=1, source_target_pairs={{0,1},{1,0},{2,3},{3,2},{4,5},{5,4},{6,7},{7,6},{8,9},{9,8},{10,11... | collective-permute-start | bytes 786440 | tf_op jit(solution)/shard_map/ppermute | solution.py:351
  43.5 10.7 %collective-permute-start.12 = (bf16[128,1024]{1,0:T(8,128)(2,1)S(1)}, bf16[128,1024]{1,0:T(8,128)(2,1)S(1)}, u32[]{:S(2)}, u32[]{:S(2)}) collective-permute-start(bf16[128,1024]{1,0:T(8,128)(2,1)S(1)} %level_1.8.rest_0_.state_ref), channel_id=1, source_target_pairs={{0,16},{8,24},{16,0},{24,8},{32,48},{40,56},{48,32},{56,40},{64,80... | collective-permute-start | bytes 786440 | tf_op jit(solution)/shard_map/ppermute | solution.py:351
  45.1 10.7 %collective-permute-start.20 = (bf16[128,1024]{1,0:T(8,128)(2,1)S(1)}, bf16[128,1024]{1,0:T(8,128)(2,1)S(1)}, u32[]{:S(2)}, u32[]{:S(2)}) collective-permute-start(bf16[128,1024]{1,0:T(8,128)(2,1)S(1)} %first_level.12.rest_0_.state_ref), channel_id=1, source_target_pairs={{0,1},{1,0},{2,3},{3,2},{4,5},{5,4},{6,7},{7,6},{8,9},{9,8},{10,11... | collective-permute-start | bytes 786440 | tf_op jit(solution)/shard_map/ppermute | solution.py:351
  45.2 13.9 %collective-permute-start.19 = (bf16[128,1024]{1,0:T(8,128)(2,1)S(1)}, bf16[128,1024]{1,0:T(8,128)(2,1)S(1)}, u32[]{:S(2)}, u32[]{:S(2)}) collective-permute-start(bf16[128,1024]{1,0:T(8,128)(2,1)S(1)} %level_1.9.rest_0_.state_ref), channel_id=1, source_target_pairs={{0,16},{8,24},{16,0},{24,8},{32,48},{40,56},{48,32},{56,40},{64,80... | collective-permute-start | bytes 786440 | tf_op jit(solution)/shard_map/ppermute | solution.py:351
  55.4 5.5 %collective-permute-start.18 = (bf16[128,1024]{1,0:T(8,128)(2,1)S(1)}, bf16[128,1024]{1,0:T(8,128)(2,1)S(1)}, u32[]{:S(2)}, u32[]{:S(2)}) collective-permute-start(bf16[128,1024]{1,0:T(8,128)(2,1)S(1)} %first_level.13.rest_0_.state_ref), channel_id=1, source_target_pairs={{0,1},{1,0},{2,3},{3,2},{4,5},{5,4},{6,7},{7,6},{8,9},{9,8},{10,11... | collective-permute-start | bytes 786440 | tf_op jit(solution)/shard_map/ppermute | solution.py:351
  55.5 10.7 %collective-permute-start.17 = (bf16[128,1024]{1,0:T(8,128)(2,1)S(1)}, bf16[128,1024]{1,0:T(8,128)(2,1)S(1)}, u32[]{:S(2)}, u32[]{:S(2)}) collective-permute-start(bf16[128,1024]{1,0:T(8,128)(2,1)S(1)} %level_1.10.rest_0_.state_ref), channel_id=1, source_target_pairs={{0,16},{8,24},{16,0},{24,8},{32,48},{40,56},{48,32},{56,40},{64,80... | collective-permute-start | bytes 786440 | tf_op jit(solution)/shard_map/ppermute | solution.py:351
  55.7 10.8 %collective-permute-start.16 = (bf16[128,1024]{1,0:T(8,128)(2,1)S(1)}, bf16[128,1024]{1,0:T(8,128)(2,1)S(1)}, u32[]{:S(2)}, u32[]{:S(2)}) collective-permute-start(bf16[128,1024]{1,0:T(8,128)(2,1)S(1)} %level_2.8.rest_0_.state_ref), channel_id=1, source_target_pairs={{0,2},{1,3},{2,0},{3,1},{4,6},{5,7},{6,4},{7,5},{8,10},{9,11},{10,... | collective-permute-start | bytes 786440 | tf_op jit(solution)/shard_map/ppermute | solution.py:351
  60.2 10.2 %collective-permute-start.24 = (bf16[128,1024]{1,0:T(8,128)(2,1)S(1)}, bf16[128,1024]{1,0:T(8,128)(2,1)S(1)}, u32[]{:S(2)}, u32[]{:S(2)}) collective-permute-start(bf16[128,1024]{1,0:T(8,128)(2,1)S(1)} %first_level.14.rest_0_.state_ref), channel_id=1, source_target_pairs={{0,1},{1,0},{2,3},{3,2},{4,5},{5,4},{6,7},{7,6},{8,9},{9,8},{10,11... | collective-permute-start | bytes 786440 | tf_op jit(solution)/shard_map/ppermute | solution.py:351
  60.3 11.0 %collective-permute-start.23 = (bf16[128,1024]{1,0:T(8,128)(2,1)S(1)}, bf16[128,1024]{1,0:T(8,128)(2,1)S(1)}, u32[]{:S(2)}, u32[]{:S(2)}) collective-permute-start(bf16[128,1024]{1,0:T(8,128)(2,1)S(1)} %level_1.11.rest_0_.state_ref), channel_id=1, source_target_pairs={{0,16},{8,24},{16,0},{24,8},{32,48},{40,56},{48,32},{56,40},{64,80... | collective-permute-start | bytes 786440 | tf_op jit(solution)/shard_map/ppermute | solution.py:351
  61.0 12.0 %collective-permute-start.22 = (bf16[128,1024]{1,0:T(8,128)(2,1)S(1)}, bf16[128,1024]{1,0:T(8,128)(2,1)S(1)}, u32[]{:S(2)}, u32[]{:S(2)}) collective-permute-start(bf16[128,1024]{1,0:T(8,128)(2,1)S(1)} %level_2.9.rest_0_.state_ref), channel_id=1, source_target_pairs={{0,2},{1,3},{2,0},{3,1},{4,6},{5,7},{6,4},{7,5},{8,10},{9,11},{10,... | collective-permute-start | bytes 786440 | tf_op jit(solution)/shard_map/ppermute | solution.py:351
  68.5 7.6 %collective-permute-start.21 = (bf16[128,1024]{1,0:T(8,128)(2,1)S(1)}, bf16[128,1024]{1,0:T(8,128)(2,1)S(1)}, u32[]{:S(2)}, u32[]{:S(2)}) collective-permute-start(bf16[128,1024]{1,0:T(8,128)(2,1)S(1)} %first_level.15.rest_0_.state_ref), channel_id=1, source_target_pairs={{0,1},{1,0},{2,3},{3,2},{4,5},{5,4},{6,7},{7,6},{8,9},{9,8},{10,11... | collective-permute-start | bytes 786440 | tf_op jit(solution)/shard_map/ppermute | solution.py:351
  68.6 10.7 %collective-permute-start.26 = (bf16[128,1024]{1,0:T(8,128)(2,1)S(1)}, bf16[128,1024]{1,0:T(8,128)(2,1)S(1)}, u32[]{:S(2)}, u32[]{:S(2)}) collective-permute-start(bf16[128,1024]{1,0:T(8,128)(2,1)S(1)} %level_1.12.rest_0_.state_ref), channel_id=1, source_target_pairs={{0,16},{8,24},{16,0},{24,8},{32,48},{40,56},{48,32},{56,40},{64,80... | collective-permute-start | bytes 786440 | tf_op jit(solution)/shard_map/ppermute | solution.py:351
  70.4 9.3 %collective-permute-start.29 = (bf16[128,1024]{1,0:T(8,128)(2,1)S(1)}, bf16[128,1024]{1,0:T(8,128)(2,1)S(1)}, u32[]{:S(2)}, u32[]{:S(2)}) collective-permute-start(bf16[128,1024]{1,0:T(8,128)(2,1)S(1)} %level_2.10.rest_0_.state_ref), channel_id=1, source_target_pairs={{0,2},{1,3},{2,0},{3,1},{4,6},{5,7},{6,4},{7,5},{8,10},{9,11},{10,... | collective-permute-start | bytes 786440 | tf_op jit(solution)/shard_map/ppermute | solution.py:351
  71.4 13.6 %collective-permute-start.30 = (bf16[128,1024]{1,0:T(8,128)(2,1)S(1)}, bf16[128,1024]{1,0:T(8,128)(2,1)S(1)}, u32[]{:S(2)}, u32[]{:S(2)}) collective-permute-start(bf16[128,1024]{1,0:T(8,128)(2,1)S(1)} %level_1.13.rest_0_.state_ref), channel_id=1, source_target_pairs={{0,16},{8,24},{16,0},{24,8},{32,48},{40,56},{48,32},{56,40},{64,80... | collective-permute-start | bytes 786440 | tf_op jit(solution)/shard_map/ppermute | solution.py:351
  73.0 12.4 %collective-permute-start.28 = (bf16[128,1024]{1,0:T(8,128)(2,1)S(1)}, bf16[128,1024]{1,0:T(8,128)(2,1)S(1)}, u32[]{:S(2)}, u32[]{:S(2)}) collective-permute-start(bf16[128,1024]{1,0:T(8,128)(2,1)S(1)} %level_2.11.rest_1_.state_ref), channel_id=1, source_target_pairs={{0,2},{1,3},{2,0},{3,1},{4,6},{5,7},{6,4},{7,5},{8,10},{9,11},{10,... | collective-permute-start | bytes 786440 | tf_op jit(solution)/shard_map/ppermute | solution.py:351
  76.2 14.4 %collective-permute-start.31 = (bf16[128,1024]{1,0:T(8,128)(2,1)S(1)}, bf16[128,1024]{1,0:T(8,128)(2,1)S(1)}, u32[]{:S(2)}, u32[]{:S(2)}) collective-permute-start(bf16[128,1024]{1,0:T(8,128)(2,1)S(1)} %level_1.14.rest_0_.state_ref), channel_id=1, source_target_pairs={{0,16},{8,24},{16,0},{24,8},{32,48},{40,56},{48,32},{56,40},{64,80... | collective-permute-start | bytes 786440 | tf_op jit(solution)/shard_map/ppermute | solution.py:351
  79.6 11.3 %collective-permute-start.27 = (bf16[128,1024]{1,0:T(8,128)(2,1)S(1)}, bf16[128,1024]{1,0:T(8,128)(2,1)S(1)}, u32[]{:S(2)}, u32[]{:S(2)}) collective-permute-start(bf16[128,1024]{1,0:T(8,128)(2,1)S(1)} %level_2.12.rest_1_.state_ref), channel_id=1, source_target_pairs={{0,2},{1,3},{2,0},{3,1},{4,6},{5,7},{6,4},{7,5},{8,10},{9,11},{10,... | collective-permute-start | bytes 786440 | tf_op jit(solution)/shard_map/ppermute | solution.py:351
  79.7 15.9 %collective-permute-start.25 = (bf16[128,1024]{1,0:T(8,128)(2,1)S(1)}, bf16[128,1024]{1,0:T(8,128)(2,1)S(1)}, u32[]{:S(2)}, u32[]{:S(2)}) collective-permute-start(bf16[128,1024]{1,0:T(8,128)(2,1)S(1)} %level_1.15.rest_0_.state_ref), channel_id=1, source_target_pairs={{0,16},{8,24},{16,0},{24,8},{32,48},{40,56},{48,32},{56,40},{64,80... | collective-permute-start | bytes 786440 | tf_op jit(solution)/shard_map/ppermute | solution.py:351
  85.3 11.1 %collective-permute-start.34 = (bf16[128,1024]{1,0:T(8,128)(2,1)S(1)}, bf16[128,1024]{1,0:T(8,128)(2,1)S(1)}, u32[]{:S(2)}, u32[]{:S(2)}) collective-permute-start(bf16[128,1024]{1,0:T(8,128)(2,1)S(1)} %level_2.13.rest_1_.state_ref), channel_id=1, source_target_pairs={{0,2},{1,3},{2,0},{3,1},{4,6},{5,7},{6,4},{7,5},{8,10},{9,11},{10,... | collective-permute-start | bytes 786440 | tf_op jit(solution)/shard_map/ppermute | solution.py:351
  90.9 11.1 %collective-permute-start.33 = (bf16[128,1024]{1,0:T(8,128)(2,1)S(1)}, bf16[128,1024]{1,0:T(8,128)(2,1)S(1)}, u32[]{:S(2)}, u32[]{:S(2)}) collective-permute-start(bf16[128,1024]{1,0:T(8,128)(2,1)S(1)} %level_2.14.rest_1_.state_ref), channel_id=1, source_target_pairs={{0,2},{1,3},{2,0},{3,1},{4,6},{5,7},{6,4},{7,5},{8,10},{9,11},{10,... | collective-permute-start | bytes 786440 | tf_op jit(solution)/shard_map/ppermute | solution.py:351
  96.0 10.8 %collective-permute-start.32 = (bf16[128,1024]{1,0:T(8,128)(2,1)S(1)}, bf16[128,1024]{1,0:T(8,128)(2,1)S(1)}, u32[]{:S(2)}, u32[]{:S(2)}) collective-permute-start(bf16[128,1024]{1,0:T(8,128)(2,1)S(1)} %level_2.15.rest_1_.state_ref), channel_id=1, source_target_pairs={{0,2},{1,3},{2,0},{3,1},{4,6},{5,7},{6,4},{7,5},{8,10},{9,11},{10,... | collective-permute-start | bytes 786440 | tf_op jit(solution)/shard_map/ppermute | solution.py:351

commit v3 on v2

--- a/solution.py
+++ b/solution.py
@@ -14,11 +14,12 @@
 ROWS = BOXES * DIRS
 LEVELS = 4
 PARTS = (2, 2, 2, 2, 2, 2, 2, 2)
-SENDS = (16,)
+GROUPS = (1, 1, 2, 2, 2)
+ORDER = "a0 a1 b0 a2 b1 b2 c0 a3 b3 c1 b4 c2 d0 a4 b5 c3 d1 b6 c4 d2 b7 c5 d3 c6 d4 c7 d5 d6 d7"
 SPAN = 1024
 FETCHES = 4
 ALONG = 4
-AHEAD = 4
+FLOPS = 10**10
 MIB = 1 << 20
 
 TURN = 32767.0 / 3.141592653589793
@@ -48,8 +49,8 @@
     return pltpu.CompilerParams(vmem_limit_bytes=mib * MIB)
 
 
-def kernel_call(*args, **kwargs):
-    cost = pl.CostEstimate(flops=1000, bytes_accessed=1000, transcendentals=0)
+def kernel_call(*args, flops=1000, **kwargs):
+    cost = pl.CostEstimate(flops=flops, bytes_accessed=1000, transcendentals=0)
     return pl.pallas_call(*args, cost_estimate=cost, **kwargs)
 
 
@@ -78,46 +79,47 @@
     return jnp.concatenate([top, low], axis=0).astype(jnp.bfloat16)
 
 
-def encode_kernel(phases_ref, *rest):
-    out_refs, (held, sems) = rest[: len(SENDS)], rest[len(SENDS) :]
+def encode_kernel(phases_ref, out_ref, held, sems):
+    span = ROWS // FETCHES
     copies = []
-    for i, n in enumerate(SENDS):
-        cols = pl.ds(sum(SENDS[:i]) * DIRS, n * DIRS)
+    for i in range(FETCHES):
+        cols = pl.ds(i * span, span)
         copies.append(pltpu.make_async_copy(phases_ref.at[0, :, cols], held.at[:, cols], sems.at[i]))
         copies[-1].start()
-    for i, n in enumerate(SENDS):
+    for i in range(FETCHES):
         copies[i].wait()
-        cols = pl.ds(sum(SENDS[:i]) * DIRS, n * DIRS)
-        out_refs[i][...] = jnp.round(held[:, cols] * TURN).astype(jnp.int32).astype(jnp.int16)
+        cols = pl.ds(i * span, span)
+        out_ref[:, cols] = jnp.round(held[:, cols] * TURN).astype(jnp.int32).astype(jnp.int16)
 
 
 def encode(phases):
     return kernel_call(
         encode_kernel,
         in_specs=[ANY],
-        out_specs=[VMEM] * len(SENDS),
-        out_shape=[pltpu.VMEM((HALF, n * DIRS), jnp.int16) for n in SENDS],
-        scratch_shapes=[pltpu.VMEM((HALF, ROWS), jnp.float32), pltpu.SemaphoreType.DMA((len(SENDS),))],
+        out_specs=VMEM,
+        out_shape=pltpu.VMEM((HALF, ROWS), jnp.int16),
+        scratch_shapes=[pltpu.VMEM((HALF, ROWS), jnp.float32), pltpu.SemaphoreType.DMA((FETCHES,))],
         compiler_params=limit(8),
         name="encode",
     )(far(phases))
 
 
-def fetch_kernel(after_ref, phases_ref, out_ref, sems):
-    copies = [pltpu.make_async_copy(phases_ref.at[k], out_ref.at[k], sems.at[k]) for k in range(LEVELS + 1)]
-    for copy in copies:
-        copy.start()
+def fetch_kernel(first, after_ref, phases_ref, out_ref, sems):
+    copies = []
+    for k in range(out_ref.shape[0]):
+        copies.append(pltpu.make_async_copy(phases_ref.at[first + k], out_ref.at[k], sems.at[k]))
+        copies[-1].start()
     for copy in copies:
         copy.wait()
 
 
-def fetch(after, phases):
-    return kernel_call(
-        fetch_kernel,
+def fetch(first, count, after, phases):
+    return kernel_call(
+        functools.partial(fetch_kernel, first),
         in_specs=[ANY, ANY],
         out_specs=VMEM,
-        out_shape=pltpu.VMEM(phases.shape, jnp.float32),
-        scratch_shapes=[pltpu.SemaphoreType.DMA((LEVELS + 1,))],
+        out_shape=pltpu.VMEM((count, HALF, ROWS), jnp.float32),
+        scratch_shapes=[pltpu.SemaphoreType.DMA((count,))],
         compiler_params=limit(2),
         name="fetch",
     )(near(after), far(phases))
@@ -211,7 +213,7 @@
     )(near(after), *map(near, parts))
 
 
-def expand_kernel(map_ref, *refs):
+def expand_kernel(after_ref, map_ref, *refs):
     parts, (mine_ref, other_ref) = refs[:-2], refs[-2:]
     place = place_of("x")
     for there, out_ref in ((place, mine_ref), (jnp.bitwise_xor(place, 1), other_ref)):
@@ -219,15 +221,15 @@
         out_ref[...] = jnp.dot(total, map_ref[...], preferred_element_type=jnp.float32)
 
 
-def expand(source_map, parts):
+def expand(after, source_map, parts):
     return kernel_call(
         expand_kernel,
-        in_specs=[VMEM] * (1 + len(parts)),
+        in_specs=[ANY] + [VMEM] * (1 + len(parts)),
         out_specs=[VMEM] * 2,
         out_shape=[pltpu.VMEM((BOXES, WIDTH), jnp.float32)] * 2,
         compiler_params=limit(4),
         name="expand",
-    )(near(source_map), *map(near, parts))
+    )(near(after), near(source_map), *map(near, parts))
 
 
 def mats_kernel(after_ref, trans_ref, *out_refs):
@@ -254,7 +256,7 @@
     return row.T[:, :1]
 
 
-def first_kernel(start, boxes, skip, x_ref, other_x_ref, mats_ref, phases_ref, other_ref, *rest):
+def first_kernel(start, boxes, x_ref, other_x_ref, mats_ref, phases_ref, other_ref, *rest):
     out_ref = rest[-1]
     per = min(boxes, SPAN // DIRS)
     for b in range(0, boxes, per):
@@ -264,8 +266,7 @@
             mine = column(x_ref, box)
             state = turn(mine[:HALF], mine[HALF:], *cos_sin(phases_ref[0, :, cols]))
             theirs = column(other_x_ref, box)
-            there = pl.ds((box - skip) * DIRS, DIRS)
-            angle = other_ref[:, there].astype(jnp.int32).astype(jnp.float32) * (1.0 / TURN)
+            angle = other_ref[:, cols].astype(jnp.int32).astype(jnp.float32) * (1.0 / TURN)
             partner = turn(theirs[:HALF], theirs[HALF:], *cos_sin(angle))
             both.append(jnp.concatenate([state, partner], axis=0))
         mixed = jnp.dot(mats_ref[...], jnp.concatenate(both, axis=1), preferred_element_type=jnp.float32)
@@ -274,24 +275,23 @@
 
 
 def first_level(start, boxes, x, other_x, mats, phases, others, after):
-    piece = 0
-    while start >= sum(SENDS[: piece + 1]):
-        piece += 1
-    return kernel_call(
-        functools.partial(first_kernel, start, boxes, sum(SENDS[:piece])),
+    return kernel_call(
+        functools.partial(first_kernel, start, boxes),
         in_specs=[VMEM] * 5 + [ANY] * len(after),
         out_specs=VMEM,
         out_shape=pltpu.VMEM((WIDTH, boxes * DIRS), jnp.bfloat16),
         compiler_params=limit(8),
-        name="first_level",
-    )(near(x), near(other_x), near(mats), near(phases), near(others[piece]), *map(near, after))
-
-
-def mix(start, level, cols, state_ref, partner_ref, mats_ref, phases_ref):
-    both = jnp.concatenate([state_ref[:, cols], partner_ref[:, cols]], axis=0)
+        flops=FLOPS,
+        name="a_%d" % start,
+    )(near(x), near(other_x), near(mats), near(phases), near(others), *map(near, after))
+
+
+def mix(start, skip, slot, cols, state_ref, partner_ref, mats_ref, phases_ref):
+    here = pl.ds((start - skip) * DIRS + cols.start, cols.size)
+    there = pl.ds(start * DIRS + cols.start, cols.size)
+    both = jnp.concatenate([state_ref[:, here], partner_ref[:, here]], axis=0)
     mixed = jnp.dot(mats_ref[...], both, preferred_element_type=jnp.float32)
-    there = pl.ds(start * DIRS + cols.start, cols.size)
-    return turn(mixed[:HALF], mixed[HALF:], *cos_sin(phases_ref[level + 1, :, there]))
+    return turn(mixed[:HALF], mixed[HALF:], *cos_sin(phases_ref[slot, :, there]))
 
 
 def spans(boxes):
@@ -299,29 +299,53 @@
     return [pl.ds(b, size) for b in range(0, boxes * DIRS, size)]
 
 
-def level_kernel(start, boxes, level, state_ref, partner_ref, mats_ref, phases_ref, *rest):
+def level_kernel(start, boxes, skip, slot, state_ref, partner_ref, mats_ref, phases_ref, *rest):
     out_ref = rest[-1]
     for cols in spans(boxes):
-        out_ref[:, cols] = mix(start, level, cols, state_ref, partner_ref, mats_ref, phases_ref)
-
-
-def next_level(start, boxes, level, state, partner, mats, phases, after):
-    return kernel_call(
-        functools.partial(level_kernel, start, boxes, level),
+        out_ref[:, cols] = mix(start, skip, slot, cols, state_ref, partner_ref, mats_ref, phases_ref)
+
+
+def next_level(name, start, boxes, skip, slot, state, partner, mats, phases, after):
+    return kernel_call(
+        functools.partial(level_kernel, start, boxes, skip, slot),
         in_specs=[VMEM] * 4 + [ANY] * len(after),
         out_specs=VMEM,
         out_shape=pltpu.VMEM((WIDTH, boxes * DIRS), jnp.bfloat16),
         compiler_params=limit(8),
-        name="level_%d" % level,
+        flops=FLOPS,
+        name="%s_%d" % (name, start),
     )(near(state), near(partner), near(mats), near(phases), *map(near, after))
 
 
-def last_kernel(start, boxes, state_ref, partner_ref, mats_ref, phases_ref, *rest):
-    out_ref, token_ref, held, sems = rest[-4:]
-    token_ref[...] = jnp.zeros_like(token_ref)
+def flush_kernel(*refs):
+    parts, out_ref, sems = refs[:-2], refs[-2], refs[-1]
+    copies, at = [], 0
+    for i, part in enumerate(parts):
+        size = part.shape[1]
+        copies.append(pltpu.make_async_copy(part, out_ref.at[:, pl.ds(at, size)], sems.at[i]))
+        copies[-1].start()
+        at += size
+    for copy in copies:
+        copy.wait()
+
+
+def flush(parts):
+    return kernel_call(
+        flush_kernel,
+        in_specs=[VMEM] * len(parts),
+        out_specs=ANY,
+        out_shape=jax.ShapeDtypeStruct((WIDTH, ROWS), jnp.bfloat16),
+        scratch_shapes=[pltpu.SemaphoreType.DMA((len(parts),))],
+        compiler_params=limit(2),
+        flops=FLOPS,
+        name="flush",
+    )(*map(near, parts))
+
+
+def last_kernel(start, boxes, slot, state_ref, partner_ref, mats_ref, phases_ref, before_ref, out_ref, held, sems):
     copies = []
     for i, cols in enumerate(spans(boxes)):
-        held[:, cols] = mix(start, LEVELS - 1, cols, state_ref, partner_ref, mats_ref, phases_ref)
+        held[:, cols] = mix(start, start, slot, cols, state_ref, partner_ref, mats_ref, phases_ref)
         there = pl.ds(start * DIRS + cols.start, cols.size)
         copies.append(pltpu.make_async_copy(held.at[:, cols], out_ref.at[:, there], sems.at[i]))
         copies[-1].start()
@@ -329,22 +353,21 @@
         copy.wait()
 
 
-def last_level(start, boxes, state, partner, mats, phases, before, after):
-    kept = [] if before is None else [far(before)]
-
-    return kernel_call(
-        functools.partial(last_kernel, start, boxes),
-        in_specs=[VMEM] * 4 + [ANY] * (len(kept) + len(after)),
-        out_specs=[ANY, VMEM],
-        out_shape=[jax.ShapeDtypeStruct((WIDTH, ROWS), jnp.bfloat16), pltpu.VMEM((8, WIDTH), jnp.float32)],
-        input_output_aliases={4: 0} if kept else {},
+def last_level(start, boxes, slot, state, partner, mats, phases, before):
+    return kernel_call(
+        functools.partial(last_kernel, start, boxes, slot),
+        in_specs=[VMEM] * 4 + [ANY],
+        out_specs=ANY,
+        out_shape=jax.ShapeDtypeStruct((WIDTH, ROWS), jnp.bfloat16),
+        input_output_aliases={4: 0},
         scratch_shapes=[
             pltpu.VMEM((WIDTH, boxes * DIRS), jnp.bfloat16),
             pltpu.SemaphoreType.DMA((len(spans(boxes)),)),
         ],
         compiler_params=limit(8),
-        name="last_level",
-    )(near(state), near(partner), near(mats), near(phases), *kept, *map(near, after))
+        flops=FLOPS,
+        name="last",
+    )(near(state), near(partner), near(mats), near(phases), far(before))
 
 
 def move(value, axis, mask):
@@ -353,46 +376,47 @@
 
 def per_device(currents, counts, box_of, source_map, phases, trans):
     turns = encode(phases)
-    others = [move(t, "bx", 1) for t in turns]
-    keep, send = box_sums(counts, turns[0], box_of[0], currents[0])
+    others = move(turns, "bx", 1)
+    keep, send = box_sums(counts, turns, box_of[0], currents[0])
     got = move(send, "by", 1)
     own, *sent = spread("z", True, keep, [keep, got], jnp.bfloat16)
-    angles = fetch(own, phases)
+    early = fetch(0, 2, own, phases)
     got = [move(v, "by", 2 * k + 2) for k, v in enumerate(sent)]
-    own, *sent = spread("y", False, angles, [own] + got, jnp.float32)
+    own, *sent = spread("y", False, early, [own] + got, jnp.float32)
     mats = pick_mats(own, trans)
     row = add(mats[0], [own] + [move(v, "bx", 4 * k + 4) for k, v in enumerate(sent)])
-    mine, theirs = expand(source_map, [row] + [move(row, "bx", k) for k in (1, 2, 3)])
+    late = fetch(2, 3, row, phases)
+    mine, theirs = expand(late, source_map, [row] + [move(row, "bx", k) for k in (1, 2, 3)])
 
     starts = [sum(PARTS[:i]) for i in range(len(PARTS))]
-    count = len(PARTS)
-    states = [{}, {}, {}, {}]
-    latest = []
-
-    def step(level, i):
-        if not 0 <= i < count:
-            return
-        where = (starts[i], PARTS[i])
-        after = latest[-1:]
-        if level == 0:
-            done = first_level(*where, mine, theirs, mats[0], angles, others, after)
+    groups = [range(sum(GROUPS[:g]), sum(GROUPS[: g + 1])) for g in range(len(GROUPS))]
+    final = len(PARTS) - 1
+    firsts, states, partners, out = {}, {}, {}, None
+    after = []
+    for name in ORDER.split():
+        level, i = name[0], int(name[1:])
+        if level == "a":
+            start, boxes = starts[groups[i][0]], sum(PARTS[p] for p in groups[i])
+            done = first_level(start, boxes, mine, theirs, mats[0], early, others, after)
+            swapped = move(done, "by", 1)
+            for p in groups[i]:
+                firsts[p] = (start, done, swapped)
+        elif level == "b":
+            skip, value, other = firsts[i]
+            done = next_level(level, starts[i], PARTS[i], skip, 0, value, other, mats[1], late, after)
+            states[i], partners[i] = done, move(done, "bx", 2)
+        elif level == "c":
+            ends = (starts[i], PARTS[i], starts[i], 1)
+            done = next_level(level, *ends, states[i], partners[i], mats[2], late, after)
+            states[i], partners[i] = done, move(done, "by", 2)
+        elif i < final:
+            ends = (starts[i], PARTS[i], starts[i], 2)
+            done = next_level(level, *ends, states[i], partners[i], mats[3], late, after)
+            states[i] = done
         else:
-            value = states[level - 1][i]
-            other = move(value, *(("by", 1), ("bx", 2), ("by", 2))[level - 1])
-            if level < 3:
-                done = next_level(*where, level, value, other, mats[level], angles, after)
-            else:
-                states[3][i], done = last_level(*where, value, other, mats[level], angles, states[3].get(i - 1), after)
-        if level < 3:
-            states[level][i] = done
-        latest.append(done)
-
-    for i in range(-AHEAD, count + 2):
-        step(0, i + AHEAD)
-        step(1, i + AHEAD - 1)
-        step(2, i)
-        step(3, i - 2)
-    return states[3][count - 1]
+            out = flush([states[p] for p in range(final)])
+            return last_level(starts[i], PARTS[i], 2, states[i], partners[i], mats[3], late, out)
+        after = [done]
 
 
 def solution(mesh):

time: 109 us -> 99.7 us (0.915)
  Pallas kernels: 30.6 us -> 26.9 us
  waiting for transfers between devices: 43.1 us -> 40.4 us
  starting transfers between devices: 34.2 us -> 31.6 us
    pallas_call x35 -> x34, Pallas kernels: 27.3 us -> 23.6 us  [the longest x23 7.66 us: next_level(): kernel_call(functools.partial(level_kernel, start, boxes, skip, slot), in...]
    ppermute x35 -> x32, waiting for transfers between devices: 43.1 us -> 40.4 us  [move(): lax.ppermute(value, axis, [(s, s ^ mask) for s in range(lax.axis_size(axi...]
    ppermute x35 -> x32, starting transfers between devices: 34.2 us -> 31.6 us  [move(): lax.ppermute(value, axis, [(s, s ^ mask) for s in range(lax.axis_size(axi...]
  transfers between devices with their start and end apart: 35 -> 32, of which waited for: 18 -> 17; matrix products, arithmetic and copies ran while one was open for 0% -> 0% of each run, Pallas kernels for 24% -> 23%
where the time goes in v3:
time: 99.7 us; the launch traced here: 99.6 us
  waiting for transfers between devices  40.4 us (41%)
  starting transfers between devices  31.6 us (32%)
  Pallas kernels  26.9 us (27%)
    ppermute x32, waiting for transfers between devices, move(): lax.ppermute(value, axis, [(s, s ^ mask) for s in range(lax.axis_size(axi...  40.4 us
    ppermute x32, starting transfers between devices, move(): lax.ppermute(value, axis, [(s, s ^ mask) for s in range(lax.axis_size(axi...  31.6 us
    pallas_call x23, Pallas kernels, next_level(): kernel_call(functools.partial(level_kernel, start, boxes, skip, slot), in...  7.66 us
    pallas_call x5, Pallas kernels, first_level(): kernel_call(functools.partial(first_kernel, start, boxes), in_specs=[VMEM...  6.74 us
    pallas_call x2, Pallas kernels, fetch(): kernel_call(functools.partial(fetch_kernel, first), in_specs=[ANY, ANY],...  5.12 us
    pallas_call x1, Pallas kernels, box_sums(): kernel_call(box_sums_kernel, in_specs=[SMEM, ANY, ANY, ANY], out_specs=[V...  3.07 us
  transfers between devices with their start and end apart: 32, of which 17 were waited for; matrix products, arithmetic and copies ran while one was open for 0% of the time, Pallas kernels for 23%

profile of v3, /device:TPU:0, one launch (start us, length us, event | category | flops | bytes accessed | tf_op | source)
XLA Modules:
  0.0 99.6 jit_solution(1429404811177561250)
XLA Ops:
  0.0 1.6 %encode.1.after_ref = s16[64,8192]{1,0:T(8,128)(2,1)S(1)} custom-call(f32[5,64,8192]{2,1,0:T(8,128)} %phases_ref.5), custom_call_target="tpu_custom_call" | custom-call | flops 1000 | bytes 1000 | tf_op jit(solution)/shard_map/encode/pallas_call | solution.py:96
  1.6 1.7 %collective-permute-start.10 = (s16[64,8192]{1,0:T(8,128)(2,1)S(1)}, s16[64,8192]{1,0:T(8,128)(2,1)S(1)}, u32[]{:S(2)}, u32[]{:S(2)}) collective-permute-start(s16[64,8192]{1,0:T(8,128)(2,1)S(1)} %encode.1.after_ref), channel_id=1, source_target_pairs={{0,8},{8,0},{16,24},{24,16},{32,40},{40,32},{48,56},{56,48},{64,72... | collective-permute-start | bytes 3145736 | tf_op jit(solution)/shard_map/ppermute | solution.py:374
  3.3 3.1 %box_sums.1 = (bf16[64,16,128]{2,1,0:T(8,128)(2,1)S(1)}, bf16[64,16,128]{2,1,0:T(8,128)(2,1)S(1)}) custom-call(s32[1,128]{1,0:T(1,128)S(1)} %copy-done.2, s16[64,8192]{1,0:T(8,128)(2,1)S(1)} %encode.1.after_ref, s32[128,128]{1,0:T(8,128)} %bitcast.3, bf16[128,128,128]{2,1,0:T(8,128)(2,1)} %bitcast.2), custom_call_target="tpu_custom_call" | custom-call | flops 1000 | bytes 1000 | tf_op jit(solution)/shard_map/box_sums/pallas_call | solution.py:159
  6.4 1.5 %collective-permute-done.refs_1_ = bf16[64,16,128]{2,1,0:T(8,128)(2,1)S(1)} collective-permute-done((bf16[64,16,128]{2,1,0:T(8,128)(2,1)S(1)}, bf16[64,16,128]{2,1,0:T(8,128)(2,1)S(1)}, u32[]{:S(2)}, u32[]{:S(2)}) %collective-permute-start) | collective-permute-done | bytes 262176 | tf_op jit(solution)/shard_map/ppermute | solution.py:374
  8.0 2.0 %collective-permute-start.1 = (bf16[16,16,128]{2,1,0:T(8,128)(2,1)S(1)}, bf16[16,16,128]{2,1,0:T(8,128)(2,1)S(1)}, u32[]{:S(2)}, u32[]{:S(2)}) collective-permute-start(bf16[16,16,128]{2,1,0:T(8,128)(2,1)S(1)} %get-tuple-element.24), channel_id=1, source_target_pairs={{0,2},{1,3},{2,0},{3,1},{4,6},{5,7},{6,4},{7,5},{8,10},{9,11},{10,... | collective-permute-start | bytes 196616 | tf_op jit(solution)/shard_map/ppermute | solution.py:374
  10.0 3.6 %collective-permute-start.2 = (bf16[16,16,128]{2,1,0:T(8,128)(2,1)S(1)}, bf16[16,16,128]{2,1,0:T(8,128)(2,1)S(1)}, u32[]{:S(2)}, u32[]{:S(2)}) collective-permute-start(bf16[16,16,128]{2,1,0:T(8,128)(2,1)S(1)} %get-tuple-element.25), channel_id=1, source_target_pairs={{0,4},{1,5},{2,6},{3,7},{4,0},{5,1},{6,2},{7,3},{8,12},{9,13},{10,... | collective-permute-start | bytes 196616 | tf_op jit(solution)/shard_map/ppermute | solution.py:374
  13.6 2.2 %fetch.2.after_ref.phases_ref = f32[2,64,8192]{2,1,0:T(8,128)S(1)} custom-call(f32[16,16,128]{2,1,0:T(8,128)S(1)} %get-tuple-element.23.after_ref.refs_0_, f32[5,64,8192]{2,1,0:T(8,128)} %phases_ref.5), custom_call_target="tpu_custom_call" | custom-call | flops 1000 | bytes 1000 | tf_op jit(solution)/shard_map/fetch/pallas_call | solution.py:117
  15.9 1.3 %collective-permute-done.2.refs_2_ = bf16[16,16,128]{2,1,0:T(8,128)(2,1)S(1)} collective-permute-done((bf16[16,16,128]{2,1,0:T(8,128)(2,1)S(1)}, bf16[16,16,128]{2,1,0:T(8,128)(2,1)S(1)}, u32[]{:S(2)}, u32[]{:S(2)}) %collective-permute-start.2) | collective-permute-done | bytes 65568 | tf_op jit(solution)/shard_map/ppermute | solution.py:374
  17.1 2.0 %collective-permute-done.3.refs_3_ = bf16[16,16,128]{2,1,0:T(8,128)(2,1)S(1)} collective-permute-done((bf16[16,16,128]{2,1,0:T(8,128)(2,1)S(1)}, bf16[16,16,128]{2,1,0:T(8,128)(2,1)S(1)}, u32[]{:S(2)}, u32[]{:S(2)}) %collective-permute-start.3) | collective-permute-done | bytes 65568 | tf_op jit(solution)/shard_map/ppermute | solution.py:374
  19.1 1.7 %collective-permute-start.4 = (f32[4,16,128]{2,1,0:T(8,128)S(1)}, f32[4,16,128]{2,1,0:T(8,128)S(1)}, u32[]{:S(2)}, u32[]{:S(2)}) collective-permute-start(f32[4,16,128]{2,1,0:T(8,128)S(1)} %get-tuple-element.29), channel_id=1, source_target_pairs={{0,32},{8,40},{16,48},{24,56},{32,0},{40,8},{48,16},{56,24},{64,96... | collective-permute-start | bytes 98312 | tf_op jit(solution)/shard_map/ppermute | solution.py:374
  20.8 2.9 %collective-permute-start.5 = (f32[4,16,128]{2,1,0:T(8,128)S(1)}, f32[4,16,128]{2,1,0:T(8,128)S(1)}, u32[]{:S(2)}, u32[]{:S(2)}) collective-permute-start(f32[4,16,128]{2,1,0:T(8,128)S(1)} %get-tuple-element.30), channel_id=1, source_target_pairs={{0,64},{8,72},{16,80},{24,88},{32,96},{40,104},{48,112},{56,120},{... | collective-permute-start | bytes 98312 | tf_op jit(solution)/shard_map/ppermute | solution.py:374
  24.1 2.2 %collective-permute-done.5.refs_2_ = f32[4,16,128]{2,1,0:T(8,128)S(1)} collective-permute-done((f32[4,16,128]{2,1,0:T(8,128)S(1)}, f32[4,16,128]{2,1,0:T(8,128)S(1)}, u32[]{:S(2)}, u32[]{:S(2)}) %collective-permute-start.5) | collective-permute-done | bytes 32800 | tf_op jit(solution)/shard_map/ppermute | solution.py:374
  26.2 2.6 %collective-permute-done.6.refs_3_ = f32[4,16,128]{2,1,0:T(8,128)S(1)} collective-permute-done((f32[4,16,128]{2,1,0:T(8,128)S(1)}, f32[4,16,128]{2,1,0:T(8,128)S(1)}, u32[]{:S(2)}, u32[]{:S(2)}) %collective-permute-start.6) | collective-permute-done | bytes 32800 | tf_op jit(solution)/shard_map/ppermute | solution.py:374
  28.8 0.6 collective-permute-start.7
  29.5 3.0 %collective-permute-start.8 = (f32[4,16,128]{2,1,0:T(8,128)S(1)}, f32[4,16,128]{2,1,0:T(8,128)S(1)}, u32[]{:S(2)}, u32[]{:S(2)}) collective-permute-start(f32[4,16,128]{2,1,0:T(8,128)S(1)} %add.1.after_ref.refs_0_), channel_id=1, source_target_pairs={{0,16},{8,24},{16,0},{24,8},{32,48},{40,56},{48,32},{56,40},{64,80... | collective-permute-start | bytes 98312 | tf_op jit(solution)/shard_map/ppermute | solution.py:374
  32.5 1.1 %collective-permute-start.9 = (f32[4,16,128]{2,1,0:T(8,128)S(1)}, f32[4,16,128]{2,1,0:T(8,128)S(1)}, u32[]{:S(2)}, u32[]{:S(2)}) collective-permute-start(f32[4,16,128]{2,1,0:T(8,128)S(1)} %add.1.after_ref.refs_0_), channel_id=1, source_target_pairs={{0,24},{8,16},{16,8},{24,0},{32,56},{40,48},{48,40},{56,32},{64,88... | collective-permute-start | bytes 98312 | tf_op jit(solution)/shard_map/ppermute | solution.py:374
  33.6 2.9 %fetch.3.after_ref.phases_ref = f32[3,64,8192]{2,1,0:T(8,128)S(1)} custom-call(f32[4,16,128]{2,1,0:T(8,128)S(1)} %add.1.after_ref.refs_0_, f32[5,64,8192]{2,1,0:T(8,128)} %phases_ref.5), custom_call_target="tpu_custom_call" | custom-call | flops 1000 | bytes 1000 | tf_op jit(solution)/shard_map/fetch/pallas_call | solution.py:117
  36.5 1.1 %collective-permute-done.9.refs_3_ = f32[4,16,128]{2,1,0:T(8,128)S(1)} collective-permute-done((f32[4,16,128]{2,1,0:T(8,128)S(1)}, f32[4,16,128]{2,1,0:T(8,128)S(1)}, u32[]{:S(2)}, u32[]{:S(2)}) %collective-permute-start.9) | collective-permute-done | bytes 32800 | tf_op jit(solution)/shard_map/ppermute | solution.py:374
  37.7 0.9 a_0.1.rest_0_.state_ref
  38.7 0.9 a_2.1.rest_0_.state_ref
  39.6 0.6 collective-permute-start.14
  40.6 0.5 collective-permute-start.12
  41.1 1.7 %a_4.1.rest_0_.state_ref = bf16[128,2048]{1,0:T(8,128)(2,1)S(1)} custom-call(f32[16,128]{1,0:T(8,128)S(1)} %get-tuple-element.32.x_ref, f32[16,128]{1,0:T(8,128)S(1)} %get-tuple-element.33.other_x_ref, bf16[128,256]{1,0:T(8,128)(2,1)S(1)} %get-tuple-element.28.after_ref.mats_ref, f32[2,64,8192]{2,1,0:T(8,128)S(1)} %fetch.2.after_ref.phases_ref, ...), custom_call_target="tpu_custom_call" | custom-call | flops 10000000000 | bytes 1000 | tf_op jit(solution)/shard_map/a_4/pallas_call | solution.py:278
  42.9 0.3 b_2.1.rest_0_.state_ref
  43.3 3.1 %collective-permute-start.18 = (bf16[128,1024]{1,0:T(8,128)(2,1)S(1)}, bf16[128,1024]{1,0:T(8,128)(2,1)S(1)}, u32[]{:S(2)}, u32[]{:S(2)}) collective-permute-start(bf16[128,1024]{1,0:T(8,128)(2,1)S(1)} %b_2.1.rest_0_.state_ref), channel_id=1, source_target_pairs={{0,16},{8,24},{16,0},{24,8},{32,48},{40,56},{48,32},{56,40},{64,80... | collective-permute-start | bytes 786440 | tf_op jit(solution)/shard_map/ppermute | solution.py:374
  46.7 1.5 %collective-permute-start.16 = (bf16[128,1024]{1,0:T(8,128)(2,1)S(1)}, bf16[128,1024]{1,0:T(8,128)(2,1)S(1)}, u32[]{:S(2)}, u32[]{:S(2)}) collective-permute-start(bf16[128,1024]{1,0:T(8,128)(2,1)S(1)} %b_4.1.rest_0_.state_ref), channel_id=1, source_target_pairs={{0,16},{8,24},{16,0},{24,8},{32,48},{40,56},{48,32},{56,40},{64,80... | collective-permute-start | bytes 786440 | tf_op jit(solution)/shard_map/ppermute | solution.py:374
  48.3 3.0 %collective-permute-done.12.partner_ref = bf16[128,1024]{1,0:T(8,128)(2,1)S(1)} collective-permute-done((bf16[128,1024]{1,0:T(8,128)(2,1)S(1)}, bf16[128,1024]{1,0:T(8,128)(2,1)S(1)}, u32[]{:S(2)}, u32[]{:S(2)}) %collective-permute-start.12) | collective-permute-done | bytes 262176 | tf_op jit(solution)/shard_map/ppermute | solution.py:374
  51.9 1.7 %a_8.1.rest_0_.state_ref = bf16[128,2048]{1,0:T(8,128)(2,1)S(1)} custom-call(f32[16,128]{1,0:T(8,128)S(1)} %get-tuple-element.32.x_ref, f32[16,128]{1,0:T(8,128)S(1)} %get-tuple-element.33.other_x_ref, bf16[128,256]{1,0:T(8,128)(2,1)S(1)} %get-tuple-element.28.after_ref.mats_ref, f32[2,64,8192]{2,1,0:T(8,128)S(1)} %fetch.2.after_ref.phases_ref, ...), custom_call_target="tpu_custom_call" | custom-call | flops 10000000000 | bytes 1000 | tf_op jit(solution)/shard_map/a_8/pallas_call | solution.py:278
  54.1 2.8 %collective-permute-done.18.partner_ref = bf16[128,1024]{1,0:T(8,128)(2,1)S(1)} collective-permute-done((bf16[128,1024]{1,0:T(8,128)(2,1)S(1)}, bf16[128,1024]{1,0:T(8,128)(2,1)S(1)}, u32[]{:S(2)}, u32[]{:S(2)}) %collective-permute-start.18) | collective-permute-done | bytes 262176 | tf_op jit(solution)/shard_map/ppermute | solution.py:374
  57.4 0.3 b_8.1.rest_0_.state_ref
  57.7 2.8 %collective-permute-start.21 = (bf16[128,1024]{1,0:T(8,128)(2,1)S(1)}, bf16[128,1024]{1,0:T(8,128)(2,1)S(1)}, u32[]{:S(2)}, u32[]{:S(2)}) collective-permute-start(bf16[128,1024]{1,0:T(8,128)(2,1)S(1)} %b_8.1.rest_0_.state_ref), channel_id=1, source_target_pairs={{0,16},{8,24},{16,0},{24,8},{32,48},{40,56},{48,32},{56,40},{64,80... | collective-permute-start | bytes 786440 | tf_op jit(solution)/shard_map/ppermute | solution.py:374
  60.5 2.0 %collective-permute-done.16.partner_ref = bf16[128,1024]{1,0:T(8,128)(2,1)S(1)} collective-permute-done((bf16[128,1024]{1,0:T(8,128)(2,1)S(1)}, bf16[128,1024]{1,0:T(8,128)(2,1)S(1)}, u32[]{:S(2)}, u32[]{:S(2)}) %collective-permute-start.16) | collective-permute-done | bytes 262176 | tf_op jit(solution)/shard_map/ppermute | solution.py:374
  63.3 1.7 %a_12.1.rest_0_.state_ref = bf16[128,2048]{1,0:T(8,128)(2,1)S(1)} custom-call(f32[16,128]{1,0:T(8,128)S(1)} %get-tuple-element.32.x_ref, f32[16,128]{1,0:T(8,128)S(1)} %get-tuple-element.33.other_x_ref, bf16[128,256]{1,0:T(8,128)(2,1)S(1)} %get-tuple-element.28.after_ref.mats_ref, f32[2,64,8192]{2,1,0:T(8,128)S(1)} %fetch.2.after_ref.phases_ref, ...), custom_call_target="tpu_custom_call" | custom-call | flops 10000000000 | bytes 1000 | tf_op jit(solution)/shard_map/a_12/pallas_call | solution.py:278
  65.5 2.7 %collective-permute-done.23.partner_ref = bf16[128,1024]{1,0:T(8,128)(2,1)S(1)} collective-permute-done((bf16[128,1024]{1,0:T(8,128)(2,1)S(1)}, bf16[128,1024]{1,0:T(8,128)(2,1)S(1)}, u32[]{:S(2)}, u32[]{:S(2)}) %collective-permute-start.23) | collective-permute-done | bytes 262176 | tf_op jit(solution)/shard_map/ppermute | solution.py:374
  68.7 0.3 d_2.1.rest_0_.refs_1_
  69.0 0.3 b_12.1.rest_0_.state_ref
  69.4 3.6 %collective-permute-start.26 = (bf16[128,1024]{1,0:T(8,128)(2,1)S(1)}, bf16[128,1024]{1,0:T(8,128)(2,1)S(1)}, u32[]{:S(2)}, u32[]{:S(2)}) collective-permute-start(bf16[128,1024]{1,0:T(8,128)(2,1)S(1)} %b_12.1.rest_0_.state_ref), channel_id=1, source_target_pairs={{0,16},{8,24},{16,0},{24,8},{32,48},{40,56},{48,32},{56,40},{64,80... | collective-permute-start | bytes 786440 | tf_op jit(solution)/shard_map/ppermute | solution.py:374
  72.9 0.9 collective-permute-done.21.partner_ref
  74.1 1.2 %collective-permute-start.25 = (bf16[128,1024]{1,0:T(8,128)(2,1)S(1)}, bf16[128,1024]{1,0:T(8,128)(2,1)S(1)}, u32[]{:S(2)}, u32[]{:S(2)}) collective-permute-start(bf16[128,1024]{1,0:T(8,128)(2,1)S(1)} %c_8.1.rest_0_.state_ref), channel_id=1, source_target_pairs={{0,2},{1,3},{2,0},{3,1},{4,6},{5,7},{6,4},{7,5},{8,10},{9,11},{10,... | collective-permute-start | bytes 786440 | tf_op jit(solution)/shard_map/ppermute | solution.py:374
  76.2 3.2 %collective-permute-done.28.partner_ref = bf16[128,1024]{1,0:T(8,128)(2,1)S(1)} collective-permute-done((bf16[128,1024]{1,0:T(8,128)(2,1)S(1)}, bf16[128,1024]{1,0:T(8,128)(2,1)S(1)}, u32[]{:S(2)}, u32[]{:S(2)}) %collective-permute-start.28) | collective-permute-done | bytes 262176 | tf_op jit(solution)/shard_map/ppermute | solution.py:374
  80.2 4.8 %collective-permute-done.26.partner_ref = bf16[128,1024]{1,0:T(8,128)(2,1)S(1)} collective-permute-done((bf16[128,1024]{1,0:T(8,128)(2,1)S(1)}, bf16[128,1024]{1,0:T(8,128)(2,1)S(1)}, u32[]{:S(2)}, u32[]{:S(2)}) %collective-permute-start.26) | collective-permute-done | bytes 262176 | tf_op jit(solution)/shard_map/ppermute | solution.py:374
  85.5 0.3 d_8.1.rest_0_.refs_4_
  85.8 4.0 %collective-permute-done.24.partner_ref = bf16[128,1024]{1,0:T(8,128)(2,1)S(1)} collective-permute-done((bf16[128,1024]{1,0:T(8,128)(2,1)S(1)}, bf16[128,1024]{1,0:T(8,128)(2,1)S(1)}, u32[]{:S(2)}, u32[]{:S(2)}) %collective-permute-start.24) | collective-permute-done | bytes 262176 | tf_op jit(solution)/shard_map/ppermute | solution.py:374
  90.3 0.3 d_10.1.rest_0_.refs_5_
  90.6 2.7 %collective-permute-done.31.partner_ref = bf16[128,1024]{1,0:T(8,128)(2,1)S(1)} collective-permute-done((bf16[128,1024]{1,0:T(8,128)(2,1)S(1)}, bf16[128,1024]{1,0:T(8,128)(2,1)S(1)}, u32[]{:S(2)}, u32[]{:S(2)}) %collective-permute-start.31) | collective-permute-done | bytes 262176 | tf_op jit(solution)/shard_map/ppermute | solution.py:374
  93.6 1.3 %flush.1.before_ref = bf16[128,8192]{1,0:T(8,128)(2,1)} custom-call(bf16[128,1024]{1,0:T(8,128)(2,1)S(1)} %d_0.1.rest_0_.refs_0_, bf16[128,1024]{1,0:T(8,128)(2,1)S(1)} %d_2.1.rest_0_.refs_1_, bf16[128,1024]{1,0:T(8,128)(2,1)S(1)} %d_4.1.rest_0_.refs_2_, bf16[128,1024]{1,0:T(8,128)(2,1)S(1)} %d_6.1.rest_0_.refs_3_, ...), custom_call_target="tpu_custom_call" | custom-call | flops 10000000000 | bytes 1000 | tf_op jit(solution)/shard_map/flush/pallas_call | solution.py:333
  94.9 3.4 %collective-permute-done.29.partner_ref = bf16[128,1024]{1,0:T(8,128)(2,1)S(1)} collective-permute-done((bf16[128,1024]{1,0:T(8,128)(2,1)S(1)}, bf16[128,1024]{1,0:T(8,128)(2,1)S(1)}, u32[]{:S(2)}, u32[]{:S(2)}) %collective-permute-start.29) | collective-permute-done | bytes 262176 | tf_op jit(solution)/shard_map/ppermute | solution.py:374
  98.4 1.0 %last.1 = bf16[128,8192]{1,0:T(8,128)(2,1)} custom-call(bf16[128,1024]{1,0:T(8,128)(2,1)S(1)} %c_14.1.rest_0_.state_ref, bf16[128,1024]{1,0:T(8,128)(2,1)S(1)} %collective-permute-done.29.partner_ref, bf16[128,256]{1,0:T(8,128)(2,1)S(1)} %get-tuple-element.36.mats_ref, f32[3,64,8192]{2,1,0:T(8,128)S(1)} %fetch.3.after_ref.phases_ref, ...), custom_call_target="tpu_custom_call", output_to_operand_aliasing={{}: (4, {})} | custom-call | flops 10000000000 | bytes 1000 | tf_op jit(solution)/shard_map/last/pallas_call | solution.py:357
  (61 shorter events, 7.8 us)
Async XLA Ops:
  0.0 3.3 %copy-start.2 = (s32[1,128]{1,0:T(1,128)S(1)}, s32[1,128]{1,0:T(1,128)}, u32[]{:S(2)}) copy-start(s32[1,128]{1,0:T(1,128)} %counts_ref.1) | copy-start | bytes 1540
  1.6 36.1 %collective-permute-start.10 = (s16[64,8192]{1,0:T(8,128)(2,1)S(1)}, s16[64,8192]{1,0:T(8,128)(2,1)S(1)}, u32[]{:S(2)}, u32[]{:S(2)}) collective-permute-start(s16[64,8192]{1,0:T(8,128)(2,1)S(1)} %encode.1.after_ref), channel_id=1, source_target_pairs={{0,8},{8,0},{16,24},{24,16},{32,40},{40,32},{48,56},{56,48},{64,72... | collective-permute-start | bytes 3145736 | tf_op jit(solution)/shard_map/ppermute | solution.py:374
  6.4 1.6 %collective-permute-start = (bf16[64,16,128]{2,1,0:T(8,128)(2,1)S(1)}, bf16[64,16,128]{2,1,0:T(8,128)(2,1)S(1)}, u32[]{:S(2)}, u32[]{:S(2)}) collective-permute-start(bf16[64,16,128]{2,1,0:T(8,128)(2,1)S(1)} %get-tuple-element.22), channel_id=1, source_target_pairs={{0,1},{1,0},{2,3},{3,2},{4,5},{5,4},{6,7},{7,6},{8,9},{9,8},{10,11... | collective-permute-start | bytes 786440 | tf_op jit(solution)/shard_map/ppermute | solution.py:374
  8.0 7.8 %collective-permute-start.1 = (bf16[16,16,128]{2,1,0:T(8,128)(2,1)S(1)}, bf16[16,16,128]{2,1,0:T(8,128)(2,1)S(1)}, u32[]{:S(2)}, u32[]{:S(2)}) collective-permute-start(bf16[16,16,128]{2,1,0:T(8,128)(2,1)S(1)} %get-tuple-element.24), channel_id=1, source_target_pairs={{0,2},{1,3},{2,0},{3,1},{4,6},{5,7},{6,4},{7,5},{8,10},{9,11},{10,... | collective-permute-start | bytes 196616 | tf_op jit(solution)/shard_map/ppermute | solution.py:374
  10.0 7.1 %collective-permute-start.2 = (bf16[16,16,128]{2,1,0:T(8,128)(2,1)S(1)}, bf16[16,16,128]{2,1,0:T(8,128)(2,1)S(1)}, u32[]{:S(2)}, u32[]{:S(2)}) collective-permute-start(bf16[16,16,128]{2,1,0:T(8,128)(2,1)S(1)} %get-tuple-element.25), channel_id=1, source_target_pairs={{0,4},{1,5},{2,6},{3,7},{4,0},{5,1},{6,2},{7,3},{8,12},{9,13},{10,... | collective-permute-start | bytes 196616 | tf_op jit(solution)/shard_map/ppermute | solution.py:374
  13.6 5.5 %collective-permute-start.3 = (bf16[16,16,128]{2,1,0:T(8,128)(2,1)S(1)}, bf16[16,16,128]{2,1,0:T(8,128)(2,1)S(1)}, u32[]{:S(2)}, u32[]{:S(2)}) collective-permute-start(bf16[16,16,128]{2,1,0:T(8,128)(2,1)S(1)} %get-tuple-element.26), channel_id=1, source_target_pairs={{0,6},{1,7},{2,4},{3,5},{4,2},{5,3},{6,0},{7,1},{8,14},{9,15},{10,... | collective-permute-start | bytes 196616 | tf_op jit(solution)/shard_map/ppermute | solution.py:374
  15.9 8.0 %copy-start = (bf16[4,2,2,128,128]{4,3,2,1,0:T(8,128)(2,1)S(1)}, bf16[4,2,2,128,128]{4,3,2,1,0:T(8,128)(2,1)}, u32[]{:S(2)}) copy-start(bf16[4,2,2,128,128]{4,3,2,1,0:T(8,128)(2,1)} %trans_ref.1) | copy-start | bytes 1572868
  19.1 4.9 %collective-permute-start.4 = (f32[4,16,128]{2,1,0:T(8,128)S(1)}, f32[4,16,128]{2,1,0:T(8,128)S(1)}, u32[]{:S(2)}, u32[]{:S(2)}) collective-permute-start(f32[4,16,128]{2,1,0:T(8,128)S(1)} %get-tuple-element.29), channel_id=1, source_target_pairs={{0,32},{8,40},{16,48},{24,56},{32,0},{40,8},{48,16},{56,24},{64,96... | collective-permute-start | bytes 98312 | tf_op jit(solution)/shard_map/ppermute | solution.py:374
  20.8 5.4 %collective-permute-start.5 = (f32[4,16,128]{2,1,0:T(8,128)S(1)}, f32[4,16,128]{2,1,0:T(8,128)S(1)}, u32[]{:S(2)}, u32[]{:S(2)}) collective-permute-start(f32[4,16,128]{2,1,0:T(8,128)S(1)} %get-tuple-element.30), channel_id=1, source_target_pairs={{0,64},{8,72},{16,80},{24,88},{32,96},{40,104},{48,112},{56,120},{... | collective-permute-start | bytes 98312 | tf_op jit(solution)/shard_map/ppermute | solution.py:374
  23.7 5.1 %collective-permute-start.6 = (f32[4,16,128]{2,1,0:T(8,128)S(1)}, f32[4,16,128]{2,1,0:T(8,128)S(1)}, u32[]{:S(2)}, u32[]{:S(2)}) collective-permute-start(f32[4,16,128]{2,1,0:T(8,128)S(1)} %get-tuple-element.31), channel_id=1, source_target_pairs={{0,96},{8,104},{16,112},{24,120},{32,64},{40,72},{48,80},{56,88},{... | collective-permute-start | bytes 98312 | tf_op jit(solution)/shard_map/ppermute | solution.py:374
  28.8 8.8 %copy-start.1 = (bf16[128,128]{1,0:T(8,128)(2,1)S(1)}, bf16[128,128]{1,0:T(8,128)(2,1)}, u32[]{:S(2)}) copy-start(bf16[128,128]{1,0:T(8,128)(2,1)} %map_ref.1) | copy-start | bytes 98308
  28.8 7.7 %collective-permute-start.7 = (f32[4,16,128]{2,1,0:T(8,128)S(1)}, f32[4,16,128]{2,1,0:T(8,128)S(1)}, u32[]{:S(2)}, u32[]{:S(2)}) collective-permute-start(f32[4,16,128]{2,1,0:T(8,128)S(1)} %add.1.after_ref.refs_0_), channel_id=1, source_target_pairs={{0,8},{8,0},{16,24},{24,16},{32,40},{40,32},{48,56},{56,48},{64,72... | collective-permute-start | bytes 98312 | tf_op jit(solution)/shard_map/ppermute | solution.py:374
  29.5 7.1 %collective-permute-start.8 = (f32[4,16,128]{2,1,0:T(8,128)S(1)}, f32[4,16,128]{2,1,0:T(8,128)S(1)}, u32[]{:S(2)}, u32[]{:S(2)}) collective-permute-start(f32[4,16,128]{2,1,0:T(8,128)S(1)} %add.1.after_ref.refs_0_), channel_id=1, source_target_pairs={{0,16},{8,24},{16,0},{24,8},{32,48},{40,56},{48,32},{56,40},{64,80... | collective-permute-start | bytes 98312 | tf_op jit(solution)/shard_map/ppermute | solution.py:374
  32.5 5.1 %collective-permute-start.9 = (f32[4,16,128]{2,1,0:T(8,128)S(1)}, f32[4,16,128]{2,1,0:T(8,128)S(1)}, u32[]{:S(2)}, u32[]{:S(2)}) collective-permute-start(f32[4,16,128]{2,1,0:T(8,128)S(1)} %add.1.after_ref.refs_0_), channel_id=1, source_target_pairs={{0,24},{8,16},{16,8},{24,0},{32,56},{40,48},{48,40},{56,32},{64,88... | collective-permute-start | bytes 98312 | tf_op jit(solution)/shard_map/ppermute | solution.py:374
  38.6 1.6 %collective-permute-start.11 = (bf16[128,1024]{1,0:T(8,128)(2,1)S(1)}, bf16[128,1024]{1,0:T(8,128)(2,1)S(1)}, u32[]{:S(2)}, u32[]{:S(2)}) collective-permute-start(bf16[128,1024]{1,0:T(8,128)(2,1)S(1)} %a_0.1.rest_0_.state_ref), channel_id=1, source_target_pairs={{0,1},{1,0},{2,3},{3,2},{4,5},{5,4},{6,7},{7,6},{8,9},{9,8},{10,11... | collective-permute-start | bytes 786440 | tf_op jit(solution)/shard_map/ppermute | solution.py:374
  39.6 3.3 %collective-permute-start.14 = (bf16[128,1024]{1,0:T(8,128)(2,1)S(1)}, bf16[128,1024]{1,0:T(8,128)(2,1)S(1)}, u32[]{:S(2)}, u32[]{:S(2)}) collective-permute-start(bf16[128,1024]{1,0:T(8,128)(2,1)S(1)} %a_2.1.rest_0_.state_ref), channel_id=1, source_target_pairs={{0,1},{1,0},{2,3},{3,2},{4,5},{5,4},{6,7},{7,6},{8,9},{9,8},{10,11... | collective-permute-start | bytes 786440 | tf_op jit(solution)/shard_map/ppermute | solution.py:374
  40.6 10.7 %collective-permute-start.12 = (bf16[128,1024]{1,0:T(8,128)(2,1)S(1)}, bf16[128,1024]{1,0:T(8,128)(2,1)S(1)}, u32[]{:S(2)}, u32[]{:S(2)}) collective-permute-start(bf16[128,1024]{1,0:T(8,128)(2,1)S(1)} %b_0.1.rest_0_.state_ref), channel_id=1, source_target_pairs={{0,16},{8,24},{16,0},{24,8},{32,48},{40,56},{48,32},{56,40},{64,80... | collective-permute-start | bytes 786440 | tf_op jit(solution)/shard_map/ppermute | solution.py:374
  42.8 3.6 %collective-permute-start.13 = (bf16[128,2048]{1,0:T(8,128)(2,1)S(1)}, bf16[128,2048]{1,0:T(8,128)(2,1)S(1)}, u32[]{:S(2)}, u32[]{:S(2)}) collective-permute-start(bf16[128,2048]{1,0:T(8,128)(2,1)S(1)} %a_4.1.rest_0_.state_ref), channel_id=1, source_target_pairs={{0,1},{1,0},{2,3},{3,2},{4,5},{5,4},{6,7},{7,6},{8,9},{9,8},{10,11... | collective-permute-start | bytes 1572872 | tf_op jit(solution)/shard_map/ppermute | solution.py:374
  43.3 13.7 %collective-permute-start.18 = (bf16[128,1024]{1,0:T(8,128)(2,1)S(1)}, bf16[128,1024]{1,0:T(8,128)(2,1)S(1)}, u32[]{:S(2)}, u32[]{:S(2)}) collective-permute-start(bf16[128,1024]{1,0:T(8,128)(2,1)S(1)} %b_2.1.rest_0_.state_ref), channel_id=1, source_target_pairs={{0,16},{8,24},{16,0},{24,8},{32,48},{40,56},{48,32},{56,40},{64,80... | collective-permute-start | bytes 786440 | tf_op jit(solution)/shard_map/ppermute | solution.py:374
  46.7 15.8 %collective-permute-start.16 = (bf16[128,1024]{1,0:T(8,128)(2,1)S(1)}, bf16[128,1024]{1,0:T(8,128)(2,1)S(1)}, u32[]{:S(2)}, u32[]{:S(2)}) collective-permute-start(bf16[128,1024]{1,0:T(8,128)(2,1)S(1)} %b_4.1.rest_0_.state_ref), channel_id=1, source_target_pairs={{0,16},{8,24},{16,0},{24,8},{32,48},{40,56},{48,32},{56,40},{64,80... | collective-permute-start | bytes 786440 | tf_op jit(solution)/shard_map/ppermute | solution.py:374
  51.7 11.3 %collective-permute-start.15 = (bf16[128,1024]{1,0:T(8,128)(2,1)S(1)}, bf16[128,1024]{1,0:T(8,128)(2,1)S(1)}, u32[]{:S(2)}, u32[]{:S(2)}) collective-permute-start(bf16[128,1024]{1,0:T(8,128)(2,1)S(1)} %c_0.1.rest_0_.state_ref), channel_id=1, source_target_pairs={{0,2},{1,3},{2,0},{3,1},{4,6},{5,7},{6,4},{7,5},{8,10},{9,11},{10,... | collective-permute-start | bytes 786440 | tf_op jit(solution)/shard_map/ppermute | solution.py:374
  53.6 3.8 %collective-permute-start.17 = (bf16[128,2048]{1,0:T(8,128)(2,1)S(1)}, bf16[128,2048]{1,0:T(8,128)(2,1)S(1)}, u32[]{:S(2)}, u32[]{:S(2)}) collective-permute-start(bf16[128,2048]{1,0:T(8,128)(2,1)S(1)} %a_8.1.rest_0_.state_ref), channel_id=1, source_target_pairs={{0,1},{1,0},{2,3},{3,2},{4,5},{5,4},{6,7},{7,6},{8,9},{9,8},{10,11... | collective-permute-start | bytes 1572872 | tf_op jit(solution)/shard_map/ppermute | solution.py:374
  54.0 14.1 %collective-permute-start.23 = (bf16[128,1024]{1,0:T(8,128)(2,1)S(1)}, bf16[128,1024]{1,0:T(8,128)(2,1)S(1)}, u32[]{:S(2)}, u32[]{:S(2)}) collective-permute-start(bf16[128,1024]{1,0:T(8,128)(2,1)S(1)} %b_6.1.rest_0_.state_ref), channel_id=1, source_target_pairs={{0,16},{8,24},{16,0},{24,8},{32,48},{40,56},{48,32},{56,40},{64,80... | collective-permute-start | bytes 786440 | tf_op jit(solution)/shard_map/ppermute | solution.py:374
  57.3 11.3 %collective-permute-start.22 = (bf16[128,1024]{1,0:T(8,128)(2,1)S(1)}, bf16[128,1024]{1,0:T(8,128)(2,1)S(1)}, u32[]{:S(2)}, u32[]{:S(2)}) collective-permute-start(bf16[128,1024]{1,0:T(8,128)(2,1)S(1)} %c_2.1.rest_0_.state_ref), channel_id=1, source_target_pairs={{0,2},{1,3},{2,0},{3,1},{4,6},{5,7},{6,4},{7,5},{8,10},{9,11},{10,... | collective-permute-start | bytes 786440 | tf_op jit(solution)/shard_map/ppermute | solution.py:374
  57.7 16.1 %collective-permute-start.21 = (bf16[128,1024]{1,0:T(8,128)(2,1)S(1)}, bf16[128,1024]{1,0:T(8,128)(2,1)S(1)}, u32[]{:S(2)}, u32[]{:S(2)}) collective-permute-start(bf16[128,1024]{1,0:T(8,128)(2,1)S(1)} %b_8.1.rest_0_.state_ref), channel_id=1, source_target_pairs={{0,16},{8,24},{16,0},{24,8},{32,48},{40,56},{48,32},{56,40},{64,80... | collective-permute-start | bytes 786440 | tf_op jit(solution)/shard_map/ppermute | solution.py:374
  62.9 12.5 %collective-permute-start.20 = (bf16[128,1024]{1,0:T(8,128)(2,1)S(1)}, bf16[128,1024]{1,0:T(8,128)(2,1)S(1)}, u32[]{:S(2)}, u32[]{:S(2)}) collective-permute-start(bf16[128,1024]{1,0:T(8,128)(2,1)S(1)} %c_4.1.rest_0_.state_ref), channel_id=1, source_target_pairs={{0,2},{1,3},{2,0},{3,1},{4,6},{5,7},{6,4},{7,5},{8,10},{9,11},{10,... | collective-permute-start | bytes 786440 | tf_op jit(solution)/shard_map/ppermute | solution.py:374
  65.0 4.0 %collective-permute-start.19 = (bf16[128,2048]{1,0:T(8,128)(2,1)S(1)}, bf16[128,2048]{1,0:T(8,128)(2,1)S(1)}, u32[]{:S(2)}, u32[]{:S(2)}) collective-permute-start(bf16[128,2048]{1,0:T(8,128)(2,1)S(1)} %a_12.1.rest_0_.state_ref), channel_id=1, source_target_pairs={{0,1},{1,0},{2,3},{3,2},{4,5},{5,4},{6,7},{7,6},{8,9},{9,8},{10,11... | collective-permute-start | bytes 1572872 | tf_op jit(solution)/shard_map/ppermute | solution.py:374
  68.2 11.2 %collective-permute-start.28 = (bf16[128,1024]{1,0:T(8,128)(2,1)S(1)}, bf16[128,1024]{1,0:T(8,128)(2,1)S(1)}, u32[]{:S(2)}, u32[]{:S(2)}) collective-permute-start(bf16[128,1024]{1,0:T(8,128)(2,1)S(1)} %b_10.1.rest_0_.state_ref), channel_id=1, source_target_pairs={{0,16},{8,24},{16,0},{24,8},{32,48},{40,56},{48,32},{56,40},{64,80... | collective-permute-start | bytes 786440 | tf_op jit(solution)/shard_map/ppermute | solution.py:374
  68.6 11.3 %collective-permute-start.27 = (bf16[128,1024]{1,0:T(8,128)(2,1)S(1)}, bf16[128,1024]{1,0:T(8,128)(2,1)S(1)}, u32[]{:S(2)}, u32[]{:S(2)}) collective-permute-start(bf16[128,1024]{1,0:T(8,128)(2,1)S(1)} %c_6.1.rest_0_.state_ref), channel_id=1, source_target_pairs={{0,2},{1,3},{2,0},{3,1},{4,6},{5,7},{6,4},{7,5},{8,10},{9,11},{10,... | collective-permute-start | bytes 786440 | tf_op jit(solution)/shard_map/ppermute | solution.py:374
  69.4 15.7 %collective-permute-start.26 = (bf16[128,1024]{1,0:T(8,128)(2,1)S(1)}, bf16[128,1024]{1,0:T(8,128)(2,1)S(1)}, u32[]{:S(2)}, u32[]{:S(2)}) collective-permute-start(bf16[128,1024]{1,0:T(8,128)(2,1)S(1)} %b_12.1.rest_0_.state_ref), channel_id=1, source_target_pairs={{0,16},{8,24},{16,0},{24,8},{32,48},{40,56},{48,32},{56,40},{64,80... | collective-permute-start | bytes 786440 | tf_op jit(solution)/shard_map/ppermute | solution.py:374
  74.1 11.3 %collective-permute-start.25 = (bf16[128,1024]{1,0:T(8,128)(2,1)S(1)}, bf16[128,1024]{1,0:T(8,128)(2,1)S(1)}, u32[]{:S(2)}, u32[]{:S(2)}) collective-permute-start(bf16[128,1024]{1,0:T(8,128)(2,1)S(1)} %c_8.1.rest_0_.state_ref), channel_id=1, source_target_pairs={{0,2},{1,3},{2,0},{3,1},{4,6},{5,7},{6,4},{7,5},{8,10},{9,11},{10,... | collective-permute-start | bytes 786440 | tf_op jit(solution)/shard_map/ppermute | solution.py:374
  76.0 13.8 %collective-permute-start.24 = (bf16[128,1024]{1,0:T(8,128)(2,1)S(1)}, bf16[128,1024]{1,0:T(8,128)(2,1)S(1)}, u32[]{:S(2)}, u32[]{:S(2)}) collective-permute-start(bf16[128,1024]{1,0:T(8,128)(2,1)S(1)} %b_14.1.rest_0_.state_ref), channel_id=1, source_target_pairs={{0,16},{8,24},{16,0},{24,8},{32,48},{40,56},{48,32},{56,40},{64,80... | collective-permute-start | bytes 786440 | tf_op jit(solution)/shard_map/ppermute | solution.py:374
  79.8 10.5 %collective-permute-start.30 = (bf16[128,1024]{1,0:T(8,128)(2,1)S(1)}, bf16[128,1024]{1,0:T(8,128)(2,1)S(1)}, u32[]{:S(2)}, u32[]{:S(2)}) collective-permute-start(bf16[128,1024]{1,0:T(8,128)(2,1)S(1)} %c_10.1.rest_0_.state_ref), channel_id=1, source_target_pairs={{0,2},{1,3},{2,0},{3,1},{4,6},{5,7},{6,4},{7,5},{8,10},{9,11},{10,... | collective-permute-start | bytes 786440 | tf_op jit(solution)/shard_map/ppermute | solution.py:374
  85.4 7.9 %collective-permute-start.31 = (bf16[128,1024]{1,0:T(8,128)(2,1)S(1)}, bf16[128,1024]{1,0:T(8,128)(2,1)S(1)}, u32[]{:S(2)}, u32[]{:S(2)}) collective-permute-start(bf16[128,1024]{1,0:T(8,128)(2,1)S(1)} %c_12.1.rest_0_.state_ref), channel_id=1, source_target_pairs={{0,2},{1,3},{2,0},{3,1},{4,6},{5,7},{6,4},{7,5},{8,10},{9,11},{10,... | collective-permute-start | bytes 786440 | tf_op jit(solution)/shard_map/ppermute | solution.py:374
  90.2 8.2 %collective-permute-start.29 = (bf16[128,1024]{1,0:T(8,128)(2,1)S(1)}, bf16[128,1024]{1,0:T(8,128)(2,1)S(1)}, u32[]{:S(2)}, u32[]{:S(2)}) collective-permute-start(bf16[128,1024]{1,0:T(8,128)(2,1)S(1)} %c_14.1.rest_0_.state_ref), channel_id=1, source_target_pairs={{0,2},{1,3},{2,0},{3,1},{4,6},{5,7},{6,4},{7,5},{8,10},{9,11},{10,... | collective-permute-start | bytes 786440 | tf_op jit(solution)/shard_map/ppermute | solution.py:374

commit v4 on v3

--- a/solution.py
+++ b/solution.py
@@ -15,7 +15,7 @@
 LEVELS = 4
 PARTS = (2, 2, 2, 2, 2, 2, 2, 2)
 GROUPS = (1, 1, 2, 2, 2)
-ORDER = "a0 a1 b0 a2 b1 b2 c0 a3 b3 c1 b4 c2 d0 a4 b5 c3 d1 b6 c4 d2 b7 c5 d3 c6 d4 c7 d5 d6 d7"
+ORDER = "a0 a1 b0 a2 b1 b2 f c0 a3 b3 c1 b4 c2 d0 a4 b5 c3 d1 b6 c4 d2 b7 c5 d3 c6 d4 c7 d5 d6 d7"
 SPAN = 1024
 FETCHES = 4
 ALONG = 4
@@ -171,46 +171,39 @@
     )(counts, near(after), far(tag), far(rows))
 
 
-def spread_kernel(part, inner, after_ref, *refs):
-    parts, outs = refs[:-ALONG], refs[-ALONG:]
-    place = place_of(part)
-    for k, out_ref in enumerate(outs):
-        there = jnp.bitwise_xor(place, k)
-        if inner:
-            for i in range(out_ref.shape[0]):
-                total = sum(p[i * ALONG + there].astype(jnp.float32) for p in parts)
-                out_ref[i] = total.astype(out_ref.dtype)
-        else:
-            some = pl.ds(there * out_ref.shape[0], out_ref.shape[0])
-            out_ref[...] = sum(p[some].astype(jnp.float32) for p in parts).astype(out_ref.dtype)
-
-
-def spread(part, inner, after, parts, sent):
-    owners = parts[0].shape[0] // ALONG
-    kinds = [jnp.float32] + [sent] * (ALONG - 1)
-    return kernel_call(
-        functools.partial(spread_kernel, part, inner),
-        in_specs=[ANY] + [VMEM] * len(parts),
-        out_specs=[VMEM] * ALONG,
-        out_shape=[pltpu.VMEM((owners, BOXES, WIDTH), kind) for kind in kinds],
+def deal_kernel(keep_ref, got_ref, out_ref):
+    for y in range(ALONG):
+        for x in range(ALONG):
+            for z in range(ALONG):
+                i = (y * ALONG + x) * ALONG + z
+                total = keep_ref[i].astype(jnp.float32) + got_ref[i].astype(jnp.float32)
+                out_ref[y * ALONG + z, x] = total.astype(jnp.bfloat16)
+
+
+def deal(keep, got):
+    return kernel_call(
+        deal_kernel,
+        in_specs=[VMEM] * 2,
+        out_specs=VMEM,
+        out_shape=pltpu.VMEM((ALONG * ALONG, ALONG, BOXES, WIDTH), jnp.bfloat16),
         compiler_params=limit(4),
-        name="by_" + part,
-    )(near(after), *map(near, parts))
-
-
-def add_kernel(after_ref, *refs):
-    refs[-1][...] = sum(r[...] for r in refs[:-1])
-
-
-def add(after, parts):
+        name="deal",
+    )(near(keep), near(got))
+
+
+def add_kernel(parts_ref, out_ref):
+    out_ref[...] = sum(parts_ref[i].astype(jnp.float32) for i in range(parts_ref.shape[0]))
+
+
+def add(parts):
     return kernel_call(
         add_kernel,
-        in_specs=[ANY] + [VMEM] * len(parts),
-        out_specs=VMEM,
-        out_shape=pltpu.VMEM(parts[0].shape, jnp.float32),
+        in_specs=[VMEM],
+        out_specs=VMEM,
+        out_shape=pltpu.VMEM(parts.shape[1:], jnp.float32),
         compiler_params=limit(4),
         name="add",
-    )(near(after), *map(near, parts))
+    )(near(parts))
 
 
 def expand_kernel(after_ref, map_ref, *refs):
@@ -379,14 +372,18 @@
     others = move(turns, "bx", 1)
     keep, send = box_sums(counts, turns, box_of[0], currents[0])
     got = move(send, "by", 1)
-    own, *sent = spread("z", True, keep, [keep, got], jnp.bfloat16)
-    early = fetch(0, 2, own, phases)
-    got = [move(v, "by", 2 * k + 2) for k, v in enumerate(sent)]
-    own, *sent = spread("y", False, early, [own] + got, jnp.float32)
-    mats = pick_mats(own, trans)
-    row = add(mats[0], [own] + [move(v, "bx", 4 * k + 4) for k, v in enumerate(sent)])
-    late = fetch(2, 3, row, phases)
-    mine, theirs = expand(late, source_map, [row] + [move(row, "bx", k) for k in (1, 2, 3)])
+    plane = [
+        [(y * ALONG + x) * 2 * ALONG + z * 2 + core for y in range(ALONG) for z in range(ALONG)]
+        for x in range(ALONG)
+        for core in range(2)
+    ]
+    parts = lax.all_to_all(
+        deal(keep, got), ("bx", "by"), split_axis=0, concat_axis=0, tiled=True, axis_index_groups=plane
+    )
+    row = add(parts)
+    early = fetch(0, 3, row, phases)
+    mats = pick_mats(row, trans)
+    mine, theirs = expand(early, source_map, [row] + [move(row, "bx", k) for k in (1, 2, 3)])
 
     starts = [sum(PARTS[:i]) for i in range(len(PARTS))]
     groups = [range(sum(GROUPS[:g]), sum(GROUPS[: g + 1])) for g in range(len(GROUPS))]
@@ -394,6 +391,9 @@
     firsts, states, partners, out = {}, {}, {}, None
     after = []
     for name in ORDER.split():
+        if name == "f":
+            after = [late := fetch(3, 2, after[0], phases)]
+            continue
         level, i = name[0], int(name[1:])
         if level == "a":
             start, boxes = starts[groups[i][0]], sum(PARTS[p] for p in groups[i])
@@ -403,19 +403,19 @@
                 firsts[p] = (start, done, swapped)
         elif level == "b":
             skip, value, other = firsts[i]
-            done = next_level(level, starts[i], PARTS[i], skip, 0, value, other, mats[1], late, after)
+            done = next_level(level, starts[i], PARTS[i], skip, 2, value, other, mats[1], early, after)
             states[i], partners[i] = done, move(done, "bx", 2)
         elif level == "c":
-            ends = (starts[i], PARTS[i], starts[i], 1)
+            ends = (starts[i], PARTS[i], starts[i], 0)
             done = next_level(level, *ends, states[i], partners[i], mats[2], late, after)
             states[i], partners[i] = done, move(done, "by", 2)
         elif i < final:
-            ends = (starts[i], PARTS[i], starts[i], 2)
+            ends = (starts[i], PARTS[i], starts[i], 1)
             done = next_level(level, *ends, states[i], partners[i], mats[3], late, after)
             states[i] = done
         else:
             out = flush([states[p] for p in range(final)])
-            return last_level(starts[i], PARTS[i], 2, states[i], partners[i], mats[3], late, out)
+            return last_level(starts[i], PARTS[i], 1, states[i], partners[i], mats[3], late, out)
         after = [done]
 
 

time: 99.7 us -> 97.2 us (0.975)
  blocking collectives: 0 us -> 16.7 us
  waiting for transfers between devices: 40.4 us -> 25.5 us
  starting transfers between devices: 31.6 us -> 27.4 us
    all_to_all x0 -> x1, blocking collectives: none -> 16.7 us  [per_device(): lax.all_to_all(deal(keep, got), ('bx', 'by'), split_axis=0, concat_axis=0...]
    ppermute x32 -> x26, waiting for transfers between devices: 40.4 us -> 25.5 us  [move(): lax.ppermute(value, axis, [(s, s ^ mask) for s in range(lax.axis_size(axi...]
    ppermute x32 -> x26, starting transfers between devices: 31.6 us -> 27.4 us  [move(): lax.ppermute(value, axis, [(s, s ^ mask) for s in range(lax.axis_size(axi...]
  transfers between devices with their start and end apart: 32 -> 26, of which waited for: 17 -> 14; matrix products, arithmetic and copies ran while one was open for 0% -> 0% of each run, Pallas kernels for 23% -> 24%
where the time goes in v4:
time: 97.2 us; the launch traced here: 97 us
  starting transfers between devices  27.4 us (28%)
  Pallas kernels  26.9 us (28%)
  waiting for transfers between devices  25.5 us (26%)
  blocking collectives  16.7 us (17%)
    ppermute x26, starting transfers between devices, move(): lax.ppermute(value, axis, [(s, s ^ mask) for s in range(lax.axis_size(axi...  27.4 us
    ppermute x26, waiting for transfers between devices, move(): lax.ppermute(value, axis, [(s, s ^ mask) for s in range(lax.axis_size(axi...  25.5 us
    all_to_all x1, blocking collectives, per_device(): lax.all_to_all(deal(keep, got), ('bx', 'by'), split_axis=0, concat_axis=0...  16.7 us
    pallas_call x23, Pallas kernels, next_level(): kernel_call(functools.partial(level_kernel, start, boxes, skip, slot), in...  7.65 us
    pallas_call x5, Pallas kernels, first_level(): kernel_call(functools.partial(first_kernel, start, boxes), in_specs=[VMEM...  6.74 us
    pallas_call x2, Pallas kernels, fetch(): kernel_call(functools.partial(fetch_kernel, first), in_specs=[ANY, ANY],...  5.12 us
    pallas_call x1, Pallas kernels, box_sums(): kernel_call(box_sums_kernel, in_specs=[SMEM, ANY, ANY, ANY], out_specs=[V...  3.07 us
  transfers between devices with their start and end apart: 26, of which 14 were waited for; matrix products, arithmetic and copies ran while one was open for 0% of the time, Pallas kernels for 24%

profile of v4, /device:TPU:0, one launch (start us, length us, event | category | flops | bytes accessed | tf_op | source)
XLA Modules:
  0.0 97.0 jit_solution(2903333387618468213)
XLA Ops:
  0.0 1.6 %encode.1.after_ref = s16[64,8192]{1,0:T(8,128)(2,1)S(1)} custom-call(f32[5,64,8192]{2,1,0:T(8,128)} %phases_ref.5), custom_call_target="tpu_custom_call" | custom-call | flops 1000 | bytes 1000 | tf_op jit(solution)/shard_map/encode/pallas_call | solution.py:96
  1.6 1.7 %collective-permute-start.4 = (s16[64,8192]{1,0:T(8,128)(2,1)S(1)}, s16[64,8192]{1,0:T(8,128)(2,1)S(1)}, u32[]{:S(2)}, u32[]{:S(2)}) collective-permute-start(s16[64,8192]{1,0:T(8,128)(2,1)S(1)} %encode.1.after_ref), channel_id=1, source_target_pairs={{0,8},{8,0},{16,24},{24,16},{32,40},{40,32},{48,56},{56,48},{64,72... | collective-permute-start | bytes 3145736 | tf_op jit(solution)/shard_map/ppermute | solution.py:367
  3.3 3.1 %box_sums.1 = (bf16[64,16,128]{2,1,0:T(8,128)(2,1)S(1)}, bf16[64,16,128]{2,1,0:T(8,128)(2,1)S(1)}) custom-call(s32[1,128]{1,0:T(1,128)S(1)} %copy-done.2, s16[64,8192]{1,0:T(8,128)(2,1)S(1)} %encode.1.after_ref, s32[128,128]{1,0:T(8,128)} %bitcast.3, bf16[128,128,128]{2,1,0:T(8,128)(2,1)} %bitcast.2), custom_call_target="tpu_custom_call" | custom-call | flops 1000 | bytes 1000 | tf_op jit(solution)/shard_map/box_sums/pallas_call | solution.py:159
  6.4 1.5 %collective-permute-done.got_ref = bf16[64,16,128]{2,1,0:T(8,128)(2,1)S(1)} collective-permute-done((bf16[64,16,128]{2,1,0:T(8,128)(2,1)S(1)}, bf16[64,16,128]{2,1,0:T(8,128)(2,1)S(1)}, u32[]{:S(2)}, u32[]{:S(2)}) %collective-permute-start) | collective-permute-done | bytes 262176 | tf_op jit(solution)/shard_map/ppermute | solution.py:367
  8.0 16.7 %all_to_all.5.parts_ref = bf16[16,4,16,128]{3,2,1,0:T(8,128)(2,1)S(1)} all-to-all(bf16[16,4,16,128]{3,2,1,0:T(8,128)(2,1)S(1)} %deal.1), channel_id=1, replica_groups={{0,2,4,6,32,34,36,38,64,66,68,70,96,98,100,102},{1,3,5,7,33,35,37,39,65..., dimensions={0} | all-to-all | bytes 524288 | tf_op jit(solution)/shard_map/all_to_all | solution.py:380
  24.8 0.6 collective-permute-start.1
  25.4 3.0 %collective-permute-start.2 = (f32[4,16,128]{2,1,0:T(8,128)S(1)}, f32[4,16,128]{2,1,0:T(8,128)S(1)}, u32[]{:S(2)}, u32[]{:S(2)}) collective-permute-start(f32[4,16,128]{2,1,0:T(8,128)S(1)} %add.1.after_ref.refs_0_), channel_id=1, source_target_pairs={{0,16},{8,24},{16,0},{24,8},{32,48},{40,56},{48,32},{56,40},{64,80... | collective-permute-start | bytes 98312 | tf_op jit(solution)/shard_map/ppermute | solution.py:367
  28.4 1.1 %collective-permute-start.3 = (f32[4,16,128]{2,1,0:T(8,128)S(1)}, f32[4,16,128]{2,1,0:T(8,128)S(1)}, u32[]{:S(2)}, u32[]{:S(2)}) collective-permute-start(f32[4,16,128]{2,1,0:T(8,128)S(1)} %add.1.after_ref.refs_0_), channel_id=1, source_target_pairs={{0,24},{8,16},{16,8},{24,0},{32,56},{40,48},{48,40},{56,32},{64,88... | collective-permute-start | bytes 98312 | tf_op jit(solution)/shard_map/ppermute | solution.py:367
  29.5 2.9 %fetch.2.after_ref.phases_ref = f32[3,64,8192]{2,1,0:T(8,128)S(1)} custom-call(f32[4,16,128]{2,1,0:T(8,128)S(1)} %add.1.after_ref.refs_0_, f32[5,64,8192]{2,1,0:T(8,128)} %phases_ref.5), custom_call_target="tpu_custom_call" | custom-call | flops 1000 | bytes 1000 | tf_op jit(solution)/shard_map/fetch/pallas_call | solution.py:117
  32.6 0.9 collective-permute-done.3.refs_3_
  33.7 0.9 a_0.1.rest_0_.state_ref
  34.6 0.9 a_2.1.rest_0_.state_ref
  35.5 0.6 collective-permute-start.8
  36.5 0.7 collective-permute-start.6
  37.2 1.7 %a_4.1.rest_0_.state_ref = bf16[128,2048]{1,0:T(8,128)(2,1)S(1)} custom-call(f32[16,128]{1,0:T(8,128)S(1)} %get-tuple-element.15.x_ref, f32[16,128]{1,0:T(8,128)S(1)} %get-tuple-element.16.other_x_ref, bf16[128,256]{1,0:T(8,128)(2,1)S(1)} %get-tuple-element.17.mats_ref, f32[3,64,8192]{2,1,0:T(8,128)S(1)} %fetch.2.after_ref.phases_ref, ...), custom_call_target="tpu_custom_call" | custom-call | flops 10000000000 | bytes 1000 | tf_op jit(solution)/shard_map/a_4/pallas_call | solution.py:271
  39.0 0.3 b_2.1.rest_0_.state_ref
  39.3 1.5 %collective-permute-done.7.partner_ref = bf16[128,2048]{1,0:T(8,128)(2,1)S(1)} collective-permute-done((bf16[128,2048]{1,0:T(8,128)(2,1)S(1)}, bf16[128,2048]{1,0:T(8,128)(2,1)S(1)}, u32[]{:S(2)}, u32[]{:S(2)}) %collective-permute-start.7) | collective-permute-done | bytes 524320 | tf_op jit(solution)/shard_map/ppermute | solution.py:367
  41.2 3.0 %collective-permute-start.12 = (bf16[128,1024]{1,0:T(8,128)(2,1)S(1)}, bf16[128,1024]{1,0:T(8,128)(2,1)S(1)}, u32[]{:S(2)}, u32[]{:S(2)}) collective-permute-start(bf16[128,1024]{1,0:T(8,128)(2,1)S(1)} %b_2.1.rest_0_.state_ref), channel_id=1, source_target_pairs={{0,16},{8,24},{16,0},{24,8},{32,48},{40,56},{48,32},{56,40},{64,80... | collective-permute-start | bytes 786440 | tf_op jit(solution)/shard_map/ppermute | solution.py:367
  44.2 2.2 %fetch.3.phases_ref.rest_0_ = f32[2,64,8192]{2,1,0:T(8,128)S(1)} custom-call(bf16[128,1024]{1,0:T(8,128)(2,1)S(1)} %b_4.1.after_ref.state_ref, f32[5,64,8192]{2,1,0:T(8,128)} %phases_ref.5), custom_call_target="tpu_custom_call" | custom-call | flops 1000 | bytes 1000 | tf_op jit(solution)/shard_map/fetch/pallas_call | solution.py:117
  46.4 0.7 collective-permute-start.10
  47.6 0.5 collective-permute-start.9
  48.1 1.7 %a_8.1.rest_0_.state_ref = bf16[128,2048]{1,0:T(8,128)(2,1)S(1)} custom-call(f32[16,128]{1,0:T(8,128)S(1)} %get-tuple-element.15.x_ref, f32[16,128]{1,0:T(8,128)S(1)} %get-tuple-element.16.other_x_ref, bf16[128,256]{1,0:T(8,128)(2,1)S(1)} %get-tuple-element.17.mats_ref, f32[3,64,8192]{2,1,0:T(8,128)S(1)} %fetch.2.after_ref.phases_ref, ...), custom_call_target="tpu_custom_call" | custom-call | flops 10000000000 | bytes 1000 | tf_op jit(solution)/shard_map/a_8/pallas_call | solution.py:271
  50.2 3.1 %collective-permute-start.17 = (bf16[128,1024]{1,0:T(8,128)(2,1)S(1)}, bf16[128,1024]{1,0:T(8,128)(2,1)S(1)}, u32[]{:S(2)}, u32[]{:S(2)}) collective-permute-start(bf16[128,1024]{1,0:T(8,128)(2,1)S(1)} %b_6.1.rest_0_.state_ref), channel_id=1, source_target_pairs={{0,16},{8,24},{16,0},{24,8},{32,48},{40,56},{48,32},{56,40},{64,80... | collective-permute-start | bytes 786440 | tf_op jit(solution)/shard_map/ppermute | solution.py:367
  53.3 0.3 c_2.1.rest_0_.state_ref
  53.6 1.7 %collective-permute-start.16 = (bf16[128,1024]{1,0:T(8,128)(2,1)S(1)}, bf16[128,1024]{1,0:T(8,128)(2,1)S(1)}, u32[]{:S(2)}, u32[]{:S(2)}) collective-permute-start(bf16[128,1024]{1,0:T(8,128)(2,1)S(1)} %c_2.1.rest_0_.state_ref), channel_id=1, source_target_pairs={{0,2},{1,3},{2,0},{3,1},{4,6},{5,7},{6,4},{7,5},{8,10},{9,11},{10,... | collective-permute-start | bytes 786440 | tf_op jit(solution)/shard_map/ppermute | solution.py:367
  55.6 0.8 collective-permute-start.15
  56.4 2.1 %collective-permute-done.10.partner_ref = bf16[128,1024]{1,0:T(8,128)(2,1)S(1)} collective-permute-done((bf16[128,1024]{1,0:T(8,128)(2,1)S(1)}, bf16[128,1024]{1,0:T(8,128)(2,1)S(1)}, u32[]{:S(2)}, u32[]{:S(2)}) %collective-permute-start.10) | collective-permute-done | bytes 262176 | tf_op jit(solution)/shard_map/ppermute | solution.py:367
  58.8 0.5 collective-permute-start.14
  59.7 1.7 %a_12.1.rest_0_.state_ref = bf16[128,2048]{1,0:T(8,128)(2,1)S(1)} custom-call(f32[16,128]{1,0:T(8,128)S(1)} %get-tuple-element.15.x_ref, f32[16,128]{1,0:T(8,128)S(1)} %get-tuple-element.16.other_x_ref, bf16[128,256]{1,0:T(8,128)(2,1)S(1)} %get-tuple-element.17.mats_ref, f32[3,64,8192]{2,1,0:T(8,128)S(1)} %fetch.2.after_ref.phases_ref, ...), custom_call_target="tpu_custom_call" | custom-call | flops 10000000000 | bytes 1000 | tf_op jit(solution)/shard_map/a_12/pallas_call | solution.py:271
  61.5 0.3 b_10.1.rest_0_.state_ref
  61.8 2.3 %collective-permute-done.17.partner_ref = bf16[128,1024]{1,0:T(8,128)(2,1)S(1)} collective-permute-done((bf16[128,1024]{1,0:T(8,128)(2,1)S(1)}, bf16[128,1024]{1,0:T(8,128)(2,1)S(1)}, u32[]{:S(2)}, u32[]{:S(2)}) %collective-permute-start.17) | collective-permute-done | bytes 262176 | tf_op jit(solution)/shard_map/ppermute | solution.py:367
  64.1 2.0 %collective-permute-start.22 = (bf16[128,1024]{1,0:T(8,128)(2,1)S(1)}, bf16[128,1024]{1,0:T(8,128)(2,1)S(1)}, u32[]{:S(2)}, u32[]{:S(2)}) collective-permute-start(bf16[128,1024]{1,0:T(8,128)(2,1)S(1)} %b_10.1.rest_0_.state_ref), channel_id=1, source_target_pairs={{0,16},{8,24},{16,0},{24,8},{32,48},{40,56},{48,32},{56,40},{64,80... | collective-permute-start | bytes 786440 | tf_op jit(solution)/shard_map/ppermute | solution.py:367
  67.1 0.3 b_12.1.rest_0_.state_ref
  67.4 1.8 %collective-permute-start.20 = (bf16[128,1024]{1,0:T(8,128)(2,1)S(1)}, bf16[128,1024]{1,0:T(8,128)(2,1)S(1)}, u32[]{:S(2)}, u32[]{:S(2)}) collective-permute-start(bf16[128,1024]{1,0:T(8,128)(2,1)S(1)} %b_12.1.rest_0_.state_ref), channel_id=1, source_target_pairs={{0,16},{8,24},{16,0},{24,8},{32,48},{40,56},{48,32},{56,40},{64,80... | collective-permute-start | bytes 786440 | tf_op jit(solution)/shard_map/ppermute | solution.py:367
  69.3 0.4 collective-permute-done.15.partner_ref
  70.0 1.2 %collective-permute-start.19 = (bf16[128,1024]{1,0:T(8,128)(2,1)S(1)}, bf16[128,1024]{1,0:T(8,128)(2,1)S(1)}, u32[]{:S(2)}, u32[]{:S(2)}) collective-permute-start(bf16[128,1024]{1,0:T(8,128)(2,1)S(1)} %c_8.1.rest_0_.state_ref), channel_id=1, source_target_pairs={{0,2},{1,3},{2,0},{3,1},{4,6},{5,7},{6,4},{7,5},{8,10},{9,11},{10,... | collective-permute-start | bytes 786440 | tf_op jit(solution)/shard_map/ppermute | solution.py:367
  71.6 0.3 b_14.1.rest_0_.state_ref
  72.0 2.1 %collective-permute-start.18 = (bf16[128,1024]{1,0:T(8,128)(2,1)S(1)}, bf16[128,1024]{1,0:T(8,128)(2,1)S(1)}, u32[]{:S(2)}, u32[]{:S(2)}) collective-permute-start(bf16[128,1024]{1,0:T(8,128)(2,1)S(1)} %b_14.1.rest_0_.state_ref), channel_id=1, source_target_pairs={{0,16},{8,24},{16,0},{24,8},{32,48},{40,56},{48,32},{56,40},{64,80... | collective-permute-start | bytes 786440 | tf_op jit(solution)/shard_map/ppermute | solution.py:367
  74.0 1.3 %collective-permute-done.22.partner_ref = bf16[128,1024]{1,0:T(8,128)(2,1)S(1)} collective-permute-done((bf16[128,1024]{1,0:T(8,128)(2,1)S(1)}, bf16[128,1024]{1,0:T(8,128)(2,1)S(1)}, u32[]{:S(2)}, u32[]{:S(2)}) %collective-permute-start.22) | collective-permute-done | bytes 262176 | tf_op jit(solution)/shard_map/ppermute | solution.py:367
  75.7 0.5 collective-permute-start.24
  76.5 4.4 %collective-permute-done.20.partner_ref = bf16[128,1024]{1,0:T(8,128)(2,1)S(1)} collective-permute-done((bf16[128,1024]{1,0:T(8,128)(2,1)S(1)}, bf16[128,1024]{1,0:T(8,128)(2,1)S(1)}, u32[]{:S(2)}, u32[]{:S(2)}) %collective-permute-start.20) | collective-permute-done | bytes 262176 | tf_op jit(solution)/shard_map/ppermute | solution.py:367
  81.3 0.5 collective-permute-start.25
  82.2 3.6 %collective-permute-done.18.partner_ref = bf16[128,1024]{1,0:T(8,128)(2,1)S(1)} collective-permute-done((bf16[128,1024]{1,0:T(8,128)(2,1)S(1)}, bf16[128,1024]{1,0:T(8,128)(2,1)S(1)}, u32[]{:S(2)}, u32[]{:S(2)}) %collective-permute-start.18) | collective-permute-done | bytes 262176 | tf_op jit(solution)/shard_map/ppermute | solution.py:367
  86.1 0.5 collective-permute-start.23
  87.1 5.3 %collective-permute-done.25.partner_ref = bf16[128,1024]{1,0:T(8,128)(2,1)S(1)} collective-permute-done((bf16[128,1024]{1,0:T(8,128)(2,1)S(1)}, bf16[128,1024]{1,0:T(8,128)(2,1)S(1)}, u32[]{:S(2)}, u32[]{:S(2)}) %collective-permute-start.25) | collective-permute-done | bytes 262176 | tf_op jit(solution)/shard_map/ppermute | solution.py:367
  92.7 1.3 %flush.1.before_ref = bf16[128,8192]{1,0:T(8,128)(2,1)} custom-call(bf16[128,1024]{1,0:T(8,128)(2,1)S(1)} %d_0.1.rest_0_.refs_0_, bf16[128,1024]{1,0:T(8,128)(2,1)S(1)} %d_2.1.rest_0_.refs_1_, bf16[128,1024]{1,0:T(8,128)(2,1)S(1)} %d_4.1.rest_0_.refs_2_, bf16[128,1024]{1,0:T(8,128)(2,1)S(1)} %d_6.1.rest_0_.refs_3_, ...), custom_call_target="tpu_custom_call" | custom-call | flops 10000000000 | bytes 1000 | tf_op jit(solution)/shard_map/flush/pallas_call | solution.py:326
  94.0 1.9 %collective-permute-done.23.partner_ref = bf16[128,1024]{1,0:T(8,128)(2,1)S(1)} collective-permute-done((bf16[128,1024]{1,0:T(8,128)(2,1)S(1)}, bf16[128,1024]{1,0:T(8,128)(2,1)S(1)}, u32[]{:S(2)}, u32[]{:S(2)}) %collective-permute-start.23) | collective-permute-done | bytes 262176 | tf_op jit(solution)/shard_map/ppermute | solution.py:367
  95.8 1.0 %last.1 = bf16[128,8192]{1,0:T(8,128)(2,1)} custom-call(bf16[128,1024]{1,0:T(8,128)(2,1)S(1)} %c_14.1.rest_0_.state_ref, bf16[128,1024]{1,0:T(8,128)(2,1)S(1)} %collective-permute-done.23.partner_ref, bf16[128,256]{1,0:T(8,128)(2,1)S(1)} %get-tuple-element.20.mats_ref, f32[2,64,8192]{2,1,0:T(8,128)S(1)} %fetch.3.phases_ref.rest_0_, ...), custom_call_target="tpu_custom_call", output_to_operand_aliasing={{}: (4, {})} | custom-call | flops 10000000000 | bytes 1000 | tf_op jit(solution)/shard_map/last/pallas_call | solution.py:350
  (49 shorter events, 7.4 us)
Async XLA Ops:
  0.0 3.3 %copy-start.2 = (s32[1,128]{1,0:T(1,128)S(1)}, s32[1,128]{1,0:T(1,128)}, u32[]{:S(2)}) copy-start(s32[1,128]{1,0:T(1,128)} %counts_ref.1) | copy-start | bytes 1540
  1.6 32.0 %collective-permute-start.4 = (s16[64,8192]{1,0:T(8,128)(2,1)S(1)}, s16[64,8192]{1,0:T(8,128)(2,1)S(1)}, u32[]{:S(2)}, u32[]{:S(2)}) collective-permute-start(s16[64,8192]{1,0:T(8,128)(2,1)S(1)} %encode.1.after_ref), channel_id=1, source_target_pairs={{0,8},{8,0},{16,24},{24,16},{32,40},{40,32},{48,56},{56,48},{64,72... | collective-permute-start | bytes 3145736 | tf_op jit(solution)/shard_map/ppermute | solution.py:367
  6.4 1.6 %collective-permute-start = (bf16[64,16,128]{2,1,0:T(8,128)(2,1)S(1)}, bf16[64,16,128]{2,1,0:T(8,128)(2,1)S(1)}, u32[]{:S(2)}, u32[]{:S(2)}) collective-permute-start(bf16[64,16,128]{2,1,0:T(8,128)(2,1)S(1)} %get-tuple-element.14), channel_id=1, source_target_pairs={{0,1},{1,0},{2,3},{3,2},{4,5},{5,4},{6,7},{7,6},{8,9},{9,8},{10,11... | collective-permute-start | bytes 786440 | tf_op jit(solution)/shard_map/ppermute | solution.py:367
  24.7 7.7 %copy-start = (bf16[4,2,2,128,128]{4,3,2,1,0:T(8,128)(2,1)S(1)}, bf16[4,2,2,128,128]{4,3,2,1,0:T(8,128)(2,1)}, u32[]{:S(2)}) copy-start(bf16[4,2,2,128,128]{4,3,2,1,0:T(8,128)(2,1)} %trans_ref.1) | copy-start | bytes 1572868
  24.7 8.8 %copy-start.1 = (bf16[128,128]{1,0:T(8,128)(2,1)S(1)}, bf16[128,128]{1,0:T(8,128)(2,1)}, u32[]{:S(2)}) copy-start(bf16[128,128]{1,0:T(8,128)(2,1)} %map_ref.1) | copy-start | bytes 98308
  24.8 7.8 %collective-permute-start.1 = (f32[4,16,128]{2,1,0:T(8,128)S(1)}, f32[4,16,128]{2,1,0:T(8,128)S(1)}, u32[]{:S(2)}, u32[]{:S(2)}) collective-permute-start(f32[4,16,128]{2,1,0:T(8,128)S(1)} %add.1.after_ref.refs_0_), channel_id=1, source_target_pairs={{0,8},{8,0},{16,24},{24,16},{32,40},{40,32},{48,56},{56,48},{64,72... | collective-permute-start | bytes 98312 | tf_op jit(solution)/shard_map/ppermute | solution.py:367
  25.4 7.2 %collective-permute-start.2 = (f32[4,16,128]{2,1,0:T(8,128)S(1)}, f32[4,16,128]{2,1,0:T(8,128)S(1)}, u32[]{:S(2)}, u32[]{:S(2)}) collective-permute-start(f32[4,16,128]{2,1,0:T(8,128)S(1)} %add.1.after_ref.refs_0_), channel_id=1, source_target_pairs={{0,16},{8,24},{16,0},{24,8},{32,48},{40,56},{48,32},{56,40},{64,80... | collective-permute-start | bytes 98312 | tf_op jit(solution)/shard_map/ppermute | solution.py:367
  28.4 5.1 %collective-permute-start.3 = (f32[4,16,128]{2,1,0:T(8,128)S(1)}, f32[4,16,128]{2,1,0:T(8,128)S(1)}, u32[]{:S(2)}, u32[]{:S(2)}) collective-permute-start(f32[4,16,128]{2,1,0:T(8,128)S(1)} %add.1.after_ref.refs_0_), channel_id=1, source_target_pairs={{0,24},{8,16},{16,8},{24,0},{32,56},{40,48},{48,40},{56,32},{64,88... | collective-permute-start | bytes 98312 | tf_op jit(solution)/shard_map/ppermute | solution.py:367
  34.5 1.6 %collective-permute-start.5 = (bf16[128,1024]{1,0:T(8,128)(2,1)S(1)}, bf16[128,1024]{1,0:T(8,128)(2,1)S(1)}, u32[]{:S(2)}, u32[]{:S(2)}) collective-permute-start(bf16[128,1024]{1,0:T(8,128)(2,1)S(1)} %a_0.1.rest_0_.state_ref), channel_id=1, source_target_pairs={{0,1},{1,0},{2,3},{3,2},{4,5},{5,4},{6,7},{7,6},{8,9},{9,8},{10,11... | collective-permute-start | bytes 786440 | tf_op jit(solution)/shard_map/ppermute | solution.py:367
  35.5 3.4 %collective-permute-start.8 = (bf16[128,1024]{1,0:T(8,128)(2,1)S(1)}, bf16[128,1024]{1,0:T(8,128)(2,1)S(1)}, u32[]{:S(2)}, u32[]{:S(2)}) collective-permute-start(bf16[128,1024]{1,0:T(8,128)(2,1)S(1)} %a_2.1.rest_0_.state_ref), channel_id=1, source_target_pairs={{0,1},{1,0},{2,3},{3,2},{4,5},{5,4},{6,7},{7,6},{8,9},{9,8},{10,11... | collective-permute-start | bytes 786440 | tf_op jit(solution)/shard_map/ppermute | solution.py:367
  36.5 10.7 %collective-permute-start.6 = (bf16[128,1024]{1,0:T(8,128)(2,1)S(1)}, bf16[128,1024]{1,0:T(8,128)(2,1)S(1)}, u32[]{:S(2)}, u32[]{:S(2)}) collective-permute-start(bf16[128,1024]{1,0:T(8,128)(2,1)S(1)} %b_0.1.rest_0_.state_ref), channel_id=1, source_target_pairs={{0,16},{8,24},{16,0},{24,8},{32,48},{40,56},{48,32},{56,40},{64,80... | collective-permute-start | bytes 786440 | tf_op jit(solution)/shard_map/ppermute | solution.py:367
  38.9 2.0 %collective-permute-start.7 = (bf16[128,2048]{1,0:T(8,128)(2,1)S(1)}, bf16[128,2048]{1,0:T(8,128)(2,1)S(1)}, u32[]{:S(2)}, u32[]{:S(2)}) collective-permute-start(bf16[128,2048]{1,0:T(8,128)(2,1)S(1)} %a_4.1.rest_0_.state_ref), channel_id=1, source_target_pairs={{0,1},{1,0},{2,3},{3,2},{4,5},{5,4},{6,7},{7,6},{8,9},{9,8},{10,11... | collective-permute-start | bytes 1572872 | tf_op jit(solution)/shard_map/ppermute | solution.py:367
  41.2 12.1 %collective-permute-start.12 = (bf16[128,1024]{1,0:T(8,128)(2,1)S(1)}, bf16[128,1024]{1,0:T(8,128)(2,1)S(1)}, u32[]{:S(2)}, u32[]{:S(2)}) collective-permute-start(bf16[128,1024]{1,0:T(8,128)(2,1)S(1)} %b_2.1.rest_0_.state_ref), channel_id=1, source_target_pairs={{0,16},{8,24},{16,0},{24,8},{32,48},{40,56},{48,32},{56,40},{64,80... | collective-permute-start | bytes 786440 | tf_op jit(solution)/shard_map/ppermute | solution.py:367
  46.4 12.0 %collective-permute-start.10 = (bf16[128,1024]{1,0:T(8,128)(2,1)S(1)}, bf16[128,1024]{1,0:T(8,128)(2,1)S(1)}, u32[]{:S(2)}, u32[]{:S(2)}) collective-permute-start(bf16[128,1024]{1,0:T(8,128)(2,1)S(1)} %b_4.1.after_ref.state_ref), channel_id=1, source_target_pairs={{0,16},{8,24},{16,0},{24,8},{32,48},{40,56},{48,32},{56,40},{64,80... | collective-permute-start | bytes 786440 | tf_op jit(solution)/shard_map/ppermute | solution.py:367
  47.6 11.8 %collective-permute-start.9 = (bf16[128,1024]{1,0:T(8,128)(2,1)S(1)}, bf16[128,1024]{1,0:T(8,128)(2,1)S(1)}, u32[]{:S(2)}, u32[]{:S(2)}) collective-permute-start(bf16[128,1024]{1,0:T(8,128)(2,1)S(1)} %c_0.1.rest_0_.state_ref), channel_id=1, source_target_pairs={{0,2},{1,3},{2,0},{3,1},{4,6},{5,7},{6,4},{7,5},{8,10},{9,11},{10,... | collective-permute-start | bytes 786440 | tf_op jit(solution)/shard_map/ppermute | solution.py:367
  49.8 5.5 %collective-permute-start.11 = (bf16[128,2048]{1,0:T(8,128)(2,1)S(1)}, bf16[128,2048]{1,0:T(8,128)(2,1)S(1)}, u32[]{:S(2)}, u32[]{:S(2)}) collective-permute-start(bf16[128,2048]{1,0:T(8,128)(2,1)S(1)} %a_8.1.rest_0_.state_ref), channel_id=1, source_target_pairs={{0,1},{1,0},{2,3},{3,2},{4,5},{5,4},{6,7},{7,6},{8,9},{9,8},{10,11... | collective-permute-start | bytes 1572872 | tf_op jit(solution)/shard_map/ppermute | solution.py:367
  50.2 13.9 %collective-permute-start.17 = (bf16[128,1024]{1,0:T(8,128)(2,1)S(1)}, bf16[128,1024]{1,0:T(8,128)(2,1)S(1)}, u32[]{:S(2)}, u32[]{:S(2)}) collective-permute-start(bf16[128,1024]{1,0:T(8,128)(2,1)S(1)} %b_6.1.rest_0_.state_ref), channel_id=1, source_target_pairs={{0,16},{8,24},{16,0},{24,8},{32,48},{40,56},{48,32},{56,40},{64,80... | collective-permute-start | bytes 786440 | tf_op jit(solution)/shard_map/ppermute | solution.py:367
  53.6 12.8 %collective-permute-start.16 = (bf16[128,1024]{1,0:T(8,128)(2,1)S(1)}, bf16[128,1024]{1,0:T(8,128)(2,1)S(1)}, u32[]{:S(2)}, u32[]{:S(2)}) collective-permute-start(bf16[128,1024]{1,0:T(8,128)(2,1)S(1)} %c_2.1.rest_0_.state_ref), channel_id=1, source_target_pairs={{0,2},{1,3},{2,0},{3,1},{4,6},{5,7},{6,4},{7,5},{8,10},{9,11},{10,... | collective-permute-start | bytes 786440 | tf_op jit(solution)/shard_map/ppermute | solution.py:367
  55.6 14.1 %collective-permute-start.15 = (bf16[128,1024]{1,0:T(8,128)(2,1)S(1)}, bf16[128,1024]{1,0:T(8,128)(2,1)S(1)}, u32[]{:S(2)}, u32[]{:S(2)}) collective-permute-start(bf16[128,1024]{1,0:T(8,128)(2,1)S(1)} %b_8.1.rest_0_.state_ref), channel_id=1, source_target_pairs={{0,16},{8,24},{16,0},{24,8},{32,48},{40,56},{48,32},{56,40},{64,80... | collective-permute-start | bytes 786440 | tf_op jit(solution)/shard_map/ppermute | solution.py:367
  58.8 12.5 %collective-permute-start.14 = (bf16[128,1024]{1,0:T(8,128)(2,1)S(1)}, bf16[128,1024]{1,0:T(8,128)(2,1)S(1)}, u32[]{:S(2)}, u32[]{:S(2)}) collective-permute-start(bf16[128,1024]{1,0:T(8,128)(2,1)S(1)} %c_4.1.rest_0_.state_ref), channel_id=1, source_target_pairs={{0,2},{1,3},{2,0},{3,1},{4,6},{5,7},{6,4},{7,5},{8,10},{9,11},{10,... | collective-permute-start | bytes 786440 | tf_op jit(solution)/shard_map/ppermute | solution.py:367
  61.4 5.7 %collective-permute-start.13 = (bf16[128,2048]{1,0:T(8,128)(2,1)S(1)}, bf16[128,2048]{1,0:T(8,128)(2,1)S(1)}, u32[]{:S(2)}, u32[]{:S(2)}) collective-permute-start(bf16[128,2048]{1,0:T(8,128)(2,1)S(1)} %a_12.1.rest_0_.state_ref), channel_id=1, source_target_pairs={{0,1},{1,0},{2,3},{3,2},{4,5},{5,4},{6,7},{7,6},{8,9},{9,8},{10,11... | collective-permute-start | bytes 1572872 | tf_op jit(solution)/shard_map/ppermute | solution.py:367
  64.1 11.2 %collective-permute-start.22 = (bf16[128,1024]{1,0:T(8,128)(2,1)S(1)}, bf16[128,1024]{1,0:T(8,128)(2,1)S(1)}, u32[]{:S(2)}, u32[]{:S(2)}) collective-permute-start(bf16[128,1024]{1,0:T(8,128)(2,1)S(1)} %b_10.1.rest_0_.state_ref), channel_id=1, source_target_pairs={{0,16},{8,24},{16,0},{24,8},{32,48},{40,56},{48,32},{56,40},{64,80... | collective-permute-start | bytes 786440 | tf_op jit(solution)/shard_map/ppermute | solution.py:367
  66.4 9.8 %collective-permute-start.21 = (bf16[128,1024]{1,0:T(8,128)(2,1)S(1)}, bf16[128,1024]{1,0:T(8,128)(2,1)S(1)}, u32[]{:S(2)}, u32[]{:S(2)}) collective-permute-start(bf16[128,1024]{1,0:T(8,128)(2,1)S(1)} %c_6.1.rest_0_.state_ref), channel_id=1, source_target_pairs={{0,2},{1,3},{2,0},{3,1},{4,6},{5,7},{6,4},{7,5},{8,10},{9,11},{10,... | collective-permute-start | bytes 786440 | tf_op jit(solution)/shard_map/ppermute | solution.py:367
  67.4 13.5 %collective-permute-start.20 = (bf16[128,1024]{1,0:T(8,128)(2,1)S(1)}, bf16[128,1024]{1,0:T(8,128)(2,1)S(1)}, u32[]{:S(2)}, u32[]{:S(2)}) collective-permute-start(bf16[128,1024]{1,0:T(8,128)(2,1)S(1)} %b_12.1.rest_0_.state_ref), channel_id=1, source_target_pairs={{0,16},{8,24},{16,0},{24,8},{32,48},{40,56},{48,32},{56,40},{64,80... | collective-permute-start | bytes 786440 | tf_op jit(solution)/shard_map/ppermute | solution.py:367
  70.0 11.8 %collective-permute-start.19 = (bf16[128,1024]{1,0:T(8,128)(2,1)S(1)}, bf16[128,1024]{1,0:T(8,128)(2,1)S(1)}, u32[]{:S(2)}, u32[]{:S(2)}) collective-permute-start(bf16[128,1024]{1,0:T(8,128)(2,1)S(1)} %c_8.1.rest_0_.state_ref), channel_id=1, source_target_pairs={{0,2},{1,3},{2,0},{3,1},{4,6},{5,7},{6,4},{7,5},{8,10},{9,11},{10,... | collective-permute-start | bytes 786440 | tf_op jit(solution)/shard_map/ppermute | solution.py:367
  72.0 13.8 %collective-permute-start.18 = (bf16[128,1024]{1,0:T(8,128)(2,1)S(1)}, bf16[128,1024]{1,0:T(8,128)(2,1)S(1)}, u32[]{:S(2)}, u32[]{:S(2)}) collective-permute-start(bf16[128,1024]{1,0:T(8,128)(2,1)S(1)} %b_14.1.rest_0_.state_ref), channel_id=1, source_target_pairs={{0,16},{8,24},{16,0},{24,8},{32,48},{40,56},{48,32},{56,40},{64,80... | collective-permute-start | bytes 786440 | tf_op jit(solution)/shard_map/ppermute | solution.py:367
  75.7 11.0 %collective-permute-start.24 = (bf16[128,1024]{1,0:T(8,128)(2,1)S(1)}, bf16[128,1024]{1,0:T(8,128)(2,1)S(1)}, u32[]{:S(2)}, u32[]{:S(2)}) collective-permute-start(bf16[128,1024]{1,0:T(8,128)(2,1)S(1)} %c_10.1.rest_0_.state_ref), channel_id=1, source_target_pairs={{0,2},{1,3},{2,0},{3,1},{4,6},{5,7},{6,4},{7,5},{8,10},{9,11},{10,... | collective-permute-start | bytes 786440 | tf_op jit(solution)/shard_map/ppermute | solution.py:367
  81.3 11.0 %collective-permute-start.25 = (bf16[128,1024]{1,0:T(8,128)(2,1)S(1)}, bf16[128,1024]{1,0:T(8,128)(2,1)S(1)}, u32[]{:S(2)}, u32[]{:S(2)}) collective-permute-start(bf16[128,1024]{1,0:T(8,128)(2,1)S(1)} %c_12.1.rest_0_.state_ref), channel_id=1, source_target_pairs={{0,2},{1,3},{2,0},{3,1},{4,6},{5,7},{6,4},{7,5},{8,10},{9,11},{10,... | collective-permute-start | bytes 786440 | tf_op jit(solution)/shard_map/ppermute | solution.py:367
  86.1 9.7 %collective-permute-start.23 = (bf16[128,1024]{1,0:T(8,128)(2,1)S(1)}, bf16[128,1024]{1,0:T(8,128)(2,1)S(1)}, u32[]{:S(2)}, u32[]{:S(2)}) collective-permute-start(bf16[128,1024]{1,0:T(8,128)(2,1)S(1)} %c_14.1.rest_0_.state_ref), channel_id=1, source_target_pairs={{0,2},{1,3},{2,0},{3,1},{4,6},{5,7},{6,4},{7,5},{8,10},{9,11},{10,... | collective-permute-start | bytes 786440 | tf_op jit(solution)/shard_map/ppermute | solution.py:367

commit v5 on v4

--- a/solution.py
+++ b/solution.py
@@ -381,9 +381,9 @@
         deal(keep, got), ("bx", "by"), split_axis=0, concat_axis=0, tiled=True, axis_index_groups=plane
     )
     row = add(parts)
-    early = fetch(0, 3, row, phases)
+    early = phases[0:3]
     mats = pick_mats(row, trans)
-    mine, theirs = expand(early, source_map, [row] + [move(row, "bx", k) for k in (1, 2, 3)])
+    mine, theirs = expand(mats[0], source_map, [row] + [move(row, "bx", k) for k in (1, 2, 3)])
 
     starts = [sum(PARTS[:i]) for i in range(len(PARTS))]
     groups = [range(sum(GROUPS[:g]), sum(GROUPS[: g + 1])) for g in range(len(GROUPS))]
@@ -392,7 +392,7 @@
     after = []
     for name in ORDER.split():
         if name == "f":
-            after = [late := fetch(3, 2, after[0], phases)]
+            late = phases[3:5]
             continue
         level, i = name[0], int(name[1:])
         if level == "a":

time: 97.2 us -> 96.2 us (0.990)
  waiting for transfers between devices: 25.5 us -> 31.3 us
  Pallas kernels: 26.9 us -> 21.9 us
  starting transfers between devices: 27.4 us -> 24 us
  local copies, waits for them, and re-layouts: 0.02 us -> 1.64 us
    ppermute x26, waiting for transfers between devices: 25.5 us -> 31.3 us  [move(): lax.ppermute(value, axis, [(s, s ^ mask) for s in range(lax.axis_size(axi...]
    pallas_call x2 -> x0, Pallas kernels: 5.12 us -> none  [fetch(): kernel_call(functools.partial(fetch_kernel, first), in_specs=[ANY, ANY],...]
    ppermute x26, starting transfers between devices: 27.4 us -> 24 us  [move(): lax.ppermute(value, axis, [(s, s ^ mask) for s in range(lax.axis_size(axi...]
  transfers between devices with their start and end apart: 26 -> 26, of which waited for: 14 -> 14; matrix products, arithmetic and copies ran while one was open for 0% -> 1% of each run, Pallas kernels for 24% -> 19%
where the time goes in v5:
time: 96.2 us; the launch traced here: 96 us
  waiting for transfers between devices  31.3 us (33%)
  starting transfers between devices  24 us (25%)
  Pallas kernels  21.9 us (23%)
  blocking collectives  16.7 us (17%)
  local copies, waits for them, and re-layouts  1.64 us (2%)
    ppermute x26, waiting for transfers between devices, move(): lax.ppermute(value, axis, [(s, s ^ mask) for s in range(lax.axis_size(axi...  31.3 us
    ppermute x26, starting transfers between devices, move(): lax.ppermute(value, axis, [(s, s ^ mask) for s in range(lax.axis_size(axi...  24 us
    all_to_all x1, blocking collectives, per_device(): lax.all_to_all(deal(keep, got), ('bx', 'by'), split_axis=0, concat_axis=0...  16.7 us
    pallas_call x23, Pallas kernels, next_level(): kernel_call(functools.partial(level_kernel, start, boxes, skip, slot), in...  7.66 us
    pallas_call x5, Pallas kernels, first_level(): kernel_call(functools.partial(first_kernel, start, boxes), in_specs=[VMEM...  6.75 us
    pallas_call x1, Pallas kernels, box_sums(): kernel_call(box_sums_kernel, in_specs=[SMEM, ANY, ANY, ANY], out_specs=[V...  3.07 us
  transfers between devices with their start and end apart: 26, of which 14 were waited for; matrix products, arithmetic and copies ran while one was open for 1% of the time, Pallas kernels for 19%

profile of v5, /device:TPU:0, one launch (start us, length us, event | category | flops | bytes accessed | tf_op | source)
XLA Modules:
  0.0 96.0 jit_solution(8995009207553256438)
XLA Ops:
  0.0 1.7 %encode.1.after_ref = s16[64,8192]{1,0:T(8,128)(2,1)S(1)} custom-call(f32[5,64,8192]{2,1,0:T(8,128)} %phases_ref.1), custom_call_target="tpu_custom_call" | custom-call | flops 1000 | bytes 1000 | tf_op jit(solution)/shard_map/encode/pallas_call | solution.py:96
  1.8 1.7 %collective-permute-start.4 = (s16[64,8192]{1,0:T(8,128)(2,1)S(1)}, s16[64,8192]{1,0:T(8,128)(2,1)S(1)}, u32[]{:S(2)}, u32[]{:S(2)}) collective-permute-start(s16[64,8192]{1,0:T(8,128)(2,1)S(1)} %encode.1.after_ref), channel_id=1, source_target_pairs={{0,8},{8,0},{16,24},{24,16},{32,40},{40,32},{48,56},{56,48},{64,72... | collective-permute-start | bytes 3145736 | tf_op jit(solution)/shard_map/ppermute | solution.py:367
  3.4 3.1 %box_sums.1 = (bf16[64,16,128]{2,1,0:T(8,128)(2,1)S(1)}, bf16[64,16,128]{2,1,0:T(8,128)(2,1)S(1)}) custom-call(s32[1,128]{1,0:T(1,128)S(1)} %copy-done.2, s16[64,8192]{1,0:T(8,128)(2,1)S(1)} %encode.1.after_ref, s32[128,128]{1,0:T(8,128)} %bitcast.3, bf16[128,128,128]{2,1,0:T(8,128)(2,1)} %bitcast.2), custom_call_target="tpu_custom_call" | custom-call | flops 1000 | bytes 1000 | tf_op jit(solution)/shard_map/box_sums/pallas_call | solution.py:159
  6.6 1.5 %collective-permute-done.got_ref = bf16[64,16,128]{2,1,0:T(8,128)(2,1)S(1)} collective-permute-done((bf16[64,16,128]{2,1,0:T(8,128)(2,1)S(1)}, bf16[64,16,128]{2,1,0:T(8,128)(2,1)S(1)}, u32[]{:S(2)}, u32[]{:S(2)}) %collective-permute-start) | collective-permute-done | bytes 262176 | tf_op jit(solution)/shard_map/ppermute | solution.py:367
  8.2 16.7 %all_to_all.5.parts_ref = bf16[16,4,16,128]{3,2,1,0:T(8,128)(2,1)S(1)} all-to-all(bf16[16,4,16,128]{3,2,1,0:T(8,128)(2,1)S(1)} %deal.1), channel_id=1, replica_groups={{0,2,4,6,32,34,36,38,64,66,68,70,96,98,100,102},{1,3,5,7,33,35,37,39,65..., dimensions={0} | all-to-all | bytes 524288 | tf_op jit(solution)/shard_map/all_to_all | solution.py:380
  24.9 1.3 %collective-permute-start.1 = (f32[4,16,128]{2,1,0:T(8,128)S(1)}, f32[4,16,128]{2,1,0:T(8,128)S(1)}, u32[]{:S(2)}, u32[]{:S(2)}) collective-permute-start(f32[4,16,128]{2,1,0:T(8,128)S(1)} %add.1.after_ref.refs_0_), channel_id=1, source_target_pairs={{0,8},{8,0},{16,24},{24,16},{32,40},{40,32},{48,56},{56,48},{64,72... | collective-permute-start | bytes 98312 | tf_op jit(solution)/shard_map/ppermute | solution.py:367
  26.2 2.7 %collective-permute-start.2 = (f32[4,16,128]{2,1,0:T(8,128)S(1)}, f32[4,16,128]{2,1,0:T(8,128)S(1)}, u32[]{:S(2)}, u32[]{:S(2)}) collective-permute-start(f32[4,16,128]{2,1,0:T(8,128)S(1)} %add.1.after_ref.refs_0_), channel_id=1, source_target_pairs={{0,16},{8,24},{16,0},{24,8},{32,48},{40,56},{48,32},{56,40},{64,80... | collective-permute-start | bytes 98312 | tf_op jit(solution)/shard_map/ppermute | solution.py:367
  28.9 0.7 collective-permute-start.3
  29.7 0.6 slice.6.phases_ref
  30.6 0.7 copy-done
  31.6 2.4 %collective-permute-done.3.refs_3_ = f32[4,16,128]{2,1,0:T(8,128)S(1)} collective-permute-done((f32[4,16,128]{2,1,0:T(8,128)S(1)}, f32[4,16,128]{2,1,0:T(8,128)S(1)}, u32[]{:S(2)}, u32[]{:S(2)}) %collective-permute-start.3) | collective-permute-done | bytes 32800 | tf_op jit(solution)/shard_map/ppermute | solution.py:367
  34.2 0.9 a_0.1.rest_0_.state_ref
  35.2 0.9 a_2.1.rest_0_.state_ref
  36.1 0.6 collective-permute-start.8
  37.0 0.4 collective-permute-start.6
  37.4 1.7 %a_4.1.rest_0_.state_ref = bf16[128,2048]{1,0:T(8,128)(2,1)S(1)} custom-call(f32[16,128]{1,0:T(8,128)S(1)} %get-tuple-element.16.x_ref, f32[16,128]{1,0:T(8,128)S(1)} %get-tuple-element.17.other_x_ref, bf16[128,256]{1,0:T(8,128)(2,1)S(1)} %get-tuple-element.15.after_ref.mats_ref, f32[3,64,8192]{2,1,0:T(8,128)S(1)} %slice.6.phases_ref, ...), custom_call_target="tpu_custom_call" | custom-call | flops 10000000000 | bytes 1000 | tf_op jit(solution)/shard_map/a_4/pallas_call | solution.py:271
  39.2 0.3 b_2.1.rest_0_.state_ref
  39.5 3.3 %collective-permute-start.12 = (bf16[128,1024]{1,0:T(8,128)(2,1)S(1)}, bf16[128,1024]{1,0:T(8,128)(2,1)S(1)}, u32[]{:S(2)}, u32[]{:S(2)}) collective-permute-start(bf16[128,1024]{1,0:T(8,128)(2,1)S(1)} %b_2.1.rest_0_.state_ref), channel_id=1, source_target_pairs={{0,16},{8,24},{16,0},{24,8},{32,48},{40,56},{48,32},{56,40},{64,80... | collective-permute-start | bytes 786440 | tf_op jit(solution)/shard_map/ppermute | solution.py:367
  43.2 1.5 %collective-permute-start.10 = (bf16[128,1024]{1,0:T(8,128)(2,1)S(1)}, bf16[128,1024]{1,0:T(8,128)(2,1)S(1)}, u32[]{:S(2)}, u32[]{:S(2)}) collective-permute-start(bf16[128,1024]{1,0:T(8,128)(2,1)S(1)} %b_4.1.rest_0_.state_ref), channel_id=1, source_target_pairs={{0,16},{8,24},{16,0},{24,8},{32,48},{40,56},{48,32},{56,40},{64,80... | collective-permute-start | bytes 786440 | tf_op jit(solution)/shard_map/ppermute | solution.py:367
  44.7 3.0 %collective-permute-done.6.partner_ref = bf16[128,1024]{1,0:T(8,128)(2,1)S(1)} collective-permute-done((bf16[128,1024]{1,0:T(8,128)(2,1)S(1)}, bf16[128,1024]{1,0:T(8,128)(2,1)S(1)}, u32[]{:S(2)}, u32[]{:S(2)}) %collective-permute-start.6) | collective-permute-done | bytes 262176 | tf_op jit(solution)/shard_map/ppermute | solution.py:367
  48.1 0.5 collective-permute-start.9
  48.6 1.7 %a_8.1.rest_0_.state_ref = bf16[128,2048]{1,0:T(8,128)(2,1)S(1)} custom-call(f32[16,128]{1,0:T(8,128)S(1)} %get-tuple-element.16.x_ref, f32[16,128]{1,0:T(8,128)S(1)} %get-tuple-element.17.other_x_ref, bf16[128,256]{1,0:T(8,128)(2,1)S(1)} %get-tuple-element.15.after_ref.mats_ref, f32[3,64,8192]{2,1,0:T(8,128)S(1)} %slice.6.phases_ref, ...), custom_call_target="tpu_custom_call" | custom-call | flops 10000000000 | bytes 1000 | tf_op jit(solution)/shard_map/a_8/pallas_call | solution.py:271
  51.0 2.4 %collective-permute-done.12.partner_ref = bf16[128,1024]{1,0:T(8,128)(2,1)S(1)} collective-permute-done((bf16[128,1024]{1,0:T(8,128)(2,1)S(1)}, bf16[128,1024]{1,0:T(8,128)(2,1)S(1)}, u32[]{:S(2)}, u32[]{:S(2)}) %collective-permute-start.12) | collective-permute-done | bytes 262176 | tf_op jit(solution)/shard_map/ppermute | solution.py:367
  53.7 0.5 collective-permute-start.16
  54.3 0.3 b_8.1.rest_0_.state_ref
  54.6 2.4 %collective-permute-start.15 = (bf16[128,1024]{1,0:T(8,128)(2,1)S(1)}, bf16[128,1024]{1,0:T(8,128)(2,1)S(1)}, u32[]{:S(2)}, u32[]{:S(2)}) collective-permute-start(bf16[128,1024]{1,0:T(8,128)(2,1)S(1)} %b_8.1.rest_0_.state_ref), channel_id=1, source_target_pairs={{0,16},{8,24},{16,0},{24,8},{32,48},{40,56},{48,32},{56,40},{64,80... | collective-permute-start | bytes 786440 | tf_op jit(solution)/shard_map/ppermute | solution.py:367
  57.0 2.0 %collective-permute-done.10.partner_ref = bf16[128,1024]{1,0:T(8,128)(2,1)S(1)} collective-permute-done((bf16[128,1024]{1,0:T(8,128)(2,1)S(1)}, bf16[128,1024]{1,0:T(8,128)(2,1)S(1)}, u32[]{:S(2)}, u32[]{:S(2)}) %collective-permute-start.10) | collective-permute-done | bytes 262176 | tf_op jit(solution)/shard_map/ppermute | solution.py:367
  59.3 0.5 collective-permute-start.14
  60.2 1.7 %a_12.1.rest_0_.state_ref = bf16[128,2048]{1,0:T(8,128)(2,1)S(1)} custom-call(f32[16,128]{1,0:T(8,128)S(1)} %get-tuple-element.16.x_ref, f32[16,128]{1,0:T(8,128)S(1)} %get-tuple-element.17.other_x_ref, bf16[128,256]{1,0:T(8,128)(2,1)S(1)} %get-tuple-element.15.after_ref.mats_ref, f32[3,64,8192]{2,1,0:T(8,128)S(1)} %slice.6.phases_ref, ...), custom_call_target="tpu_custom_call" | custom-call | flops 10000000000 | bytes 1000 | tf_op jit(solution)/shard_map/a_12/pallas_call | solution.py:271
  62.0 0.3 b_10.1.rest_0_.state_ref
  62.3 2.3 %collective-permute-done.17.partner_ref = bf16[128,1024]{1,0:T(8,128)(2,1)S(1)} collective-permute-done((bf16[128,1024]{1,0:T(8,128)(2,1)S(1)}, bf16[128,1024]{1,0:T(8,128)(2,1)S(1)}, u32[]{:S(2)}, u32[]{:S(2)}) %collective-permute-start.17) | collective-permute-done | bytes 262176 | tf_op jit(solution)/shard_map/ppermute | solution.py:367
  65.0 0.5 collective-permute-start.21
  65.9 0.3 b_12.1.rest_0_.state_ref
  66.3 3.6 %collective-permute-start.20 = (bf16[128,1024]{1,0:T(8,128)(2,1)S(1)}, bf16[128,1024]{1,0:T(8,128)(2,1)S(1)}, u32[]{:S(2)}, u32[]{:S(2)}) collective-permute-start(bf16[128,1024]{1,0:T(8,128)(2,1)S(1)} %b_12.1.rest_0_.state_ref), channel_id=1, source_target_pairs={{0,16},{8,24},{16,0},{24,8},{32,48},{40,56},{48,32},{56,40},{64,80... | collective-permute-start | bytes 786440 | tf_op jit(solution)/shard_map/ppermute | solution.py:367
  69.8 0.4 collective-permute-done.15.partner_ref
  70.6 1.2 %collective-permute-start.19 = (bf16[128,1024]{1,0:T(8,128)(2,1)S(1)}, bf16[128,1024]{1,0:T(8,128)(2,1)S(1)}, u32[]{:S(2)}, u32[]{:S(2)}) collective-permute-start(bf16[128,1024]{1,0:T(8,128)(2,1)S(1)} %c_8.1.rest_0_.state_ref), channel_id=1, source_target_pairs={{0,2},{1,3},{2,0},{3,1},{4,6},{5,7},{6,4},{7,5},{8,10},{9,11},{10,... | collective-permute-start | bytes 786440 | tf_op jit(solution)/shard_map/ppermute | solution.py:367
  71.8 0.3 d_4.1.rest_0_.refs_2_
  72.6 3.2 %collective-permute-done.22.partner_ref = bf16[128,1024]{1,0:T(8,128)(2,1)S(1)} collective-permute-done((bf16[128,1024]{1,0:T(8,128)(2,1)S(1)}, bf16[128,1024]{1,0:T(8,128)(2,1)S(1)}, u32[]{:S(2)}, u32[]{:S(2)}) %collective-permute-start.22) | collective-permute-done | bytes 262176 | tf_op jit(solution)/shard_map/ppermute | solution.py:367
  76.2 0.5 collective-permute-start.24
  77.1 4.4 %collective-permute-done.20.partner_ref = bf16[128,1024]{1,0:T(8,128)(2,1)S(1)} collective-permute-done((bf16[128,1024]{1,0:T(8,128)(2,1)S(1)}, bf16[128,1024]{1,0:T(8,128)(2,1)S(1)}, u32[]{:S(2)}, u32[]{:S(2)}) %collective-permute-start.20) | collective-permute-done | bytes 262176 | tf_op jit(solution)/shard_map/ppermute | solution.py:367
  81.8 0.5 collective-permute-start.25
  82.4 0.3 d_8.1.rest_0_.refs_4_
  82.7 3.6 %collective-permute-done.18.partner_ref = bf16[128,1024]{1,0:T(8,128)(2,1)S(1)} collective-permute-done((bf16[128,1024]{1,0:T(8,128)(2,1)S(1)}, bf16[128,1024]{1,0:T(8,128)(2,1)S(1)}, u32[]{:S(2)}, u32[]{:S(2)}) %collective-permute-start.18) | collective-permute-done | bytes 262176 | tf_op jit(solution)/shard_map/ppermute | solution.py:367
  86.6 0.5 collective-permute-start.23
  87.5 2.2 %collective-permute-done.25.partner_ref = bf16[128,1024]{1,0:T(8,128)(2,1)S(1)} collective-permute-done((bf16[128,1024]{1,0:T(8,128)(2,1)S(1)}, bf16[128,1024]{1,0:T(8,128)(2,1)S(1)}, u32[]{:S(2)}, u32[]{:S(2)}) %collective-permute-start.25) | collective-permute-done | bytes 262176 | tf_op jit(solution)/shard_map/ppermute | solution.py:367
  90.1 1.3 %flush.1.before_ref = bf16[128,8192]{1,0:T(8,128)(2,1)} custom-call(bf16[128,1024]{1,0:T(8,128)(2,1)S(1)} %d_0.1.rest_0_.refs_0_, bf16[128,1024]{1,0:T(8,128)(2,1)S(1)} %d_2.1.rest_0_.refs_1_, bf16[128,1024]{1,0:T(8,128)(2,1)S(1)} %d_4.1.rest_0_.refs_2_, bf16[128,1024]{1,0:T(8,128)(2,1)S(1)} %d_6.1.rest_0_.refs_3_, ...), custom_call_target="tpu_custom_call" | custom-call | flops 10000000000 | bytes 1000 | tf_op jit(solution)/shard_map/flush/pallas_call | solution.py:326
  91.4 3.5 %collective-permute-done.23.partner_ref = bf16[128,1024]{1,0:T(8,128)(2,1)S(1)} collective-permute-done((bf16[128,1024]{1,0:T(8,128)(2,1)S(1)}, bf16[128,1024]{1,0:T(8,128)(2,1)S(1)}, u32[]{:S(2)}, u32[]{:S(2)}) %collective-permute-start.23) | collective-permute-done | bytes 262176 | tf_op jit(solution)/shard_map/ppermute | solution.py:367
  94.8 1.0 %last.1 = bf16[128,8192]{1,0:T(8,128)(2,1)} custom-call(bf16[128,1024]{1,0:T(8,128)(2,1)S(1)} %c_14.1.rest_0_.state_ref, bf16[128,1024]{1,0:T(8,128)(2,1)S(1)} %collective-permute-done.23.partner_ref, bf16[128,256]{1,0:T(8,128)(2,1)S(1)} %get-tuple-element.20.mats_ref, f32[2,64,8192]{2,1,0:T(8,128)S(1)} %slice.7.phases_ref, ...), custom_call_target="tpu_custom_call", output_to_operand_aliasing={{}: (4, {})} | custom-call | flops 10000000000 | bytes 1000 | tf_op jit(solution)/shard_map/last/pallas_call | solution.py:350
  (51 shorter events, 7.5 us)
Async XLA Ops:
  0.0 3.4 %copy-start.2 = (s32[1,128]{1,0:T(1,128)S(1)}, s32[1,128]{1,0:T(1,128)}, u32[]{:S(2)}) copy-start(s32[1,128]{1,0:T(1,128)} %counts_ref.1) | copy-start | bytes 1540
  0.0 29.7 %copy-start.3 = (f32[5,64,8192]{2,1,0:T(8,128)S(1)}, f32[5,64,8192]{2,1,0:T(8,128)}, u32[]{:S(2)}) copy-start(f32[5,64,8192]{2,1,0:T(8,128)} %phases_ref.1) | copy-start | bytes 31457284
  1.8 32.4 %collective-permute-start.4 = (s16[64,8192]{1,0:T(8,128)(2,1)S(1)}, s16[64,8192]{1,0:T(8,128)(2,1)S(1)}, u32[]{:S(2)}, u32[]{:S(2)}) collective-permute-start(s16[64,8192]{1,0:T(8,128)(2,1)S(1)} %encode.1.after_ref), channel_id=1, source_target_pairs={{0,8},{8,0},{16,24},{24,16},{32,40},{40,32},{48,56},{56,48},{64,72... | collective-permute-start | bytes 3145736 | tf_op jit(solution)/shard_map/ppermute | solution.py:367
  6.5 1.6 %collective-permute-start = (bf16[64,16,128]{2,1,0:T(8,128)(2,1)S(1)}, bf16[64,16,128]{2,1,0:T(8,128)(2,1)S(1)}, u32[]{:S(2)}, u32[]{:S(2)}) collective-permute-start(bf16[64,16,128]{2,1,0:T(8,128)(2,1)S(1)} %get-tuple-element.14), channel_id=1, source_target_pairs={{0,1},{1,0},{2,3},{3,2},{4,5},{5,4},{6,7},{7,6},{8,9},{9,8},{10,11... | collective-permute-start | bytes 786440 | tf_op jit(solution)/shard_map/ppermute | solution.py:367
  24.9 6.6 %collective-permute-start.1 = (f32[4,16,128]{2,1,0:T(8,128)S(1)}, f32[4,16,128]{2,1,0:T(8,128)S(1)}, u32[]{:S(2)}, u32[]{:S(2)}) collective-permute-start(f32[4,16,128]{2,1,0:T(8,128)S(1)} %add.1.after_ref.refs_0_), channel_id=1, source_target_pairs={{0,8},{8,0},{16,24},{24,16},{32,40},{40,32},{48,56},{56,48},{64,72... | collective-permute-start | bytes 98312 | tf_op jit(solution)/shard_map/ppermute | solution.py:367
  26.2 5.4 %collective-permute-start.2 = (f32[4,16,128]{2,1,0:T(8,128)S(1)}, f32[4,16,128]{2,1,0:T(8,128)S(1)}, u32[]{:S(2)}, u32[]{:S(2)}) collective-permute-start(f32[4,16,128]{2,1,0:T(8,128)S(1)} %add.1.after_ref.refs_0_), channel_id=1, source_target_pairs={{0,16},{8,24},{16,0},{24,8},{32,48},{40,56},{48,32},{56,40},{64,80... | collective-permute-start | bytes 98312 | tf_op jit(solution)/shard_map/ppermute | solution.py:367
  28.9 5.1 %collective-permute-start.3 = (f32[4,16,128]{2,1,0:T(8,128)S(1)}, f32[4,16,128]{2,1,0:T(8,128)S(1)}, u32[]{:S(2)}, u32[]{:S(2)}) collective-permute-start(f32[4,16,128]{2,1,0:T(8,128)S(1)} %add.1.after_ref.refs_0_), channel_id=1, source_target_pairs={{0,24},{8,16},{16,8},{24,0},{32,56},{40,48},{48,40},{56,32},{64,88... | collective-permute-start | bytes 98312 | tf_op jit(solution)/shard_map/ppermute | solution.py:367
  30.3 1.0 %copy-start = (bf16[4,2,2,128,128]{4,3,2,1,0:T(8,128)(2,1)S(1)}, bf16[4,2,2,128,128]{4,3,2,1,0:T(8,128)(2,1)}, u32[]{:S(2)}) copy-start(bf16[4,2,2,128,128]{4,3,2,1,0:T(8,128)(2,1)} %trans_ref.1) | copy-start | bytes 1572868
  30.3 3.8 %copy-start.1 = (bf16[128,128]{1,0:T(8,128)(2,1)S(1)}, bf16[128,128]{1,0:T(8,128)(2,1)}, u32[]{:S(2)}) copy-start(bf16[128,128]{1,0:T(8,128)(2,1)} %map_ref.1) | copy-start | bytes 98308
  35.1 1.6 %collective-permute-start.5 = (bf16[128,1024]{1,0:T(8,128)(2,1)S(1)}, bf16[128,1024]{1,0:T(8,128)(2,1)S(1)}, u32[]{:S(2)}, u32[]{:S(2)}) collective-permute-start(bf16[128,1024]{1,0:T(8,128)(2,1)S(1)} %a_0.1.rest_0_.state_ref), channel_id=1, source_target_pairs={{0,1},{1,0},{2,3},{3,2},{4,5},{5,4},{6,7},{7,6},{8,9},{9,8},{10,11... | collective-permute-start | bytes 786440 | tf_op jit(solution)/shard_map/ppermute | solution.py:367
  36.1 3.1 %collective-permute-start.8 = (bf16[128,1024]{1,0:T(8,128)(2,1)S(1)}, bf16[128,1024]{1,0:T(8,128)(2,1)S(1)}, u32[]{:S(2)}, u32[]{:S(2)}) collective-permute-start(bf16[128,1024]{1,0:T(8,128)(2,1)S(1)} %a_2.1.rest_0_.state_ref), channel_id=1, source_target_pairs={{0,1},{1,0},{2,3},{3,2},{4,5},{5,4},{6,7},{7,6},{8,9},{9,8},{10,11... | collective-permute-start | bytes 786440 | tf_op jit(solution)/shard_map/ppermute | solution.py:367
  37.0 10.7 %collective-permute-start.6 = (bf16[128,1024]{1,0:T(8,128)(2,1)S(1)}, bf16[128,1024]{1,0:T(8,128)(2,1)S(1)}, u32[]{:S(2)}, u32[]{:S(2)}) collective-permute-start(bf16[128,1024]{1,0:T(8,128)(2,1)S(1)} %b_0.1.rest_0_.state_ref), channel_id=1, source_target_pairs={{0,16},{8,24},{16,0},{24,8},{32,48},{40,56},{48,32},{56,40},{64,80... | collective-permute-start | bytes 786440 | tf_op jit(solution)/shard_map/ppermute | solution.py:367
  39.1 3.8 %collective-permute-start.7 = (bf16[128,2048]{1,0:T(8,128)(2,1)S(1)}, bf16[128,2048]{1,0:T(8,128)(2,1)S(1)}, u32[]{:S(2)}, u32[]{:S(2)}) collective-permute-start(bf16[128,2048]{1,0:T(8,128)(2,1)S(1)} %a_4.1.rest_0_.state_ref), channel_id=1, source_target_pairs={{0,1},{1,0},{2,3},{3,2},{4,5},{5,4},{6,7},{7,6},{8,9},{9,8},{10,11... | collective-permute-start | bytes 1572872 | tf_op jit(solution)/shard_map/ppermute | solution.py:367
  39.5 13.9 %collective-permute-start.12 = (bf16[128,1024]{1,0:T(8,128)(2,1)S(1)}, bf16[128,1024]{1,0:T(8,128)(2,1)S(1)}, u32[]{:S(2)}, u32[]{:S(2)}) collective-permute-start(bf16[128,1024]{1,0:T(8,128)(2,1)S(1)} %b_2.1.rest_0_.state_ref), channel_id=1, source_target_pairs={{0,16},{8,24},{16,0},{24,8},{32,48},{40,56},{48,32},{56,40},{64,80... | collective-permute-start | bytes 786440 | tf_op jit(solution)/shard_map/ppermute | solution.py:367
  43.2 15.8 %collective-permute-start.10 = (bf16[128,1024]{1,0:T(8,128)(2,1)S(1)}, bf16[128,1024]{1,0:T(8,128)(2,1)S(1)}, u32[]{:S(2)}, u32[]{:S(2)}) collective-permute-start(bf16[128,1024]{1,0:T(8,128)(2,1)S(1)} %b_4.1.rest_0_.state_ref), channel_id=1, source_target_pairs={{0,16},{8,24},{16,0},{24,8},{32,48},{40,56},{48,32},{56,40},{64,80... | collective-permute-start | bytes 786440 | tf_op jit(solution)/shard_map/ppermute | solution.py:367
  48.1 11.8 %collective-permute-start.9 = (bf16[128,1024]{1,0:T(8,128)(2,1)S(1)}, bf16[128,1024]{1,0:T(8,128)(2,1)S(1)}, u32[]{:S(2)}, u32[]{:S(2)}) collective-permute-start(bf16[128,1024]{1,0:T(8,128)(2,1)S(1)} %c_0.1.rest_0_.state_ref), channel_id=1, source_target_pairs={{0,2},{1,3},{2,0},{3,1},{4,6},{5,7},{6,4},{7,5},{8,10},{9,11},{10,... | collective-permute-start | bytes 786440 | tf_op jit(solution)/shard_map/ppermute | solution.py:367
  50.3 3.9 %collective-permute-start.11 = (bf16[128,2048]{1,0:T(8,128)(2,1)S(1)}, bf16[128,2048]{1,0:T(8,128)(2,1)S(1)}, u32[]{:S(2)}, u32[]{:S(2)}) collective-permute-start(bf16[128,2048]{1,0:T(8,128)(2,1)S(1)} %a_8.1.rest_0_.state_ref), channel_id=1, source_target_pairs={{0,1},{1,0},{2,3},{3,2},{4,5},{5,4},{6,7},{7,6},{8,9},{9,8},{10,11... | collective-permute-start | bytes 1572872 | tf_op jit(solution)/shard_map/ppermute | solution.py:367
  50.9 13.7 %collective-permute-start.17 = (bf16[128,1024]{1,0:T(8,128)(2,1)S(1)}, bf16[128,1024]{1,0:T(8,128)(2,1)S(1)}, u32[]{:S(2)}, u32[]{:S(2)}) collective-permute-start(bf16[128,1024]{1,0:T(8,128)(2,1)S(1)} %b_6.1.rest_0_.state_ref), channel_id=1, source_target_pairs={{0,16},{8,24},{16,0},{24,8},{32,48},{40,56},{48,32},{56,40},{64,80... | collective-permute-start | bytes 786440 | tf_op jit(solution)/shard_map/ppermute | solution.py:367
  53.7 11.3 %collective-permute-start.16 = (bf16[128,1024]{1,0:T(8,128)(2,1)S(1)}, bf16[128,1024]{1,0:T(8,128)(2,1)S(1)}, u32[]{:S(2)}, u32[]{:S(2)}) collective-permute-start(bf16[128,1024]{1,0:T(8,128)(2,1)S(1)} %c_2.1.rest_0_.state_ref), channel_id=1, source_target_pairs={{0,2},{1,3},{2,0},{3,1},{4,6},{5,7},{6,4},{7,5},{8,10},{9,11},{10,... | collective-permute-start | bytes 786440 | tf_op jit(solution)/shard_map/ppermute | solution.py:367
  54.6 15.6 %collective-permute-start.15 = (bf16[128,1024]{1,0:T(8,128)(2,1)S(1)}, bf16[128,1024]{1,0:T(8,128)(2,1)S(1)}, u32[]{:S(2)}, u32[]{:S(2)}) collective-permute-start(bf16[128,1024]{1,0:T(8,128)(2,1)S(1)} %b_8.1.rest_0_.state_ref), channel_id=1, source_target_pairs={{0,16},{8,24},{16,0},{24,8},{32,48},{40,56},{48,32},{56,40},{64,80... | collective-permute-start | bytes 786440 | tf_op jit(solution)/shard_map/ppermute | solution.py:367
  59.3 12.5 %collective-permute-start.14 = (bf16[128,1024]{1,0:T(8,128)(2,1)S(1)}, bf16[128,1024]{1,0:T(8,128)(2,1)S(1)}, u32[]{:S(2)}, u32[]{:S(2)}) collective-permute-start(bf16[128,1024]{1,0:T(8,128)(2,1)S(1)} %c_4.1.rest_0_.state_ref), channel_id=1, source_target_pairs={{0,2},{1,3},{2,0},{3,1},{4,6},{5,7},{6,4},{7,5},{8,10},{9,11},{10,... | collective-permute-start | bytes 786440 | tf_op jit(solution)/shard_map/ppermute | solution.py:367
  61.9 4.0 %collective-permute-start.13 = (bf16[128,2048]{1,0:T(8,128)(2,1)S(1)}, bf16[128,2048]{1,0:T(8,128)(2,1)S(1)}, u32[]{:S(2)}, u32[]{:S(2)}) collective-permute-start(bf16[128,2048]{1,0:T(8,128)(2,1)S(1)} %a_12.1.rest_0_.state_ref), channel_id=1, source_target_pairs={{0,1},{1,0},{2,3},{3,2},{4,5},{5,4},{6,7},{7,6},{8,9},{9,8},{10,11... | collective-permute-start | bytes 1572872 | tf_op jit(solution)/shard_map/ppermute | solution.py:367
  64.6 11.2 %collective-permute-start.22 = (bf16[128,1024]{1,0:T(8,128)(2,1)S(1)}, bf16[128,1024]{1,0:T(8,128)(2,1)S(1)}, u32[]{:S(2)}, u32[]{:S(2)}) collective-permute-start(bf16[128,1024]{1,0:T(8,128)(2,1)S(1)} %b_10.1.rest_0_.state_ref), channel_id=1, source_target_pairs={{0,16},{8,24},{16,0},{24,8},{32,48},{40,56},{48,32},{56,40},{64,80... | collective-permute-start | bytes 786440 | tf_op jit(solution)/shard_map/ppermute | solution.py:367
  65.0 11.7 %collective-permute-start.21 = (bf16[128,1024]{1,0:T(8,128)(2,1)S(1)}, bf16[128,1024]{1,0:T(8,128)(2,1)S(1)}, u32[]{:S(2)}, u32[]{:S(2)}) collective-permute-start(bf16[128,1024]{1,0:T(8,128)(2,1)S(1)} %c_6.1.rest_0_.state_ref), channel_id=1, source_target_pairs={{0,2},{1,3},{2,0},{3,1},{4,6},{5,7},{6,4},{7,5},{8,10},{9,11},{10,... | collective-permute-start | bytes 786440 | tf_op jit(solution)/shard_map/ppermute | solution.py:367
  66.3 15.2 %collective-permute-start.20 = (bf16[128,1024]{1,0:T(8,128)(2,1)S(1)}, bf16[128,1024]{1,0:T(8,128)(2,1)S(1)}, u32[]{:S(2)}, u32[]{:S(2)}) collective-permute-start(bf16[128,1024]{1,0:T(8,128)(2,1)S(1)} %b_12.1.rest_0_.state_ref), channel_id=1, source_target_pairs={{0,16},{8,24},{16,0},{24,8},{32,48},{40,56},{48,32},{56,40},{64,80... | collective-permute-start | bytes 786440 | tf_op jit(solution)/shard_map/ppermute | solution.py:367
  70.6 11.8 %collective-permute-start.19 = (bf16[128,1024]{1,0:T(8,128)(2,1)S(1)}, bf16[128,1024]{1,0:T(8,128)(2,1)S(1)}, u32[]{:S(2)}, u32[]{:S(2)}) collective-permute-start(bf16[128,1024]{1,0:T(8,128)(2,1)S(1)} %c_8.1.rest_0_.state_ref), channel_id=1, source_target_pairs={{0,2},{1,3},{2,0},{3,1},{4,6},{5,7},{6,4},{7,5},{8,10},{9,11},{10,... | collective-permute-start | bytes 786440 | tf_op jit(solution)/shard_map/ppermute | solution.py:367
  72.5 13.8 %collective-permute-start.18 = (bf16[128,1024]{1,0:T(8,128)(2,1)S(1)}, bf16[128,1024]{1,0:T(8,128)(2,1)S(1)}, u32[]{:S(2)}, u32[]{:S(2)}) collective-permute-start(bf16[128,1024]{1,0:T(8,128)(2,1)S(1)} %b_14.1.rest_0_.state_ref), channel_id=1, source_target_pairs={{0,16},{8,24},{16,0},{24,8},{32,48},{40,56},{48,32},{56,40},{64,80... | collective-permute-start | bytes 786440 | tf_op jit(solution)/shard_map/ppermute | solution.py:367
  76.2 11.0 %collective-permute-start.24 = (bf16[128,1024]{1,0:T(8,128)(2,1)S(1)}, bf16[128,1024]{1,0:T(8,128)(2,1)S(1)}, u32[]{:S(2)}, u32[]{:S(2)}) collective-permute-start(bf16[128,1024]{1,0:T(8,128)(2,1)S(1)} %c_10.1.rest_0_.state_ref), channel_id=1, source_target_pairs={{0,2},{1,3},{2,0},{3,1},{4,6},{5,7},{6,4},{7,5},{8,10},{9,11},{10,... | collective-permute-start | bytes 786440 | tf_op jit(solution)/shard_map/ppermute | solution.py:367
  81.8 7.9 %collective-permute-start.25 = (bf16[128,1024]{1,0:T(8,128)(2,1)S(1)}, bf16[128,1024]{1,0:T(8,128)(2,1)S(1)}, u32[]{:S(2)}, u32[]{:S(2)}) collective-permute-start(bf16[128,1024]{1,0:T(8,128)(2,1)S(1)} %c_12.1.rest_0_.state_ref), channel_id=1, source_target_pairs={{0,2},{1,3},{2,0},{3,1},{4,6},{5,7},{6,4},{7,5},{8,10},{9,11},{10,... | collective-permute-start | bytes 786440 | tf_op jit(solution)/shard_map/ppermute | solution.py:367
  86.6 8.2 %collective-permute-start.23 = (bf16[128,1024]{1,0:T(8,128)(2,1)S(1)}, bf16[128,1024]{1,0:T(8,128)(2,1)S(1)}, u32[]{:S(2)}, u32[]{:S(2)}) collective-permute-start(bf16[128,1024]{1,0:T(8,128)(2,1)S(1)} %c_14.1.rest_0_.state_ref), channel_id=1, source_target_pairs={{0,2},{1,3},{2,0},{3,1},{4,6},{5,7},{6,4},{7,5},{8,10},{9,11},{10,... | collective-permute-start | bytes 786440 | tf_op jit(solution)/shard_map/ppermute | solution.py:367

commit v6 on v5

--- a/solution.py
+++ b/solution.py
@@ -13,9 +13,14 @@
 WIDTH = 128
 ROWS = BOXES * DIRS
 LEVELS = 4
-PARTS = (2, 2, 2, 2, 2, 2, 2, 2)
-GROUPS = (1, 1, 2, 2, 2)
-ORDER = "a0 a1 b0 a2 b1 b2 f c0 a3 b3 c1 b4 c2 d0 a4 b5 c3 d1 b6 c4 d2 b7 c5 d3 c6 d4 c7 d5 d6 d7"
+PARTS = (2, 2, 2, 2, 2, 2, 2, 1, 1)
+GROUPS = (1, 1, 2, 2, 3)
+ORDER = (
+    "a0", "a1", "b0", "a2", "b1", "b2", "c0", "a3", "b3",
+    "c1", "b4", "c2", "d0", "a4", "b5", "c3", "d1", "b6",
+    "c4", "d2", "b7", "c5", "b8", "d3", "c6", "d4", "c7",
+    "d5", "c8", "d6", "d7", "d8",
+)
 SPAN = 1024
 FETCHES = 4
 ALONG = 4
@@ -102,27 +107,6 @@
         compiler_params=limit(8),
         name="encode",
     )(far(phases))
-
-
-def fetch_kernel(first, after_ref, phases_ref, out_ref, sems):
-    copies = []
-    for k in range(out_ref.shape[0]):
-        copies.append(pltpu.make_async_copy(phases_ref.at[first + k], out_ref.at[k], sems.at[k]))
-        copies[-1].start()
-    for copy in copies:
-        copy.wait()
-
-
-def fetch(first, count, after, phases):
-    return kernel_call(
-        functools.partial(fetch_kernel, first),
-        in_specs=[ANY, ANY],
-        out_specs=VMEM,
-        out_shape=pltpu.VMEM((count, HALF, ROWS), jnp.float32),
-        scratch_shapes=[pltpu.SemaphoreType.DMA((count,))],
-        compiler_params=limit(2),
-        name="fetch",
-    )(near(after), far(phases))
 
 
 def box_sums_kernel(counts_ref, after_ref, tag_hbm_ref, rows_ref, keep_ref, send_ref, tag_ref, held, sems):
@@ -359,7 +343,7 @@
         ],
         compiler_params=limit(8),
         flops=FLOPS,
-        name="last",
+        name="last_%d" % start,
     )(near(state), near(partner), near(mats), near(phases), far(before))
 
 
@@ -381,42 +365,41 @@
         deal(keep, got), ("bx", "by"), split_axis=0, concat_axis=0, tiled=True, axis_index_groups=plane
     )
     row = add(parts)
-    early = phases[0:3]
     mats = pick_mats(row, trans)
     mine, theirs = expand(mats[0], source_map, [row] + [move(row, "bx", k) for k in (1, 2, 3)])
 
     starts = [sum(PARTS[:i]) for i in range(len(PARTS))]
     groups = [range(sum(GROUPS[:g]), sum(GROUPS[: g + 1])) for g in range(len(GROUPS))]
-    final = len(PARTS) - 1
+    flushed = len(PARTS) - 2
     firsts, states, partners, out = {}, {}, {}, None
     after = []
-    for name in ORDER.split():
-        if name == "f":
-            late = phases[3:5]
-            continue
+    for name in ORDER:
         level, i = name[0], int(name[1:])
         if level == "a":
             start, boxes = starts[groups[i][0]], sum(PARTS[p] for p in groups[i])
-            done = first_level(start, boxes, mine, theirs, mats[0], early, others, after)
+            done = first_level(start, boxes, mine, theirs, mats[0], phases, others, after)
             swapped = move(done, "by", 1)
             for p in groups[i]:
                 firsts[p] = (start, done, swapped)
         elif level == "b":
             skip, value, other = firsts[i]
-            done = next_level(level, starts[i], PARTS[i], skip, 2, value, other, mats[1], early, after)
+            done = next_level(level, starts[i], PARTS[i], skip, 2, value, other, mats[1], phases, after)
             states[i], partners[i] = done, move(done, "bx", 2)
         elif level == "c":
-            ends = (starts[i], PARTS[i], starts[i], 0)
-            done = next_level(level, *ends, states[i], partners[i], mats[2], late, after)
+            ends = (starts[i], PARTS[i], starts[i], 3)
+            done = next_level(level, *ends, states[i], partners[i], mats[2], phases, after)
             states[i], partners[i] = done, move(done, "by", 2)
-        elif i < final:
-            ends = (starts[i], PARTS[i], starts[i], 1)
-            done = next_level(level, *ends, states[i], partners[i], mats[3], late, after)
+        elif i < flushed:
+            ends = (starts[i], PARTS[i], starts[i], 4)
+            done = next_level(level, *ends, states[i], partners[i], mats[3], phases, after)
             states[i] = done
         else:
-            out = flush([states[p] for p in range(final)])
-            return last_level(starts[i], PARTS[i], 1, states[i], partners[i], mats[3], late, out)
+            if out is None:
+                out = flush([states[p] for p in range(flushed)])
+            out = last_level(starts[i], PARTS[i], 4, states[i], partners[i], mats[3], phases, out)
+            continue
         after = [done]
+    return out
 
 
 def solution(mesh):

time: 96.2 us -> 95.8 us (level)
  local copies, waits for them, and re-layouts: 1.64 us -> 0.04 us
  starting transfers between devices: 24 us -> 25.3 us
  waiting for transfers between devices: 31.3 us -> 30.1 us
  Pallas kernels: 21.9 us -> 22.9 us
    ppermute x26 -> x28, starting transfers between devices: 24 us -> 25.3 us  [move(): lax.ppermute(value, axis, [(s, s ^ mask) for s in range(lax.axis_size(axi...]
    ppermute x26 -> x28, waiting for transfers between devices: 31.3 us -> 30.1 us  [move(): lax.ppermute(value, axis, [(s, s ^ mask) for s in range(lax.axis_size(axi...]
    pallas_call x23 -> x25, Pallas kernels: 7.66 us -> 7.82 us  [next_level(): kernel_call(functools.partial(level_kernel, start, boxes, skip, slot), in...]
  transfers between devices with their start and end apart: 26 -> 28, of which waited for: 14 -> 16; matrix products, arithmetic and copies ran while one was open for 1% -> 0% of each run, Pallas kernels for 19% -> 20%
where the time goes in v6:
time: 95.8 us; the launch traced here: 95.6 us
  waiting for transfers between devices  30.1 us (31%)
  starting transfers between devices  25.3 us (26%)
  Pallas kernels  22.9 us (24%)
  blocking collectives  16.7 us (17%)
    ppermute x28, waiting for transfers between devices, move(): lax.ppermute(value, axis, [(s, s ^ mask) for s in range(lax.axis_size(axi...  30.1 us
    ppermute x28, starting transfers between devices, move(): lax.ppermute(value, axis, [(s, s ^ mask) for s in range(lax.axis_size(axi...  25.3 us
    all_to_all x1, blocking collectives, per_device(): lax.all_to_all(deal(keep, got), ('bx', 'by'), split_axis=0, concat_axis=0...  16.7 us
    pallas_call x25, Pallas kernels, next_level(): kernel_call(functools.partial(level_kernel, start, boxes, skip, slot), in...  7.82 us
    pallas_call x5, Pallas kernels, first_level(): kernel_call(functools.partial(first_kernel, start, boxes), in_specs=[VMEM...  6.73 us
    pallas_call x1, Pallas kernels, box_sums(): kernel_call(box_sums_kernel, in_specs=[SMEM, ANY, ANY, ANY], out_specs=[V...  3.23 us
  transfers between devices with their start and end apart: 28, of which 16 were waited for; matrix products, arithmetic and copies ran while one was open for 0% of the time, Pallas kernels for 20%

profile of v6, /device:TPU:0, one launch (start us, length us, event | category | flops | bytes accessed | tf_op | source)
XLA Modules:
  0.0 95.6 jit_solution(81684467235041422)
XLA Ops:
  0.0 1.7 %encode.1.after_ref = s16[64,8192]{1,0:T(8,128)(2,1)S(1)} custom-call(f32[5,64,8192]{2,1,0:T(8,128)} %phases_ref.65), custom_call_target="tpu_custom_call" | custom-call | flops 1000 | bytes 1000 | tf_op jit(solution)/shard_map/encode/pallas_call | solution.py:101
  1.8 1.7 %collective-permute-start.4 = (s16[64,8192]{1,0:T(8,128)(2,1)S(1)}, s16[64,8192]{1,0:T(8,128)(2,1)S(1)}, u32[]{:S(2)}, u32[]{:S(2)}) collective-permute-start(s16[64,8192]{1,0:T(8,128)(2,1)S(1)} %encode.1.after_ref), channel_id=1, source_target_pairs={{0,8},{8,0},{16,24},{24,16},{32,40},{40,32},{48,56},{56,48},{64,72... | collective-permute-start | bytes 3145736 | tf_op jit(solution)/shard_map/ppermute | solution.py:351
  3.4 3.2 %box_sums.1 = (bf16[64,16,128]{2,1,0:T(8,128)(2,1)S(1)}, bf16[64,16,128]{2,1,0:T(8,128)(2,1)S(1)}) custom-call(s32[1,128]{1,0:T(1,128)S(1)} %copy-done.2, s16[64,8192]{1,0:T(8,128)(2,1)S(1)} %encode.1.after_ref, s32[128,128]{1,0:T(8,128)} %bitcast.5, bf16[128,128,128]{2,1,0:T(8,128)(2,1)} %bitcast.4), custom_call_target="tpu_custom_call" | custom-call | flops 1000 | bytes 1000 | tf_op jit(solution)/shard_map/box_sums/pallas_call | solution.py:143
  6.8 1.5 %collective-permute-done.got_ref = bf16[64,16,128]{2,1,0:T(8,128)(2,1)S(1)} collective-permute-done((bf16[64,16,128]{2,1,0:T(8,128)(2,1)S(1)}, bf16[64,16,128]{2,1,0:T(8,128)(2,1)S(1)}, u32[]{:S(2)}, u32[]{:S(2)}) %collective-permute-start) | collective-permute-done | bytes 262176 | tf_op jit(solution)/shard_map/ppermute | solution.py:351
  8.4 16.7 %all_to_all.5.parts_ref = bf16[16,4,16,128]{3,2,1,0:T(8,128)(2,1)S(1)} all-to-all(bf16[16,4,16,128]{3,2,1,0:T(8,128)(2,1)S(1)} %deal.1), channel_id=1, replica_groups={{0,2,4,6,32,34,36,38,64,66,68,70,96,98,100,102},{1,3,5,7,33,35,37,39,65..., dimensions={0} | all-to-all | bytes 524288 | tf_op jit(solution)/shard_map/all_to_all | solution.py:364
  25.1 1.1 %collective-permute-start.1 = (f32[4,16,128]{2,1,0:T(8,128)S(1)}, f32[4,16,128]{2,1,0:T(8,128)S(1)}, u32[]{:S(2)}, u32[]{:S(2)}) collective-permute-start(f32[4,16,128]{2,1,0:T(8,128)S(1)} %add.1.after_ref.refs_0_), channel_id=1, source_target_pairs={{0,8},{8,0},{16,24},{24,16},{32,40},{40,32},{48,56},{56,48},{64,72... | collective-permute-start | bytes 98312 | tf_op jit(solution)/shard_map/ppermute | solution.py:351
  26.1 2.6 %collective-permute-start.2 = (f32[4,16,128]{2,1,0:T(8,128)S(1)}, f32[4,16,128]{2,1,0:T(8,128)S(1)}, u32[]{:S(2)}, u32[]{:S(2)}) collective-permute-start(f32[4,16,128]{2,1,0:T(8,128)S(1)} %add.1.after_ref.refs_0_), channel_id=1, source_target_pairs={{0,16},{8,24},{16,0},{24,8},{32,48},{40,56},{48,32},{56,40},{64,80... | collective-permute-start | bytes 98312 | tf_op jit(solution)/shard_map/ppermute | solution.py:351
  28.7 1.2 %collective-permute-start.3 = (f32[4,16,128]{2,1,0:T(8,128)S(1)}, f32[4,16,128]{2,1,0:T(8,128)S(1)}, u32[]{:S(2)}, u32[]{:S(2)}) collective-permute-start(f32[4,16,128]{2,1,0:T(8,128)S(1)} %add.1.after_ref.refs_0_), channel_id=1, source_target_pairs={{0,24},{8,16},{16,8},{24,0},{32,56},{40,48},{48,40},{56,32},{64,88... | collective-permute-start | bytes 98312 | tf_op jit(solution)/shard_map/ppermute | solution.py:351
  30.0 1.6 %collective-permute-done.2.refs_2_ = f32[4,16,128]{2,1,0:T(8,128)S(1)} collective-permute-done((f32[4,16,128]{2,1,0:T(8,128)S(1)}, f32[4,16,128]{2,1,0:T(8,128)S(1)}, u32[]{:S(2)}, u32[]{:S(2)}) %collective-permute-start.2) | collective-permute-done | bytes 32800 | tf_op jit(solution)/shard_map/ppermute | solution.py:351
  31.5 2.3 %collective-permute-done.3.refs_3_ = f32[4,16,128]{2,1,0:T(8,128)S(1)} collective-permute-done((f32[4,16,128]{2,1,0:T(8,128)S(1)}, f32[4,16,128]{2,1,0:T(8,128)S(1)}, u32[]{:S(2)}, u32[]{:S(2)}) %collective-permute-start.3) | collective-permute-done | bytes 32800 | tf_op jit(solution)/shard_map/ppermute | solution.py:351
  34.0 0.9 a_0.1.rest_0_.state_ref
  35.0 0.9 a_2.1.rest_0_.state_ref
  35.8 0.6 collective-permute-start.8
  36.8 0.4 collective-permute-start.6
  37.2 1.7 %a_4.1.rest_0_.state_ref = bf16[128,2048]{1,0:T(8,128)(2,1)S(1)} custom-call(f32[16,128]{1,0:T(8,128)S(1)} %get-tuple-element.16.x_ref, f32[16,128]{1,0:T(8,128)S(1)} %get-tuple-element.17.other_x_ref, bf16[128,256]{1,0:T(8,128)(2,1)S(1)} %get-tuple-element.15.after_ref.mats_ref, f32[5,64,8192]{2,1,0:T(8,128)S(1)} %bitcast.3, ...), custom_call_target="tpu_custom_call" | custom-call | flops 10000000000 | bytes 1000 | tf_op jit(solution)/shard_map/a_4/pallas_call | solution.py:255
  39.3 3.3 %collective-permute-start.12 = (bf16[128,1024]{1,0:T(8,128)(2,1)S(1)}, bf16[128,1024]{1,0:T(8,128)(2,1)S(1)}, u32[]{:S(2)}, u32[]{:S(2)}) collective-permute-start(bf16[128,1024]{1,0:T(8,128)(2,1)S(1)} %b_2.1.rest_0_.state_ref), channel_id=1, source_target_pairs={{0,16},{8,24},{16,0},{24,8},{32,48},{40,56},{48,32},{56,40},{64,80... | collective-permute-start | bytes 786440 | tf_op jit(solution)/shard_map/ppermute | solution.py:351
  43.0 1.5 %collective-permute-start.10 = (bf16[128,1024]{1,0:T(8,128)(2,1)S(1)}, bf16[128,1024]{1,0:T(8,128)(2,1)S(1)}, u32[]{:S(2)}, u32[]{:S(2)}) collective-permute-start(bf16[128,1024]{1,0:T(8,128)(2,1)S(1)} %b_4.1.rest_0_.state_ref), channel_id=1, source_target_pairs={{0,16},{8,24},{16,0},{24,8},{32,48},{40,56},{48,32},{56,40},{64,80... | collective-permute-start | bytes 786440 | tf_op jit(solution)/shard_map/ppermute | solution.py:351
  44.5 3.1 %collective-permute-done.6.partner_ref = bf16[128,1024]{1,0:T(8,128)(2,1)S(1)} collective-permute-done((bf16[128,1024]{1,0:T(8,128)(2,1)S(1)}, bf16[128,1024]{1,0:T(8,128)(2,1)S(1)}, u32[]{:S(2)}, u32[]{:S(2)}) %collective-permute-start.6) | collective-permute-done | bytes 262176 | tf_op jit(solution)/shard_map/ppermute | solution.py:351
  47.9 0.5 collective-permute-start.9
  48.4 1.7 %a_8.1.rest_0_.state_ref = bf16[128,2048]{1,0:T(8,128)(2,1)S(1)} custom-call(f32[16,128]{1,0:T(8,128)S(1)} %get-tuple-element.16.x_ref, f32[16,128]{1,0:T(8,128)S(1)} %get-tuple-element.17.other_x_ref, bf16[128,256]{1,0:T(8,128)(2,1)S(1)} %get-tuple-element.15.after_ref.mats_ref, f32[5,64,8192]{2,1,0:T(8,128)S(1)} %bitcast.3, ...), custom_call_target="tpu_custom_call" | custom-call | flops 10000000000 | bytes 1000 | tf_op jit(solution)/shard_map/a_8/pallas_call | solution.py:255
  50.8 2.4 %collective-permute-done.12.partner_ref = bf16[128,1024]{1,0:T(8,128)(2,1)S(1)} collective-permute-done((bf16[128,1024]{1,0:T(8,128)(2,1)S(1)}, bf16[128,1024]{1,0:T(8,128)(2,1)S(1)}, u32[]{:S(2)}, u32[]{:S(2)}) %collective-permute-start.12) | collective-permute-done | bytes 262176 | tf_op jit(solution)/shard_map/ppermute | solution.py:351
  53.5 0.5 collective-permute-start.17
  54.4 2.4 %collective-permute-start.16 = (bf16[128,1024]{1,0:T(8,128)(2,1)S(1)}, bf16[128,1024]{1,0:T(8,128)(2,1)S(1)}, u32[]{:S(2)}, u32[]{:S(2)}) collective-permute-start(bf16[128,1024]{1,0:T(8,128)(2,1)S(1)} %b_8.1.rest_0_.state_ref), channel_id=1, source_target_pairs={{0,16},{8,24},{16,0},{24,8},{32,48},{40,56},{48,32},{56,40},{64,80... | collective-permute-start | bytes 786440 | tf_op jit(solution)/shard_map/ppermute | solution.py:351
  56.7 2.0 %collective-permute-done.10.partner_ref = bf16[128,1024]{1,0:T(8,128)(2,1)S(1)} collective-permute-done((bf16[128,1024]{1,0:T(8,128)(2,1)S(1)}, bf16[128,1024]{1,0:T(8,128)(2,1)S(1)}, u32[]{:S(2)}, u32[]{:S(2)}) %collective-permute-start.10) | collective-permute-done | bytes 262176 | tf_op jit(solution)/shard_map/ppermute | solution.py:351
  59.1 0.5 collective-permute-start.15
  60.0 1.7 %a_12.1.rest_0_.state_ref = bf16[128,2048]{1,0:T(8,128)(2,1)S(1)} custom-call(f32[16,128]{1,0:T(8,128)S(1)} %get-tuple-element.16.x_ref, f32[16,128]{1,0:T(8,128)S(1)} %get-tuple-element.17.other_x_ref, bf16[128,256]{1,0:T(8,128)(2,1)S(1)} %get-tuple-element.15.after_ref.mats_ref, f32[5,64,8192]{2,1,0:T(8,128)S(1)} %bitcast.3, ...), custom_call_target="tpu_custom_call" | custom-call | flops 10000000000 | bytes 1000 | tf_op jit(solution)/shard_map/a_12/pallas_call | solution.py:255
  61.8 0.3 b_10.1.rest_0_.state_ref
  62.1 2.3 %collective-permute-done.18.partner_ref = bf16[128,1024]{1,0:T(8,128)(2,1)S(1)} collective-permute-done((bf16[128,1024]{1,0:T(8,128)(2,1)S(1)}, bf16[128,1024]{1,0:T(8,128)(2,1)S(1)}, u32[]{:S(2)}, u32[]{:S(2)}) %collective-permute-start.18) | collective-permute-done | bytes 262176 | tf_op jit(solution)/shard_map/ppermute | solution.py:351
  64.8 0.5 collective-permute-start.24
  66.0 3.6 %collective-permute-start.23 = (bf16[128,1024]{1,0:T(8,128)(2,1)S(1)}, bf16[128,1024]{1,0:T(8,128)(2,1)S(1)}, u32[]{:S(2)}, u32[]{:S(2)}) collective-permute-start(bf16[128,1024]{1,0:T(8,128)(2,1)S(1)} %b_12.1.rest_0_.state_ref), channel_id=1, source_target_pairs={{0,16},{8,24},{16,0},{24,8},{32,48},{40,56},{48,32},{56,40},{64,80... | collective-permute-start | bytes 786440 | tf_op jit(solution)/shard_map/ppermute | solution.py:351
  69.6 0.4 collective-permute-done.16.partner_ref
  70.4 1.2 %collective-permute-start.22 = (bf16[128,1024]{1,0:T(8,128)(2,1)S(1)}, bf16[128,1024]{1,0:T(8,128)(2,1)S(1)}, u32[]{:S(2)}, u32[]{:S(2)}) collective-permute-start(bf16[128,1024]{1,0:T(8,128)(2,1)S(1)} %c_8.1.rest_0_.state_ref), channel_id=1, source_target_pairs={{0,2},{1,3},{2,0},{3,1},{4,6},{5,7},{6,4},{7,5},{8,10},{9,11},{10,... | collective-permute-start | bytes 786440 | tf_op jit(solution)/shard_map/ppermute | solution.py:351
  71.6 0.3 d_4.1.rest_0_.refs_2_
  72.3 3.4 %collective-permute-done.14.partner_ref = bf16[128,1024]{1,0:T(8,128)(2,1)S(1)} collective-permute-done((bf16[128,1024]{1,0:T(8,128)(2,1)S(1)}, bf16[128,1024]{1,0:T(8,128)(2,1)S(1)}, u32[]{:S(2)}, u32[]{:S(2)}) %collective-permute-start.14) | collective-permute-done | bytes 262176 | tf_op jit(solution)/shard_map/ppermute | solution.py:351
  76.0 0.5 collective-permute-start.20
  76.7 0.6 collective-permute-start.19
  77.7 3.5 %collective-permute-done.23.partner_ref = bf16[128,1024]{1,0:T(8,128)(2,1)S(1)} collective-permute-done((bf16[128,1024]{1,0:T(8,128)(2,1)S(1)}, bf16[128,1024]{1,0:T(8,128)(2,1)S(1)}, u32[]{:S(2)}, u32[]{:S(2)}) %collective-permute-start.23) | collective-permute-done | bytes 262176 | tf_op jit(solution)/shard_map/ppermute | solution.py:351
  81.6 0.5 collective-permute-start.27
  82.5 1.6 %collective-permute-done.21.partner_ref = bf16[128,512]{1,0:T(8,128)(2,1)S(1)} collective-permute-done((bf16[128,512]{1,0:T(8,128)(2,1)S(1)}, bf16[128,512]{1,0:T(8,128)(2,1)S(1)}, u32[]{:S(2)}, u32[]{:S(2)}) %collective-permute-start.21) | collective-permute-done | bytes 131104 | tf_op jit(solution)/shard_map/ppermute | solution.py:351
  84.3 0.5 collective-permute-start.26
  85.2 0.9 collective-permute-done.19.partner_ref
  86.3 0.8 collective-permute-start.25
  87.0 3.9 %collective-permute-done.27.partner_ref = bf16[128,1024]{1,0:T(8,128)(2,1)S(1)} collective-permute-done((bf16[128,1024]{1,0:T(8,128)(2,1)S(1)}, bf16[128,1024]{1,0:T(8,128)(2,1)S(1)}, u32[]{:S(2)}, u32[]{:S(2)}) %collective-permute-start.27) | collective-permute-done | bytes 262176 | tf_op jit(solution)/shard_map/ppermute | solution.py:351
  91.3 1.3 %flush.1.before_ref = bf16[128,8192]{1,0:T(8,128)(2,1)} custom-call(bf16[128,1024]{1,0:T(8,128)(2,1)S(1)} %copy-done.4, bf16[128,1024]{1,0:T(8,128)(2,1)S(1)} %d_2.1.rest_0_.refs_1_, bf16[128,1024]{1,0:T(8,128)(2,1)S(1)} %d_4.1.rest_0_.refs_2_, bf16[128,1024]{1,0:T(8,128)(2,1)S(1)} %d_6.1.rest_0_.refs_3_, bf16[128,1024]{1,0:T(8,128)(2,1)S(1)} %d_8.1.rest_0_.refs_4_, ...), custom_call_target="tpu_custom_call" | custom-call | flops 10000000000 | bytes 1000 | tf_op jit(solution)/shard_map/flush/pallas_call | solution.py:310
  92.6 0.6 collective-permute-done.26.partner_ref
  93.2 0.9 last_14.1.before_ref
  94.1 0.5 collective-permute-done.25.partner_ref
  94.6 0.9 last_15.1
  (65 shorter events, 8.5 us)
Async XLA Ops:
  0.0 3.4 %copy-start.2 = (s32[1,128]{1,0:T(1,128)S(1)}, s32[1,128]{1,0:T(1,128)}, u32[]{:S(2)}) copy-start(s32[1,128]{1,0:T(1,128)} %counts_ref.1) | copy-start | bytes 1540
  0.0 33.9 %slice-start = ((s8[10485760]{0:T(1024)(128)(4,1)}), s8[4194304]{0:T(1024)(128)(4,1)S(1)}, s32[]{:S(2)}) async-start(s8[10485760]{0:T(1024)(128)(4,1)} %bitcast.2), calls=%async_computation.1 | async-start | bytes 8388608
  0.0 33.9 %slice-start.1 = ((s8[10485760]{0:T(1024)(128)(4,1)}), s8[4194304]{0:T(1024)(128)(4,1)S(1)}, s32[]{:S(2)}) async-start(s8[10485760]{0:T(1024)(128)(4,1)} %bitcast.2), calls=%async_computation.2 | async-start | bytes 8388608
  1.8 32.2 %collective-permute-start.4 = (s16[64,8192]{1,0:T(8,128)(2,1)S(1)}, s16[64,8192]{1,0:T(8,128)(2,1)S(1)}, u32[]{:S(2)}, u32[]{:S(2)}) collective-permute-start(s16[64,8192]{1,0:T(8,128)(2,1)S(1)} %encode.1.after_ref), channel_id=1, source_target_pairs={{0,8},{8,0},{16,24},{24,16},{32,40},{40,32},{48,56},{56,48},{64,72... | collective-permute-start | bytes 3145736 | tf_op jit(solution)/shard_map/ppermute | solution.py:351
  3.4 26.4 %copy-start = (bf16[4,2,2,128,128]{4,3,2,1,0:T(8,128)(2,1)S(1)}, bf16[4,2,2,128,128]{4,3,2,1,0:T(8,128)(2,1)}, u32[]{:S(2)}) copy-start(bf16[4,2,2,128,128]{4,3,2,1,0:T(8,128)(2,1)} %trans_ref.1) | copy-start | bytes 1572868
  3.4 30.5 %slice-start.2 = ((s8[10485760]{0:T(1024)(128)(4,1)}), s8[2097152]{0:T(1024)(128)(4,1)S(1)}, s32[]{:S(2)}) async-start(s8[10485760]{0:T(1024)(128)(4,1)} %bitcast.2), calls=%async_computation.3 | async-start | bytes 4194304
  6.7 27.1 %copy-start.1 = (bf16[128,128]{1,0:T(8,128)(2,1)S(1)}, bf16[128,128]{1,0:T(8,128)(2,1)}, u32[]{:S(2)}) copy-start(bf16[128,128]{1,0:T(8,128)(2,1)} %map_ref.1) | copy-start | bytes 98308
  6.7 1.6 %collective-permute-start = (bf16[64,16,128]{2,1,0:T(8,128)(2,1)S(1)}, bf16[64,16,128]{2,1,0:T(8,128)(2,1)S(1)}, u32[]{:S(2)}, u32[]{:S(2)}) collective-permute-start(bf16[64,16,128]{2,1,0:T(8,128)(2,1)S(1)} %get-tuple-element.14), channel_id=1, source_target_pairs={{0,1},{1,0},{2,3},{3,2},{4,5},{5,4},{6,7},{7,6},{8,9},{9,8},{10,11... | collective-permute-start | bytes 786440 | tf_op jit(solution)/shard_map/ppermute | solution.py:351
  25.1 4.9 %collective-permute-start.1 = (f32[4,16,128]{2,1,0:T(8,128)S(1)}, f32[4,16,128]{2,1,0:T(8,128)S(1)}, u32[]{:S(2)}, u32[]{:S(2)}) collective-permute-start(f32[4,16,128]{2,1,0:T(8,128)S(1)} %add.1.after_ref.refs_0_), channel_id=1, source_target_pairs={{0,8},{8,0},{16,24},{24,16},{32,40},{40,32},{48,56},{56,48},{64,72... | collective-permute-start | bytes 98312 | tf_op jit(solution)/shard_map/ppermute | solution.py:351
  26.1 5.4 %collective-permute-start.2 = (f32[4,16,128]{2,1,0:T(8,128)S(1)}, f32[4,16,128]{2,1,0:T(8,128)S(1)}, u32[]{:S(2)}, u32[]{:S(2)}) collective-permute-start(f32[4,16,128]{2,1,0:T(8,128)S(1)} %add.1.after_ref.refs_0_), channel_id=1, source_target_pairs={{0,16},{8,24},{16,0},{24,8},{32,48},{40,56},{48,32},{56,40},{64,80... | collective-permute-start | bytes 98312 | tf_op jit(solution)/shard_map/ppermute | solution.py:351
  28.7 5.1 %collective-permute-start.3 = (f32[4,16,128]{2,1,0:T(8,128)S(1)}, f32[4,16,128]{2,1,0:T(8,128)S(1)}, u32[]{:S(2)}, u32[]{:S(2)}) collective-permute-start(f32[4,16,128]{2,1,0:T(8,128)S(1)} %add.1.after_ref.refs_0_), channel_id=1, source_target_pairs={{0,24},{8,16},{16,8},{24,0},{32,56},{40,48},{48,40},{56,32},{64,88... | collective-permute-start | bytes 98312 | tf_op jit(solution)/shard_map/ppermute | solution.py:351
  34.9 1.6 %collective-permute-start.5 = (bf16[128,1024]{1,0:T(8,128)(2,1)S(1)}, bf16[128,1024]{1,0:T(8,128)(2,1)S(1)}, u32[]{:S(2)}, u32[]{:S(2)}) collective-permute-start(bf16[128,1024]{1,0:T(8,128)(2,1)S(1)} %a_0.1.rest_0_.state_ref), channel_id=1, source_target_pairs={{0,1},{1,0},{2,3},{3,2},{4,5},{5,4},{6,7},{7,6},{8,9},{9,8},{10,11... | collective-permute-start | bytes 786440 | tf_op jit(solution)/shard_map/ppermute | solution.py:351
  35.8 3.1 %collective-permute-start.8 = (bf16[128,1024]{1,0:T(8,128)(2,1)S(1)}, bf16[128,1024]{1,0:T(8,128)(2,1)S(1)}, u32[]{:S(2)}, u32[]{:S(2)}) collective-permute-start(bf16[128,1024]{1,0:T(8,128)(2,1)S(1)} %a_2.1.rest_0_.state_ref), channel_id=1, source_target_pairs={{0,1},{1,0},{2,3},{3,2},{4,5},{5,4},{6,7},{7,6},{8,9},{9,8},{10,11... | collective-permute-start | bytes 786440 | tf_op jit(solution)/shard_map/ppermute | solution.py:351
  36.8 10.7 %collective-permute-start.6 = (bf16[128,1024]{1,0:T(8,128)(2,1)S(1)}, bf16[128,1024]{1,0:T(8,128)(2,1)S(1)}, u32[]{:S(2)}, u32[]{:S(2)}) collective-permute-start(bf16[128,1024]{1,0:T(8,128)(2,1)S(1)} %b_0.1.rest_0_.state_ref), channel_id=1, source_target_pairs={{0,16},{8,24},{16,0},{24,8},{32,48},{40,56},{48,32},{56,40},{64,80... | collective-permute-start | bytes 786440 | tf_op jit(solution)/shard_map/ppermute | solution.py:351
  38.9 3.8 %collective-permute-start.7 = (bf16[128,2048]{1,0:T(8,128)(2,1)S(1)}, bf16[128,2048]{1,0:T(8,128)(2,1)S(1)}, u32[]{:S(2)}, u32[]{:S(2)}) collective-permute-start(bf16[128,2048]{1,0:T(8,128)(2,1)S(1)} %a_4.1.rest_0_.state_ref), channel_id=1, source_target_pairs={{0,1},{1,0},{2,3},{3,2},{4,5},{5,4},{6,7},{7,6},{8,9},{9,8},{10,11... | collective-permute-start | bytes 1572872 | tf_op jit(solution)/shard_map/ppermute | solution.py:351
  39.3 13.9 %collective-permute-start.12 = (bf16[128,1024]{1,0:T(8,128)(2,1)S(1)}, bf16[128,1024]{1,0:T(8,128)(2,1)S(1)}, u32[]{:S(2)}, u32[]{:S(2)}) collective-permute-start(bf16[128,1024]{1,0:T(8,128)(2,1)S(1)} %b_2.1.rest_0_.state_ref), channel_id=1, source_target_pairs={{0,16},{8,24},{16,0},{24,8},{32,48},{40,56},{48,32},{56,40},{64,80... | collective-permute-start | bytes 786440 | tf_op jit(solution)/shard_map/ppermute | solution.py:351
  43.0 15.8 %collective-permute-start.10 = (bf16[128,1024]{1,0:T(8,128)(2,1)S(1)}, bf16[128,1024]{1,0:T(8,128)(2,1)S(1)}, u32[]{:S(2)}, u32[]{:S(2)}) collective-permute-start(bf16[128,1024]{1,0:T(8,128)(2,1)S(1)} %b_4.1.rest_0_.state_ref), channel_id=1, source_target_pairs={{0,16},{8,24},{16,0},{24,8},{32,48},{40,56},{48,32},{56,40},{64,80... | collective-permute-start | bytes 786440 | tf_op jit(solution)/shard_map/ppermute | solution.py:351
  47.9 11.8 %collective-permute-start.9 = (bf16[128,1024]{1,0:T(8,128)(2,1)S(1)}, bf16[128,1024]{1,0:T(8,128)(2,1)S(1)}, u32[]{:S(2)}, u32[]{:S(2)}) collective-permute-start(bf16[128,1024]{1,0:T(8,128)(2,1)S(1)} %c_0.1.rest_0_.state_ref), channel_id=1, source_target_pairs={{0,2},{1,3},{2,0},{3,1},{4,6},{5,7},{6,4},{7,5},{8,10},{9,11},{10,... | collective-permute-start | bytes 786440 | tf_op jit(solution)/shard_map/ppermute | solution.py:351
  50.1 4.0 %collective-permute-start.11 = (bf16[128,2048]{1,0:T(8,128)(2,1)S(1)}, bf16[128,2048]{1,0:T(8,128)(2,1)S(1)}, u32[]{:S(2)}, u32[]{:S(2)}) collective-permute-start(bf16[128,2048]{1,0:T(8,128)(2,1)S(1)} %a_8.1.rest_0_.state_ref), channel_id=1, source_target_pairs={{0,1},{1,0},{2,3},{3,2},{4,5},{5,4},{6,7},{7,6},{8,9},{9,8},{10,11... | collective-permute-start | bytes 1572872 | tf_op jit(solution)/shard_map/ppermute | solution.py:351
  50.5 13.9 %collective-permute-start.18 = (bf16[128,1024]{1,0:T(8,128)(2,1)S(1)}, bf16[128,1024]{1,0:T(8,128)(2,1)S(1)}, u32[]{:S(2)}, u32[]{:S(2)}) collective-permute-start(bf16[128,1024]{1,0:T(8,128)(2,1)S(1)} %b_6.1.rest_0_.state_ref), channel_id=1, source_target_pairs={{0,16},{8,24},{16,0},{24,8},{32,48},{40,56},{48,32},{56,40},{64,80... | collective-permute-start | bytes 786440 | tf_op jit(solution)/shard_map/ppermute | solution.py:351
  53.5 11.3 %collective-permute-start.17 = (bf16[128,1024]{1,0:T(8,128)(2,1)S(1)}, bf16[128,1024]{1,0:T(8,128)(2,1)S(1)}, u32[]{:S(2)}, u32[]{:S(2)}) collective-permute-start(bf16[128,1024]{1,0:T(8,128)(2,1)S(1)} %c_2.1.rest_0_.state_ref), channel_id=1, source_target_pairs={{0,2},{1,3},{2,0},{3,1},{4,6},{5,7},{6,4},{7,5},{8,10},{9,11},{10,... | collective-permute-start | bytes 786440 | tf_op jit(solution)/shard_map/ppermute | solution.py:351
  54.4 15.6 %collective-permute-start.16 = (bf16[128,1024]{1,0:T(8,128)(2,1)S(1)}, bf16[128,1024]{1,0:T(8,128)(2,1)S(1)}, u32[]{:S(2)}, u32[]{:S(2)}) collective-permute-start(bf16[128,1024]{1,0:T(8,128)(2,1)S(1)} %b_8.1.rest_0_.state_ref), channel_id=1, source_target_pairs={{0,16},{8,24},{16,0},{24,8},{32,48},{40,56},{48,32},{56,40},{64,80... | collective-permute-start | bytes 786440 | tf_op jit(solution)/shard_map/ppermute | solution.py:351
  59.1 12.5 %collective-permute-start.15 = (bf16[128,1024]{1,0:T(8,128)(2,1)S(1)}, bf16[128,1024]{1,0:T(8,128)(2,1)S(1)}, u32[]{:S(2)}, u32[]{:S(2)}) collective-permute-start(bf16[128,1024]{1,0:T(8,128)(2,1)S(1)} %c_4.1.rest_0_.state_ref), channel_id=1, source_target_pairs={{0,2},{1,3},{2,0},{3,1},{4,6},{5,7},{6,4},{7,5},{8,10},{9,11},{10,... | collective-permute-start | bytes 786440 | tf_op jit(solution)/shard_map/ppermute | solution.py:351
  60.0 1.7 %copy-start.3 = (bf16[128,1024]{1,0:T(8,128)(2,1)}, bf16[128,1024]{1,0:T(8,128)(2,1)S(1)}, u32[]{:S(2)}) copy-start(bf16[128,1024]{1,0:T(8,128)(2,1)S(1)} %d_0.1.rest_0_.refs_0_) | copy-start | bytes 786436
  61.7 4.0 %collective-permute-start.13 = (bf16[128,2048]{1,0:T(8,128)(2,1)S(1)}, bf16[128,2048]{1,0:T(8,128)(2,1)S(1)}, u32[]{:S(2)}, u32[]{:S(2)}) collective-permute-start(bf16[128,2048]{1,0:T(8,128)(2,1)S(1)} %a_12.1.rest_0_.state_ref), channel_id=1, source_target_pairs={{0,1},{1,0},{2,3},{3,2},{4,5},{5,4},{6,7},{7,6},{8,9},{9,8},{10,11... | collective-permute-start | bytes 1572872 | tf_op jit(solution)/shard_map/ppermute | solution.py:351
  64.4 11.2 %collective-permute-start.14 = (bf16[128,1024]{1,0:T(8,128)(2,1)S(1)}, bf16[128,1024]{1,0:T(8,128)(2,1)S(1)}, u32[]{:S(2)}, u32[]{:S(2)}) collective-permute-start(bf16[128,1024]{1,0:T(8,128)(2,1)S(1)} %b_10.1.rest_0_.state_ref), channel_id=1, source_target_pairs={{0,16},{8,24},{16,0},{24,8},{32,48},{40,56},{48,32},{56,40},{64,80... | collective-permute-start | bytes 786440 | tf_op jit(solution)/shard_map/ppermute | solution.py:351
  64.8 11.9 %collective-permute-start.24 = (bf16[128,1024]{1,0:T(8,128)(2,1)S(1)}, bf16[128,1024]{1,0:T(8,128)(2,1)S(1)}, u32[]{:S(2)}, u32[]{:S(2)}) collective-permute-start(bf16[128,1024]{1,0:T(8,128)(2,1)S(1)} %c_6.1.rest_0_.state_ref), channel_id=1, source_target_pairs={{0,2},{1,3},{2,0},{3,1},{4,6},{5,7},{6,4},{7,5},{8,10},{9,11},{10,... | collective-permute-start | bytes 786440 | tf_op jit(solution)/shard_map/ppermute | solution.py:351
  66.0 15.2 %collective-permute-start.23 = (bf16[128,1024]{1,0:T(8,128)(2,1)S(1)}, bf16[128,1024]{1,0:T(8,128)(2,1)S(1)}, u32[]{:S(2)}, u32[]{:S(2)}) collective-permute-start(bf16[128,1024]{1,0:T(8,128)(2,1)S(1)} %b_12.1.rest_0_.state_ref), channel_id=1, source_target_pairs={{0,16},{8,24},{16,0},{24,8},{32,48},{40,56},{48,32},{56,40},{64,80... | collective-permute-start | bytes 786440 | tf_op jit(solution)/shard_map/ppermute | solution.py:351
  70.4 11.8 %collective-permute-start.22 = (bf16[128,1024]{1,0:T(8,128)(2,1)S(1)}, bf16[128,1024]{1,0:T(8,128)(2,1)S(1)}, u32[]{:S(2)}, u32[]{:S(2)}) collective-permute-start(bf16[128,1024]{1,0:T(8,128)(2,1)S(1)} %c_8.1.rest_0_.state_ref), channel_id=1, source_target_pairs={{0,2},{1,3},{2,0},{3,1},{4,6},{5,7},{6,4},{7,5},{8,10},{9,11},{10,... | collective-permute-start | bytes 786440 | tf_op jit(solution)/shard_map/ppermute | solution.py:351
  72.2 11.9 %collective-permute-start.21 = (bf16[128,512]{1,0:T(8,128)(2,1)S(1)}, bf16[128,512]{1,0:T(8,128)(2,1)S(1)}, u32[]{:S(2)}, u32[]{:S(2)}) collective-permute-start(bf16[128,512]{1,0:T(8,128)(2,1)S(1)} %b_14.1.rest_0_.state_ref), channel_id=1, source_target_pairs={{0,16},{8,24},{16,0},{24,8},{32,48},{40,56},{48,32},{56,40},{64,80... | collective-permute-start | bytes 393224 | tf_op jit(solution)/shard_map/ppermute | solution.py:351
  76.0 8.8 %collective-permute-start.20 = (bf16[128,1024]{1,0:T(8,128)(2,1)S(1)}, bf16[128,1024]{1,0:T(8,128)(2,1)S(1)}, u32[]{:S(2)}, u32[]{:S(2)}) collective-permute-start(bf16[128,1024]{1,0:T(8,128)(2,1)S(1)} %c_10.1.rest_0_.state_ref), channel_id=1, source_target_pairs={{0,2},{1,3},{2,0},{3,1},{4,6},{5,7},{6,4},{7,5},{8,10},{9,11},{10,... | collective-permute-start | bytes 786440 | tf_op jit(solution)/shard_map/ppermute | solution.py:351
  76.7 9.3 %collective-permute-start.19 = (bf16[128,512]{1,0:T(8,128)(2,1)S(1)}, bf16[128,512]{1,0:T(8,128)(2,1)S(1)}, u32[]{:S(2)}, u32[]{:S(2)}) collective-permute-start(bf16[128,512]{1,0:T(8,128)(2,1)S(1)} %b_15.1.rest_0_.state_ref), channel_id=1, source_target_pairs={{0,16},{8,24},{16,0},{24,8},{32,48},{40,56},{48,32},{56,40},{64,80... | collective-permute-start | bytes 393224 | tf_op jit(solution)/shard_map/ppermute | solution.py:351
  81.6 9.3 %collective-permute-start.27 = (bf16[128,1024]{1,0:T(8,128)(2,1)S(1)}, bf16[128,1024]{1,0:T(8,128)(2,1)S(1)}, u32[]{:S(2)}, u32[]{:S(2)}) collective-permute-start(bf16[128,1024]{1,0:T(8,128)(2,1)S(1)} %c_12.1.rest_0_.state_ref), channel_id=1, source_target_pairs={{0,2},{1,3},{2,0},{3,1},{4,6},{5,7},{6,4},{7,5},{8,10},{9,11},{10,... | collective-permute-start | bytes 786440 | tf_op jit(solution)/shard_map/ppermute | solution.py:351
  84.3 8.9 %collective-permute-start.26 = (bf16[128,512]{1,0:T(8,128)(2,1)S(1)}, bf16[128,512]{1,0:T(8,128)(2,1)S(1)}, u32[]{:S(2)}, u32[]{:S(2)}) collective-permute-start(bf16[128,512]{1,0:T(8,128)(2,1)S(1)} %c_14.1.rest_0_.state_ref), channel_id=1, source_target_pairs={{0,2},{1,3},{2,0},{3,1},{4,6},{5,7},{6,4},{7,5},{8,10},{9,11},{10,... | collective-permute-start | bytes 393224 | tf_op jit(solution)/shard_map/ppermute | solution.py:351
  86.3 5.0 %copy-start.4 = (bf16[128,1024]{1,0:T(8,128)(2,1)S(1)}, bf16[128,1024]{1,0:T(8,128)(2,1)}, u32[]{:S(2)}) copy-start(bf16[128,1024]{1,0:T(8,128)(2,1)} %copy-done.3) | copy-start | bytes 786436
  86.3 8.3 %collective-permute-start.25 = (bf16[128,512]{1,0:T(8,128)(2,1)S(1)}, bf16[128,512]{1,0:T(8,128)(2,1)S(1)}, u32[]{:S(2)}, u32[]{:S(2)}) collective-permute-start(bf16[128,512]{1,0:T(8,128)(2,1)S(1)} %c_15.1.rest_0_.state_ref), channel_id=1, source_target_pairs={{0,2},{1,3},{2,0},{3,1},{4,6},{5,7},{6,4},{7,5},{8,10},{9,11},{10,... | collective-permute-start | bytes 393224 | tf_op jit(solution)/shard_map/ppermute | solution.py:351

commit v7 on v6

--- a/solution.py
+++ b/solution.py
@@ -175,16 +175,18 @@
     )(near(keep), near(got))
 
 
-def add_kernel(parts_ref, out_ref):
-    out_ref[...] = sum(parts_ref[i].astype(jnp.float32) for i in range(parts_ref.shape[0]))
+def add_kernel(parts_ref, out_ref, sent_ref):
+    total = sum(parts_ref[i].astype(jnp.float32) for i in range(parts_ref.shape[0]))
+    out_ref[...] = total
+    sent_ref[...] = total.astype(jnp.bfloat16)
 
 
 def add(parts):
     return kernel_call(
         add_kernel,
         in_specs=[VMEM],
-        out_specs=VMEM,
-        out_shape=pltpu.VMEM(parts.shape[1:], jnp.float32),
+        out_specs=[VMEM] * 2,
+        out_shape=[pltpu.VMEM(parts.shape[1:], kind) for kind in (jnp.float32, jnp.bfloat16)],
         compiler_params=limit(4),
         name="add",
     )(near(parts))
@@ -194,7 +196,7 @@
     parts, (mine_ref, other_ref) = refs[:-2], refs[-2:]
     place = place_of("x")
     for there, out_ref in ((place, mine_ref), (jnp.bitwise_xor(place, 1), other_ref)):
-        total = sum(p[there] for p in parts).astype(jnp.bfloat16)
+        total = sum(p[there].astype(jnp.float32) for p in parts).astype(jnp.bfloat16)
         out_ref[...] = jnp.dot(total, map_ref[...], preferred_element_type=jnp.float32)
 
 
@@ -364,9 +366,9 @@
     parts = lax.all_to_all(
         deal(keep, got), ("bx", "by"), split_axis=0, concat_axis=0, tiled=True, axis_index_groups=plane
     )
-    row = add(parts)
+    row, sent = add(parts)
     mats = pick_mats(row, trans)
-    mine, theirs = expand(mats[0], source_map, [row] + [move(row, "bx", k) for k in (1, 2, 3)])
+    mine, theirs = expand(mats[0], source_map, [row] + [move(sent, "bx", k) for k in (1, 2, 3)])
 
     starts = [sum(PARTS[:i]) for i in range(len(PARTS))]
     groups = [range(sum(GROUPS[:g]), sum(GROUPS[: g + 1])) for g in range(len(GROUPS))]

time: 95.8 us -> 95.6 us (level)
  no operation moved by 1% of the time
where the time goes in v7:
time: 95.6 us; the launch traced here: 95.5 us
  waiting for transfers between devices  29.9 us (31%)
  starting transfers between devices  25.4 us (27%)
  Pallas kernels  22.9 us (24%)
  blocking collectives  16.7 us (17%)
    ppermute x28, waiting for transfers between devices, move(): lax.ppermute(value, axis, [(s, s ^ mask) for s in range(lax.axis_size(axi...  29.9 us
    ppermute x28, starting transfers between devices, move(): lax.ppermute(value, axis, [(s, s ^ mask) for s in range(lax.axis_size(axi...  25.4 us
    all_to_all x1, blocking collectives, per_device(): lax.all_to_all(deal(keep, got), ('bx', 'by'), split_axis=0, concat_axis=0...  16.7 us
    pallas_call x25, Pallas kernels, next_level(): kernel_call(functools.partial(level_kernel, start, boxes, skip, slot), in...  7.82 us
    pallas_call x5, Pallas kernels, first_level(): kernel_call(functools.partial(first_kernel, start, boxes), in_specs=[VMEM...  6.73 us
    pallas_call x1, Pallas kernels, box_sums(): kernel_call(box_sums_kernel, in_specs=[SMEM, ANY, ANY, ANY], out_specs=[V...  3.23 us
  transfers between devices with their start and end apart: 28, of which 16 were waited for; matrix products, arithmetic and copies ran while one was open for 0% of the time, Pallas kernels for 20%

profile of v7, /device:TPU:0, one launch (start us, length us, event | category | flops | bytes accessed | tf_op | source)
XLA Modules:
  0.0 95.5 jit_solution(6052790721495332733)
XLA Ops:
  0.0 1.7 %encode.1.after_ref = s16[64,8192]{1,0:T(8,128)(2,1)S(1)} custom-call(f32[5,64,8192]{2,1,0:T(8,128)} %phases_ref.65), custom_call_target="tpu_custom_call" | custom-call | flops 1000 | bytes 1000 | tf_op jit(solution)/shard_map/encode/pallas_call | solution.py:101
  1.8 1.7 %collective-permute-start.4 = (s16[64,8192]{1,0:T(8,128)(2,1)S(1)}, s16[64,8192]{1,0:T(8,128)(2,1)S(1)}, u32[]{:S(2)}, u32[]{:S(2)}) collective-permute-start(s16[64,8192]{1,0:T(8,128)(2,1)S(1)} %encode.1.after_ref), channel_id=1, source_target_pairs={{0,8},{8,0},{16,24},{24,16},{32,40},{40,32},{48,56},{56,48},{64,72... | collective-permute-start | bytes 3145736 | tf_op jit(solution)/shard_map/ppermute | solution.py:353
  3.4 3.2 %box_sums.1 = (bf16[64,16,128]{2,1,0:T(8,128)(2,1)S(1)}, bf16[64,16,128]{2,1,0:T(8,128)(2,1)S(1)}) custom-call(s32[1,128]{1,0:T(1,128)S(1)} %copy-done.2, s16[64,8192]{1,0:T(8,128)(2,1)S(1)} %encode.1.after_ref, s32[128,128]{1,0:T(8,128)} %bitcast.5, bf16[128,128,128]{2,1,0:T(8,128)(2,1)} %bitcast.4), custom_call_target="tpu_custom_call" | custom-call | flops 1000 | bytes 1000 | tf_op jit(solution)/shard_map/box_sums/pallas_call | solution.py:143
  6.8 1.5 %collective-permute-done.got_ref = bf16[64,16,128]{2,1,0:T(8,128)(2,1)S(1)} collective-permute-done((bf16[64,16,128]{2,1,0:T(8,128)(2,1)S(1)}, bf16[64,16,128]{2,1,0:T(8,128)(2,1)S(1)}, u32[]{:S(2)}, u32[]{:S(2)}) %collective-permute-start) | collective-permute-done | bytes 262176 | tf_op jit(solution)/shard_map/ppermute | solution.py:353
  8.4 16.7 %all_to_all.5.parts_ref = bf16[16,4,16,128]{3,2,1,0:T(8,128)(2,1)S(1)} all-to-all(bf16[16,4,16,128]{3,2,1,0:T(8,128)(2,1)S(1)} %deal.1), channel_id=1, replica_groups={{0,2,4,6,32,34,36,38,64,66,68,70,96,98,100,102},{1,3,5,7,33,35,37,39,65..., dimensions={0} | all-to-all | bytes 524288 | tf_op jit(solution)/shard_map/all_to_all | solution.py:366
  25.1 1.1 %collective-permute-start.1 = (bf16[4,16,128]{2,1,0:T(8,128)(2,1)S(1)}, bf16[4,16,128]{2,1,0:T(8,128)(2,1)S(1)}, u32[]{:S(2)}, u32[]{:S(2)}) collective-permute-start(bf16[4,16,128]{2,1,0:T(8,128)(2,1)S(1)} %get-tuple-element.19), channel_id=1, source_target_pairs={{0,8},{8,0},{16,24},{24,16},{32,40},{40,32},{48,56},{56,48},{64,72... | collective-permute-start | bytes 49160 | tf_op jit(solution)/shard_map/ppermute | solution.py:353
  26.1 2.6 %collective-permute-start.2 = (bf16[4,16,128]{2,1,0:T(8,128)(2,1)S(1)}, bf16[4,16,128]{2,1,0:T(8,128)(2,1)S(1)}, u32[]{:S(2)}, u32[]{:S(2)}) collective-permute-start(bf16[4,16,128]{2,1,0:T(8,128)(2,1)S(1)} %get-tuple-element.19), channel_id=1, source_target_pairs={{0,16},{8,24},{16,0},{24,8},{32,48},{40,56},{48,32},{56,40},{64,80... | collective-permute-start | bytes 49160 | tf_op jit(solution)/shard_map/ppermute | solution.py:353
  28.7 1.2 %collective-permute-start.3 = (bf16[4,16,128]{2,1,0:T(8,128)(2,1)S(1)}, bf16[4,16,128]{2,1,0:T(8,128)(2,1)S(1)}, u32[]{:S(2)}, u32[]{:S(2)}) collective-permute-start(bf16[4,16,128]{2,1,0:T(8,128)(2,1)S(1)} %get-tuple-element.19), channel_id=1, source_target_pairs={{0,24},{8,16},{16,8},{24,0},{32,56},{40,48},{48,40},{56,32},{64,88... | collective-permute-start | bytes 49160 | tf_op jit(solution)/shard_map/ppermute | solution.py:353
  30.0 1.4 %collective-permute-done.2.refs_2_ = bf16[4,16,128]{2,1,0:T(8,128)(2,1)S(1)} collective-permute-done((bf16[4,16,128]{2,1,0:T(8,128)(2,1)S(1)}, bf16[4,16,128]{2,1,0:T(8,128)(2,1)S(1)}, u32[]{:S(2)}, u32[]{:S(2)}) %collective-permute-start.2) | collective-permute-done | bytes 16416 | tf_op jit(solution)/shard_map/ppermute | solution.py:353
  31.4 2.3 %collective-permute-done.3.refs_3_ = bf16[4,16,128]{2,1,0:T(8,128)(2,1)S(1)} collective-permute-done((bf16[4,16,128]{2,1,0:T(8,128)(2,1)S(1)}, bf16[4,16,128]{2,1,0:T(8,128)(2,1)S(1)}, u32[]{:S(2)}, u32[]{:S(2)}) %collective-permute-start.3) | collective-permute-done | bytes 16416 | tf_op jit(solution)/shard_map/ppermute | solution.py:353
  33.8 0.9 a_0.1.rest_0_.state_ref
  34.8 0.9 a_2.1.rest_0_.state_ref
  35.7 0.6 collective-permute-start.8
  36.6 0.4 collective-permute-start.6
  37.0 1.7 %a_4.1.rest_0_.state_ref = bf16[128,2048]{1,0:T(8,128)(2,1)S(1)} custom-call(f32[16,128]{1,0:T(8,128)S(1)} %get-tuple-element.20.x_ref, f32[16,128]{1,0:T(8,128)S(1)} %get-tuple-element.21.other_x_ref, bf16[128,256]{1,0:T(8,128)(2,1)S(1)} %get-tuple-element.18.after_ref.mats_ref, f32[5,64,8192]{2,1,0:T(8,128)S(1)} %bitcast.3, ...), custom_call_target="tpu_custom_call" | custom-call | flops 10000000000 | bytes 1000 | tf_op jit(solution)/shard_map/a_4/pallas_call | solution.py:257
  39.1 3.3 %collective-permute-start.12 = (bf16[128,1024]{1,0:T(8,128)(2,1)S(1)}, bf16[128,1024]{1,0:T(8,128)(2,1)S(1)}, u32[]{:S(2)}, u32[]{:S(2)}) collective-permute-start(bf16[128,1024]{1,0:T(8,128)(2,1)S(1)} %b_2.1.rest_0_.state_ref), channel_id=1, source_target_pairs={{0,16},{8,24},{16,0},{24,8},{32,48},{40,56},{48,32},{56,40},{64,80... | collective-permute-start | bytes 786440 | tf_op jit(solution)/shard_map/ppermute | solution.py:353
  42.8 1.5 %collective-permute-start.10 = (bf16[128,1024]{1,0:T(8,128)(2,1)S(1)}, bf16[128,1024]{1,0:T(8,128)(2,1)S(1)}, u32[]{:S(2)}, u32[]{:S(2)}) collective-permute-start(bf16[128,1024]{1,0:T(8,128)(2,1)S(1)} %b_4.1.rest_0_.state_ref), channel_id=1, source_target_pairs={{0,16},{8,24},{16,0},{24,8},{32,48},{40,56},{48,32},{56,40},{64,80... | collective-permute-start | bytes 786440 | tf_op jit(solution)/shard_map/ppermute | solution.py:353
  44.3 3.0 %collective-permute-done.6.partner_ref = bf16[128,1024]{1,0:T(8,128)(2,1)S(1)} collective-permute-done((bf16[128,1024]{1,0:T(8,128)(2,1)S(1)}, bf16[128,1024]{1,0:T(8,128)(2,1)S(1)}, u32[]{:S(2)}, u32[]{:S(2)}) %collective-permute-start.6) | collective-permute-done | bytes 262176 | tf_op jit(solution)/shard_map/ppermute | solution.py:353
  47.7 0.5 collective-permute-start.9
  48.3 1.7 %a_8.1.rest_0_.state_ref = bf16[128,2048]{1,0:T(8,128)(2,1)S(1)} custom-call(f32[16,128]{1,0:T(8,128)S(1)} %get-tuple-element.20.x_ref, f32[16,128]{1,0:T(8,128)S(1)} %get-tuple-element.21.other_x_ref, bf16[128,256]{1,0:T(8,128)(2,1)S(1)} %get-tuple-element.18.after_ref.mats_ref, f32[5,64,8192]{2,1,0:T(8,128)S(1)} %bitcast.3, ...), custom_call_target="tpu_custom_call" | custom-call | flops 10000000000 | bytes 1000 | tf_op jit(solution)/shard_map/a_8/pallas_call | solution.py:257
  50.6 2.4 %collective-permute-done.12.partner_ref = bf16[128,1024]{1,0:T(8,128)(2,1)S(1)} collective-permute-done((bf16[128,1024]{1,0:T(8,128)(2,1)S(1)}, bf16[128,1024]{1,0:T(8,128)(2,1)S(1)}, u32[]{:S(2)}, u32[]{:S(2)}) %collective-permute-start.12) | collective-permute-done | bytes 262176 | tf_op jit(solution)/shard_map/ppermute | solution.py:353
  53.3 0.5 collective-permute-start.17
  54.2 2.3 %collective-permute-start.16 = (bf16[128,1024]{1,0:T(8,128)(2,1)S(1)}, bf16[128,1024]{1,0:T(8,128)(2,1)S(1)}, u32[]{:S(2)}, u32[]{:S(2)}) collective-permute-start(bf16[128,1024]{1,0:T(8,128)(2,1)S(1)} %b_8.1.rest_0_.state_ref), channel_id=1, source_target_pairs={{0,16},{8,24},{16,0},{24,8},{32,48},{40,56},{48,32},{56,40},{64,80... | collective-permute-start | bytes 786440 | tf_op jit(solution)/shard_map/ppermute | solution.py:353
  56.6 2.0 %collective-permute-done.10.partner_ref = bf16[128,1024]{1,0:T(8,128)(2,1)S(1)} collective-permute-done((bf16[128,1024]{1,0:T(8,128)(2,1)S(1)}, bf16[128,1024]{1,0:T(8,128)(2,1)S(1)}, u32[]{:S(2)}, u32[]{:S(2)}) %collective-permute-start.10) | collective-permute-done | bytes 262176 | tf_op jit(solution)/shard_map/ppermute | solution.py:353
  59.0 0.5 collective-permute-start.15
  59.8 1.7 %a_12.1.rest_0_.state_ref = bf16[128,2048]{1,0:T(8,128)(2,1)S(1)} custom-call(f32[16,128]{1,0:T(8,128)S(1)} %get-tuple-element.20.x_ref, f32[16,128]{1,0:T(8,128)S(1)} %get-tuple-element.21.other_x_ref, bf16[128,256]{1,0:T(8,128)(2,1)S(1)} %get-tuple-element.18.after_ref.mats_ref, f32[5,64,8192]{2,1,0:T(8,128)S(1)} %bitcast.3, ...), custom_call_target="tpu_custom_call" | custom-call | flops 10000000000 | bytes 1000 | tf_op jit(solution)/shard_map/a_12/pallas_call | solution.py:257
  62.0 2.3 %collective-permute-done.18.partner_ref = bf16[128,1024]{1,0:T(8,128)(2,1)S(1)} collective-permute-done((bf16[128,1024]{1,0:T(8,128)(2,1)S(1)}, bf16[128,1024]{1,0:T(8,128)(2,1)S(1)}, u32[]{:S(2)}, u32[]{:S(2)}) %collective-permute-start.18) | collective-permute-done | bytes 262176 | tf_op jit(solution)/shard_map/ppermute | solution.py:353
  64.6 0.5 collective-permute-start.24
  65.9 3.6 %collective-permute-start.23 = (bf16[128,1024]{1,0:T(8,128)(2,1)S(1)}, bf16[128,1024]{1,0:T(8,128)(2,1)S(1)}, u32[]{:S(2)}, u32[]{:S(2)}) collective-permute-start(bf16[128,1024]{1,0:T(8,128)(2,1)S(1)} %b_12.1.rest_0_.state_ref), channel_id=1, source_target_pairs={{0,16},{8,24},{16,0},{24,8},{32,48},{40,56},{48,32},{56,40},{64,80... | collective-permute-start | bytes 786440 | tf_op jit(solution)/shard_map/ppermute | solution.py:353
  69.4 0.4 collective-permute-done.16.partner_ref
  69.8 0.3 c_8.1.rest_0_.state_ref
  70.2 1.2 %collective-permute-start.22 = (bf16[128,1024]{1,0:T(8,128)(2,1)S(1)}, bf16[128,1024]{1,0:T(8,128)(2,1)S(1)}, u32[]{:S(2)}, u32[]{:S(2)}) collective-permute-start(bf16[128,1024]{1,0:T(8,128)(2,1)S(1)} %c_8.1.rest_0_.state_ref), channel_id=1, source_target_pairs={{0,2},{1,3},{2,0},{3,1},{4,6},{5,7},{6,4},{7,5},{8,10},{9,11},{10,... | collective-permute-start | bytes 786440 | tf_op jit(solution)/shard_map/ppermute | solution.py:353
  71.4 0.3 d_4.1.rest_0_.refs_2_
  72.1 3.3 %collective-permute-done.14.partner_ref = bf16[128,1024]{1,0:T(8,128)(2,1)S(1)} collective-permute-done((bf16[128,1024]{1,0:T(8,128)(2,1)S(1)}, bf16[128,1024]{1,0:T(8,128)(2,1)S(1)}, u32[]{:S(2)}, u32[]{:S(2)}) %collective-permute-start.14) | collective-permute-done | bytes 262176 | tf_op jit(solution)/shard_map/ppermute | solution.py:353
  75.8 0.5 collective-permute-start.20
  76.6 0.6 collective-permute-start.19
  77.5 3.5 %collective-permute-done.23.partner_ref = bf16[128,1024]{1,0:T(8,128)(2,1)S(1)} collective-permute-done((bf16[128,1024]{1,0:T(8,128)(2,1)S(1)}, bf16[128,1024]{1,0:T(8,128)(2,1)S(1)}, u32[]{:S(2)}, u32[]{:S(2)}) %collective-permute-start.23) | collective-permute-done | bytes 262176 | tf_op jit(solution)/shard_map/ppermute | solution.py:353
  81.4 0.5 collective-permute-start.27
  82.3 1.6 %collective-permute-done.21.partner_ref = bf16[128,512]{1,0:T(8,128)(2,1)S(1)} collective-permute-done((bf16[128,512]{1,0:T(8,128)(2,1)S(1)}, bf16[128,512]{1,0:T(8,128)(2,1)S(1)}, u32[]{:S(2)}, u32[]{:S(2)}) %collective-permute-start.21) | collective-permute-done | bytes 131104 | tf_op jit(solution)/shard_map/ppermute | solution.py:353
  84.1 0.5 collective-permute-start.26
  85.0 0.9 collective-permute-done.19.partner_ref
  86.1 0.7 collective-permute-start.25
  86.9 3.9 %collective-permute-done.27.partner_ref = bf16[128,1024]{1,0:T(8,128)(2,1)S(1)} collective-permute-done((bf16[128,1024]{1,0:T(8,128)(2,1)S(1)}, bf16[128,1024]{1,0:T(8,128)(2,1)S(1)}, u32[]{:S(2)}, u32[]{:S(2)}) %collective-permute-start.27) | collective-permute-done | bytes 262176 | tf_op jit(solution)/shard_map/ppermute | solution.py:353
  91.1 1.3 %flush.1.before_ref = bf16[128,8192]{1,0:T(8,128)(2,1)} custom-call(bf16[128,1024]{1,0:T(8,128)(2,1)S(1)} %copy-done.4, bf16[128,1024]{1,0:T(8,128)(2,1)S(1)} %d_2.1.rest_0_.refs_1_, bf16[128,1024]{1,0:T(8,128)(2,1)S(1)} %d_4.1.rest_0_.refs_2_, bf16[128,1024]{1,0:T(8,128)(2,1)S(1)} %d_6.1.rest_0_.refs_3_, bf16[128,1024]{1,0:T(8,128)(2,1)S(1)} %d_8.1.rest_0_.refs_4_, ...), custom_call_target="tpu_custom_call" | custom-call | flops 10000000000 | bytes 1000 | tf_op jit(solution)/shard_map/flush/pallas_call | solution.py:312
  92.4 0.6 collective-permute-done.26.partner_ref
  93.0 0.9 last_14.1.before_ref
  93.9 0.5 collective-permute-done.25.partner_ref
  94.4 0.9 last_15.1
  (65 shorter events, 8.5 us)
Async XLA Ops:
  0.0 3.4 %copy-start.2 = (s32[1,128]{1,0:T(1,128)S(1)}, s32[1,128]{1,0:T(1,128)}, u32[]{:S(2)}) copy-start(s32[1,128]{1,0:T(1,128)} %counts_ref.1) | copy-start | bytes 1540
  0.0 33.8 %slice-start = ((s8[10485760]{0:T(1024)(128)(4,1)}), s8[4194304]{0:T(1024)(128)(4,1)S(1)}, s32[]{:S(2)}) async-start(s8[10485760]{0:T(1024)(128)(4,1)} %bitcast.2), calls=%async_computation.1 | async-start | bytes 8388608
  0.0 33.8 %slice-start.1 = ((s8[10485760]{0:T(1024)(128)(4,1)}), s8[4194304]{0:T(1024)(128)(4,1)S(1)}, s32[]{:S(2)}) async-start(s8[10485760]{0:T(1024)(128)(4,1)} %bitcast.2), calls=%async_computation.2 | async-start | bytes 8388608
  1.8 32.0 %collective-permute-start.4 = (s16[64,8192]{1,0:T(8,128)(2,1)S(1)}, s16[64,8192]{1,0:T(8,128)(2,1)S(1)}, u32[]{:S(2)}, u32[]{:S(2)}) collective-permute-start(s16[64,8192]{1,0:T(8,128)(2,1)S(1)} %encode.1.after_ref), channel_id=1, source_target_pairs={{0,8},{8,0},{16,24},{24,16},{32,40},{40,32},{48,56},{56,48},{64,72... | collective-permute-start | bytes 3145736 | tf_op jit(solution)/shard_map/ppermute | solution.py:353
  3.4 26.4 %copy-start = (bf16[4,2,2,128,128]{4,3,2,1,0:T(8,128)(2,1)S(1)}, bf16[4,2,2,128,128]{4,3,2,1,0:T(8,128)(2,1)}, u32[]{:S(2)}) copy-start(bf16[4,2,2,128,128]{4,3,2,1,0:T(8,128)(2,1)} %trans_ref.1) | copy-start | bytes 1572868
  3.4 30.4 %slice-start.2 = ((s8[10485760]{0:T(1024)(128)(4,1)}), s8[2097152]{0:T(1024)(128)(4,1)S(1)}, s32[]{:S(2)}) async-start(s8[10485760]{0:T(1024)(128)(4,1)} %bitcast.2), calls=%async_computation.3 | async-start | bytes 4194304
  6.7 27.0 %copy-start.1 = (bf16[128,128]{1,0:T(8,128)(2,1)S(1)}, bf16[128,128]{1,0:T(8,128)(2,1)}, u32[]{:S(2)}) copy-start(bf16[128,128]{1,0:T(8,128)(2,1)} %map_ref.1) | copy-start | bytes 98308
  6.7 1.6 %collective-permute-start = (bf16[64,16,128]{2,1,0:T(8,128)(2,1)S(1)}, bf16[64,16,128]{2,1,0:T(8,128)(2,1)S(1)}, u32[]{:S(2)}, u32[]{:S(2)}) collective-permute-start(bf16[64,16,128]{2,1,0:T(8,128)(2,1)S(1)} %get-tuple-element.16), channel_id=1, source_target_pairs={{0,1},{1,0},{2,3},{3,2},{4,5},{5,4},{6,7},{7,6},{8,9},{9,8},{10,11... | collective-permute-start | bytes 786440 | tf_op jit(solution)/shard_map/ppermute | solution.py:353
  25.1 4.9 %collective-permute-start.1 = (bf16[4,16,128]{2,1,0:T(8,128)(2,1)S(1)}, bf16[4,16,128]{2,1,0:T(8,128)(2,1)S(1)}, u32[]{:S(2)}, u32[]{:S(2)}) collective-permute-start(bf16[4,16,128]{2,1,0:T(8,128)(2,1)S(1)} %get-tuple-element.19), channel_id=1, source_target_pairs={{0,8},{8,0},{16,24},{24,16},{32,40},{40,32},{48,56},{56,48},{64,72... | collective-permute-start | bytes 49160 | tf_op jit(solution)/shard_map/ppermute | solution.py:353
  26.1 5.2 %collective-permute-start.2 = (bf16[4,16,128]{2,1,0:T(8,128)(2,1)S(1)}, bf16[4,16,128]{2,1,0:T(8,128)(2,1)S(1)}, u32[]{:S(2)}, u32[]{:S(2)}) collective-permute-start(bf16[4,16,128]{2,1,0:T(8,128)(2,1)S(1)} %get-tuple-element.19), channel_id=1, source_target_pairs={{0,16},{8,24},{16,0},{24,8},{32,48},{40,56},{48,32},{56,40},{64,80... | collective-permute-start | bytes 49160 | tf_op jit(solution)/shard_map/ppermute | solution.py:353
  28.7 4.9 %collective-permute-start.3 = (bf16[4,16,128]{2,1,0:T(8,128)(2,1)S(1)}, bf16[4,16,128]{2,1,0:T(8,128)(2,1)S(1)}, u32[]{:S(2)}, u32[]{:S(2)}) collective-permute-start(bf16[4,16,128]{2,1,0:T(8,128)(2,1)S(1)} %get-tuple-element.19), channel_id=1, source_target_pairs={{0,24},{8,16},{16,8},{24,0},{32,56},{40,48},{48,40},{56,32},{64,88... | collective-permute-start | bytes 49160 | tf_op jit(solution)/shard_map/ppermute | solution.py:353
  34.7 1.6 %collective-permute-start.5 = (bf16[128,1024]{1,0:T(8,128)(2,1)S(1)}, bf16[128,1024]{1,0:T(8,128)(2,1)S(1)}, u32[]{:S(2)}, u32[]{:S(2)}) collective-permute-start(bf16[128,1024]{1,0:T(8,128)(2,1)S(1)} %a_0.1.rest_0_.state_ref), channel_id=1, source_target_pairs={{0,1},{1,0},{2,3},{3,2},{4,5},{5,4},{6,7},{7,6},{8,9},{9,8},{10,11... | collective-permute-start | bytes 786440 | tf_op jit(solution)/shard_map/ppermute | solution.py:353
  35.7 3.1 %collective-permute-start.8 = (bf16[128,1024]{1,0:T(8,128)(2,1)S(1)}, bf16[128,1024]{1,0:T(8,128)(2,1)S(1)}, u32[]{:S(2)}, u32[]{:S(2)}) collective-permute-start(bf16[128,1024]{1,0:T(8,128)(2,1)S(1)} %a_2.1.rest_0_.state_ref), channel_id=1, source_target_pairs={{0,1},{1,0},{2,3},{3,2},{4,5},{5,4},{6,7},{7,6},{8,9},{9,8},{10,11... | collective-permute-start | bytes 786440 | tf_op jit(solution)/shard_map/ppermute | solution.py:353
  36.6 10.7 %collective-permute-start.6 = (bf16[128,1024]{1,0:T(8,128)(2,1)S(1)}, bf16[128,1024]{1,0:T(8,128)(2,1)S(1)}, u32[]{:S(2)}, u32[]{:S(2)}) collective-permute-start(bf16[128,1024]{1,0:T(8,128)(2,1)S(1)} %b_0.1.rest_0_.state_ref), channel_id=1, source_target_pairs={{0,16},{8,24},{16,0},{24,8},{32,48},{40,56},{48,32},{56,40},{64,80... | collective-permute-start | bytes 786440 | tf_op jit(solution)/shard_map/ppermute | solution.py:353
  38.7 3.8 %collective-permute-start.7 = (bf16[128,2048]{1,0:T(8,128)(2,1)S(1)}, bf16[128,2048]{1,0:T(8,128)(2,1)S(1)}, u32[]{:S(2)}, u32[]{:S(2)}) collective-permute-start(bf16[128,2048]{1,0:T(8,128)(2,1)S(1)} %a_4.1.rest_0_.state_ref), channel_id=1, source_target_pairs={{0,1},{1,0},{2,3},{3,2},{4,5},{5,4},{6,7},{7,6},{8,9},{9,8},{10,11... | collective-permute-start | bytes 1572872 | tf_op jit(solution)/shard_map/ppermute | solution.py:353
  39.1 13.9 %collective-permute-start.12 = (bf16[128,1024]{1,0:T(8,128)(2,1)S(1)}, bf16[128,1024]{1,0:T(8,128)(2,1)S(1)}, u32[]{:S(2)}, u32[]{:S(2)}) collective-permute-start(bf16[128,1024]{1,0:T(8,128)(2,1)S(1)} %b_2.1.rest_0_.state_ref), channel_id=1, source_target_pairs={{0,16},{8,24},{16,0},{24,8},{32,48},{40,56},{48,32},{56,40},{64,80... | collective-permute-start | bytes 786440 | tf_op jit(solution)/shard_map/ppermute | solution.py:353
  42.8 15.8 %collective-permute-start.10 = (bf16[128,1024]{1,0:T(8,128)(2,1)S(1)}, bf16[128,1024]{1,0:T(8,128)(2,1)S(1)}, u32[]{:S(2)}, u32[]{:S(2)}) collective-permute-start(bf16[128,1024]{1,0:T(8,128)(2,1)S(1)} %b_4.1.rest_0_.state_ref), channel_id=1, source_target_pairs={{0,16},{8,24},{16,0},{24,8},{32,48},{40,56},{48,32},{56,40},{64,80... | collective-permute-start | bytes 786440 | tf_op jit(solution)/shard_map/ppermute | solution.py:353
  47.7 11.8 %collective-permute-start.9 = (bf16[128,1024]{1,0:T(8,128)(2,1)S(1)}, bf16[128,1024]{1,0:T(8,128)(2,1)S(1)}, u32[]{:S(2)}, u32[]{:S(2)}) collective-permute-start(bf16[128,1024]{1,0:T(8,128)(2,1)S(1)} %c_0.1.rest_0_.state_ref), channel_id=1, source_target_pairs={{0,2},{1,3},{2,0},{3,1},{4,6},{5,7},{6,4},{7,5},{8,10},{9,11},{10,... | collective-permute-start | bytes 786440 | tf_op jit(solution)/shard_map/ppermute | solution.py:353
  49.9 4.0 %collective-permute-start.11 = (bf16[128,2048]{1,0:T(8,128)(2,1)S(1)}, bf16[128,2048]{1,0:T(8,128)(2,1)S(1)}, u32[]{:S(2)}, u32[]{:S(2)}) collective-permute-start(bf16[128,2048]{1,0:T(8,128)(2,1)S(1)} %a_8.1.rest_0_.state_ref), channel_id=1, source_target_pairs={{0,1},{1,0},{2,3},{3,2},{4,5},{5,4},{6,7},{7,6},{8,9},{9,8},{10,11... | collective-permute-start | bytes 1572872 | tf_op jit(solution)/shard_map/ppermute | solution.py:353
  50.4 13.9 %collective-permute-start.18 = (bf16[128,1024]{1,0:T(8,128)(2,1)S(1)}, bf16[128,1024]{1,0:T(8,128)(2,1)S(1)}, u32[]{:S(2)}, u32[]{:S(2)}) collective-permute-start(bf16[128,1024]{1,0:T(8,128)(2,1)S(1)} %b_6.1.rest_0_.state_ref), channel_id=1, source_target_pairs={{0,16},{8,24},{16,0},{24,8},{32,48},{40,56},{48,32},{56,40},{64,80... | collective-permute-start | bytes 786440 | tf_op jit(solution)/shard_map/ppermute | solution.py:353
  53.3 11.3 %collective-permute-start.17 = (bf16[128,1024]{1,0:T(8,128)(2,1)S(1)}, bf16[128,1024]{1,0:T(8,128)(2,1)S(1)}, u32[]{:S(2)}, u32[]{:S(2)}) collective-permute-start(bf16[128,1024]{1,0:T(8,128)(2,1)S(1)} %c_2.1.rest_0_.state_ref), channel_id=1, source_target_pairs={{0,2},{1,3},{2,0},{3,1},{4,6},{5,7},{6,4},{7,5},{8,10},{9,11},{10,... | collective-permute-start | bytes 786440 | tf_op jit(solution)/shard_map/ppermute | solution.py:353
  54.2 15.6 %collective-permute-start.16 = (bf16[128,1024]{1,0:T(8,128)(2,1)S(1)}, bf16[128,1024]{1,0:T(8,128)(2,1)S(1)}, u32[]{:S(2)}, u32[]{:S(2)}) collective-permute-start(bf16[128,1024]{1,0:T(8,128)(2,1)S(1)} %b_8.1.rest_0_.state_ref), channel_id=1, source_target_pairs={{0,16},{8,24},{16,0},{24,8},{32,48},{40,56},{48,32},{56,40},{64,80... | collective-permute-start | bytes 786440 | tf_op jit(solution)/shard_map/ppermute | solution.py:353
  59.0 12.5 %collective-permute-start.15 = (bf16[128,1024]{1,0:T(8,128)(2,1)S(1)}, bf16[128,1024]{1,0:T(8,128)(2,1)S(1)}, u32[]{:S(2)}, u32[]{:S(2)}) collective-permute-start(bf16[128,1024]{1,0:T(8,128)(2,1)S(1)} %c_4.1.rest_0_.state_ref), channel_id=1, source_target_pairs={{0,2},{1,3},{2,0},{3,1},{4,6},{5,7},{6,4},{7,5},{8,10},{9,11},{10,... | collective-permute-start | bytes 786440 | tf_op jit(solution)/shard_map/ppermute | solution.py:353
  59.8 1.7 %copy-start.3 = (bf16[128,1024]{1,0:T(8,128)(2,1)}, bf16[128,1024]{1,0:T(8,128)(2,1)S(1)}, u32[]{:S(2)}) copy-start(bf16[128,1024]{1,0:T(8,128)(2,1)S(1)} %d_0.1.rest_0_.refs_0_) | copy-start | bytes 786436
  61.5 4.0 %collective-permute-start.13 = (bf16[128,2048]{1,0:T(8,128)(2,1)S(1)}, bf16[128,2048]{1,0:T(8,128)(2,1)S(1)}, u32[]{:S(2)}, u32[]{:S(2)}) collective-permute-start(bf16[128,2048]{1,0:T(8,128)(2,1)S(1)} %a_12.1.rest_0_.state_ref), channel_id=1, source_target_pairs={{0,1},{1,0},{2,3},{3,2},{4,5},{5,4},{6,7},{7,6},{8,9},{9,8},{10,11... | collective-permute-start | bytes 1572872 | tf_op jit(solution)/shard_map/ppermute | solution.py:353
  64.2 11.2 %collective-permute-start.14 = (bf16[128,1024]{1,0:T(8,128)(2,1)S(1)}, bf16[128,1024]{1,0:T(8,128)(2,1)S(1)}, u32[]{:S(2)}, u32[]{:S(2)}) collective-permute-start(bf16[128,1024]{1,0:T(8,128)(2,1)S(1)} %b_10.1.rest_0_.state_ref), channel_id=1, source_target_pairs={{0,16},{8,24},{16,0},{24,8},{32,48},{40,56},{48,32},{56,40},{64,80... | collective-permute-start | bytes 786440 | tf_op jit(solution)/shard_map/ppermute | solution.py:353
  64.6 11.9 %collective-permute-start.24 = (bf16[128,1024]{1,0:T(8,128)(2,1)S(1)}, bf16[128,1024]{1,0:T(8,128)(2,1)S(1)}, u32[]{:S(2)}, u32[]{:S(2)}) collective-permute-start(bf16[128,1024]{1,0:T(8,128)(2,1)S(1)} %c_6.1.rest_0_.state_ref), channel_id=1, source_target_pairs={{0,2},{1,3},{2,0},{3,1},{4,6},{5,7},{6,4},{7,5},{8,10},{9,11},{10,... | collective-permute-start | bytes 786440 | tf_op jit(solution)/shard_map/ppermute | solution.py:353
  65.9 15.2 %collective-permute-start.23 = (bf16[128,1024]{1,0:T(8,128)(2,1)S(1)}, bf16[128,1024]{1,0:T(8,128)(2,1)S(1)}, u32[]{:S(2)}, u32[]{:S(2)}) collective-permute-start(bf16[128,1024]{1,0:T(8,128)(2,1)S(1)} %b_12.1.rest_0_.state_ref), channel_id=1, source_target_pairs={{0,16},{8,24},{16,0},{24,8},{32,48},{40,56},{48,32},{56,40},{64,80... | collective-permute-start | bytes 786440 | tf_op jit(solution)/shard_map/ppermute | solution.py:353
  70.2 11.8 %collective-permute-start.22 = (bf16[128,1024]{1,0:T(8,128)(2,1)S(1)}, bf16[128,1024]{1,0:T(8,128)(2,1)S(1)}, u32[]{:S(2)}, u32[]{:S(2)}) collective-permute-start(bf16[128,1024]{1,0:T(8,128)(2,1)S(1)} %c_8.1.rest_0_.state_ref), channel_id=1, source_target_pairs={{0,2},{1,3},{2,0},{3,1},{4,6},{5,7},{6,4},{7,5},{8,10},{9,11},{10,... | collective-permute-start | bytes 786440 | tf_op jit(solution)/shard_map/ppermute | solution.py:353
  72.0 11.9 %collective-permute-start.21 = (bf16[128,512]{1,0:T(8,128)(2,1)S(1)}, bf16[128,512]{1,0:T(8,128)(2,1)S(1)}, u32[]{:S(2)}, u32[]{:S(2)}) collective-permute-start(bf16[128,512]{1,0:T(8,128)(2,1)S(1)} %b_14.1.rest_0_.state_ref), channel_id=1, source_target_pairs={{0,16},{8,24},{16,0},{24,8},{32,48},{40,56},{48,32},{56,40},{64,80... | collective-permute-start | bytes 393224 | tf_op jit(solution)/shard_map/ppermute | solution.py:353
  75.8 8.8 %collective-permute-start.20 = (bf16[128,1024]{1,0:T(8,128)(2,1)S(1)}, bf16[128,1024]{1,0:T(8,128)(2,1)S(1)}, u32[]{:S(2)}, u32[]{:S(2)}) collective-permute-start(bf16[128,1024]{1,0:T(8,128)(2,1)S(1)} %c_10.1.rest_0_.state_ref), channel_id=1, source_target_pairs={{0,2},{1,3},{2,0},{3,1},{4,6},{5,7},{6,4},{7,5},{8,10},{9,11},{10,... | collective-permute-start | bytes 786440 | tf_op jit(solution)/shard_map/ppermute | solution.py:353
  76.6 9.3 %collective-permute-start.19 = (bf16[128,512]{1,0:T(8,128)(2,1)S(1)}, bf16[128,512]{1,0:T(8,128)(2,1)S(1)}, u32[]{:S(2)}, u32[]{:S(2)}) collective-permute-start(bf16[128,512]{1,0:T(8,128)(2,1)S(1)} %b_15.1.rest_0_.state_ref), channel_id=1, source_target_pairs={{0,16},{8,24},{16,0},{24,8},{32,48},{40,56},{48,32},{56,40},{64,80... | collective-permute-start | bytes 393224 | tf_op jit(solution)/shard_map/ppermute | solution.py:353
  81.4 9.3 %collective-permute-start.27 = (bf16[128,1024]{1,0:T(8,128)(2,1)S(1)}, bf16[128,1024]{1,0:T(8,128)(2,1)S(1)}, u32[]{:S(2)}, u32[]{:S(2)}) collective-permute-start(bf16[128,1024]{1,0:T(8,128)(2,1)S(1)} %c_12.1.rest_0_.state_ref), channel_id=1, source_target_pairs={{0,2},{1,3},{2,0},{3,1},{4,6},{5,7},{6,4},{7,5},{8,10},{9,11},{10,... | collective-permute-start | bytes 786440 | tf_op jit(solution)/shard_map/ppermute | solution.py:353
  84.1 8.9 %collective-permute-start.26 = (bf16[128,512]{1,0:T(8,128)(2,1)S(1)}, bf16[128,512]{1,0:T(8,128)(2,1)S(1)}, u32[]{:S(2)}, u32[]{:S(2)}) collective-permute-start(bf16[128,512]{1,0:T(8,128)(2,1)S(1)} %c_14.1.rest_0_.state_ref), channel_id=1, source_target_pairs={{0,2},{1,3},{2,0},{3,1},{4,6},{5,7},{6,4},{7,5},{8,10},{9,11},{10,... | collective-permute-start | bytes 393224 | tf_op jit(solution)/shard_map/ppermute | solution.py:353
  86.1 5.0 %copy-start.4 = (bf16[128,1024]{1,0:T(8,128)(2,1)S(1)}, bf16[128,1024]{1,0:T(8,128)(2,1)}, u32[]{:S(2)}) copy-start(bf16[128,1024]{1,0:T(8,128)(2,1)} %copy-done.3) | copy-start | bytes 786436
  86.1 8.3 %collective-permute-start.25 = (bf16[128,512]{1,0:T(8,128)(2,1)S(1)}, bf16[128,512]{1,0:T(8,128)(2,1)S(1)}, u32[]{:S(2)}, u32[]{:S(2)}) collective-permute-start(bf16[128,512]{1,0:T(8,128)(2,1)S(1)} %c_15.1.rest_0_.state_ref), channel_id=1, source_target_pairs={{0,2},{1,3},{2,0},{3,1},{4,6},{5,7},{6,4},{7,5},{8,10},{9,11},{10,... | collective-permute-start | bytes 393224 | tf_op jit(solution)/shard_map/ppermute | solution.py:353
